TPU v7x, 512 devices: a whole 4x4x16 slice. The times are simulated.
512 devices in a mesh: gx: 32 (over z, core), gy: 16 (over x, y).
Axes of the slice: x: 4, y: 4, z: 16, core: 2. Of those that a mesh axis runs over, the one named last changes fastest.
Arguments:
- right_side: float32 [3, 512, 2048], P(None, 'gx', 'gy'), may hold values from -40 to 40
- stiffness: float32 [33, 3, 3, 512, 2048], P(None, None, None, 'gx', 'gy'), may hold values from -0.1 to 15, as said below
- factor: float32 [17, 3, 3, 512, 2048], P(None, None, None, 'gx', 'gy'), may hold values from -0.05 to 0.35, as said below
- intact: int32 [32, 512, 2048], P(None, 'gx', 'gy'), may hold values 0 or 1
Outputs:
- solution_field: float32 [3, 512, 2048], P(None, 'gx', 'gy')
- residual: float32 [3, 512, 2048], P(None, 'gx', 'gy')
Inputs may be any that keep to these rules, and one draw needn't show every extreme that they name: `stiffness`: in the block for offset 16 the diagonal entries lie between 10 and 15; every other entry of every block lies within -0.1 to 0.1. `factor`: in the block for offset 16 the diagonal entries lie between 0.25 and 0.35 and its other entries within -0.02 to 0.02; the entries of the other blocks lie within -0.05 to 0.05.
All inputs are finite; a program needn't handle non-finite values. No bound on the sum of `intact` on one device may be relied on, other than what follows from the above.
Results may differ from a plain program's by a relative error of at most 0.0065.
Values sent between devices are 32-bit elements; how exact they have to be, the bound alone decides.
No kernel may reach another device: no remote copies, remote signals or barrier semaphores. Data moves between devices by JAX's collectives and lax.ppermute only.
A program may use at most 128 MiB of HBM per device.

v0:
```python
import jax
import jax.numpy as jnp
from jax import lax
from jax.sharding import PartitionSpec as P

NZ = 4
ITERS = 2


def extended_2(cells, sides, width):
    for axis, dim in sides:
        count = lax.axis_size(axis)
        ends = count - 1
        head = lax.slice_in_dim(cells, 0, width, axis=dim)
        tail = lax.slice_in_dim(cells, cells.shape[dim] - width, cells.shape[dim], axis=dim)
        cells = jnp.concatenate(
            [
                lax.ppermute(tail, axis, [(i, (i + 1) % count) for i in range(ends)]),
                cells,
                lax.ppermute(head, axis, [((i + 1) % count, i) for i in range(ends)]),
            ],
            axis=dim,
        )
    return cells


def from_behind(shard, axis, by):
    count = lax.axis_size(axis)
    pairs = [(i, i + by) for i in range(count) if 0 <= i + by < count]
    return lax.ppermute(shard, axis, pairs)


def bond_offsets():
    return [
        (a, b, c)
        for a in range(-2, 3)
        for b in range(-2, 3)
        for c in range(-2, 3)
        if a * a + b * b + c * c <= 4
    ]


def forward(blocks, extended, shift, weights, offsets):
    rows = extended.shape[1] - 2 * shift
    cols = extended.shape[2] - 2 * shift * NZ
    zpos = lax.iota(jnp.int32, cols) % NZ
    total = jnp.zeros((3, rows, cols), jnp.float32)
    for index, (dx, dy, dz) in enumerate(offsets):
        start_y = (shift + dy) * NZ + dz
        piece = extended[:, shift + dx : shift + dx + rows, start_y : start_y + cols]
        valid = ((zpos + dz >= 0) & (zpos + dz < NZ)).astype(jnp.float32)
        scale = valid if weights is None else valid * weights[index]
        total = total + jnp.sum(blocks[index] * (piece * scale)[None], axis=1)
    return total


def backward(blocks_ext, extended, margin, offsets):
    rows = extended.shape[1] - 2 * margin
    cols = extended.shape[2] - 2 * margin * NZ
    zpos = lax.iota(jnp.int32, cols) % NZ
    total = jnp.zeros((3, rows, cols), jnp.float32)
    for index, (dx, dy, dz) in enumerate(offsets):
        start_x = margin - dx
        start_y = (margin - dy) * NZ - dz
        block = blocks_ext[index, :, :, start_x : start_x + rows, start_y : start_y + cols]
        piece = extended[:, start_x : start_x + rows, start_y : start_y + cols]
        valid = ((zpos - dz >= 0) & (zpos - dz < NZ)).astype(jnp.float32)
        total = total + jnp.sum(block * (piece * valid)[:, None], axis=0)
    return total


def extend(field, depth):
    wider = extended_2(field, (("gx", 1),), depth)
    return extended_2(wider, (("gy", 2),), depth * NZ)


def inner_sum(first, second):
    return lax.psum(jnp.sum(first * second), ("gx", "gy"))


def local(right_side, stiffness, factor, intact):
    offsets = bond_offsets()
    lower = offsets[:17]
    mask = intact.astype(jnp.float32)
    weights = jnp.concatenate([mask[:16], jnp.ones_like(mask[:1]), mask[16:]], axis=0)
    upper_rows = from_behind(factor[:, :, :, :2], "gx", -1)
    factor_wide = jnp.concatenate([jnp.zeros_like(upper_rows), factor, upper_rows], axis=3)
    factor_ext = extended_2(factor_wide, (("gy", 4),), 2 * NZ)

    def precondition(field):
        image = forward(factor, extend(field, 2), 2, None, lower)
        image_ext = extend(image, 2)
        return backward(factor_ext, image_ext, 2, lower)

    solution_field = jnp.zeros_like(right_side)
    residual = right_side
    zvec = precondition(residual)
    direction = zvec
    rho = inner_sum(residual, zvec)
    for step in range(ITERS):
        image = forward(stiffness, extend(direction, 2), 2, weights, offsets)
        alpha = rho / inner_sum(direction, image)
        solution_field = solution_field + alpha * direction
        residual = residual - alpha * image
        if step + 1 < ITERS:
            zvec = precondition(residual)
            rho_next = inner_sum(residual, zvec)
            direction = zvec + rho_next / rho * direction
            rho = rho_next
    return (solution_field, residual)


def solution(mesh):
    in_specs = (
        P(None, "gx", "gy"),
        P(None, None, None, "gx", "gy"),
        P(None, None, None, "gx", "gy"),
        P(None, "gx", "gy"),
    )
    out_specs = (P(None, "gx", "gy"), P(None, "gx", "gy"))
    return jax.shard_map(local, mesh=mesh, in_specs=in_specs, out_specs=out_specs, check_vma=False)
```

profile of v0, /device:TPU:1, one launch (start us, length us, event | category | flops | bytes accessed | tf_op | source)
XLA Modules:
  0.0 515.7 jit_solution(10757847150073007536)
XLA Ops:
  1.5 4.9 collective-permute-start.1
  6.4 5.1 collective-permute-start.2
  12.7 1.9 collective-permute-start
  18.2 5.9 %copy.312 = f32[17,3,3,16,128]{3,4,2,1,0:T(8,128)} copy(f32[17,3,3,16,128]{4,3,2,1,0:T(8,128)S(1)} %copy-done) | data formatting | bytes 2506752 | tf_op args[2]
  24.2 1.3 collective-permute-start.3
  25.5 1.3 collective-permute-start.4
  26.8 3.4 collective-permute-done.4
  30.7 1.9 collective-permute-start.5
  32.6 4.8 collective-permute-start.7
  38.2 2.2 collective-permute-start.10
  40.4 1.3 collective-permute-start.8
  41.7 3.4 collective-permute-done.8
  46.1 6.6 %copy.313 = f32[17,3,3,2,128]{3,4,2,1,0:T(8,128)} copy(f32[17,3,3,2,128]{4,0,3,2,1:T(8,128)S(1)} %collective-permute-done) | data formatting | bytes 313344 | tf_op jit(solution)/shard_map/ppermute | solution.py:30
  52.7 15.7 %pad_maximum_fusion = f32[17,3,3,20,128]{3,4,2,1,0:T(8,128)} fusion(f32[17,3,3,2,128]{3,4,2,1,0:T(8,128)} %copy.313, f32[17,3,3,16,128]{3,4,2,1,0:T(8,128)} %copy.312, f32[20]{0:T(128)S(1)} %pad.71.clone), kind=kLoop, calls=%fused_computation | loop fusion | flops 783360 | bytes 2976848 | tf_op jit(solution)/shard_map/concatenate | solution.py:87
  68.5 2.4 fusion.162
  70.9 7.2 %copy.314 = f32[17,3,3,20,128]{4,3,2,1,0:T(8,128)S(1)} copy(f32[17,3,3,20,128]{3,4,2,1,0:T(8,128)} %pad_maximum_fusion) | data formatting | bytes 3133440 | tf_op jit(solution)/shard_map/concatenate | solution.py:87
  78.1 1.3 collective-permute-start.6
  79.4 5.9 %collective-permute-start.9 = (f32[17,3,3,20,8]{3,4,2,1,0:T(8,128)}, f32[17,3,3,20,8]{3,4,2,1,0:T(8,128)}, u32[]{:S(2)}, u32[]{:S(2)}) collective-permute-start(f32[17,3,3,20,8]{3,4,2,1,0:T(8,128)} %get-tuple-element.155), channel_id=1, source_target_pairs={{0,1},{1,2},{2,3},{3,4},{4,5},{5,6},{6,7},{7,8},{8,9},{9,10},{10,1... | collective-permute-start | bytes 293768 | tf_op jit(solution)/shard_map/ppermute | solution.py:18
  85.3 1.7 copy_dynamic-update-slice_fusion
  87.0 1.6 multiply_reduce_fusion.31
  88.6 7.4 %collective-permute-done.6 = f32[17,3,3,20,8]{3,4,2,1,0:T(8,128)} collective-permute-done((f32[17,3,3,20,8]{3,4,2,1,0:T(8,128)}, f32[17,3,3,20,8]{3,4,2,1,0:T(8,128)}, u32[]{:S(2)}, u32[]{:S(2)}) %collective-permute-start.6) | collective-permute-done | bytes 97952 | tf_op jit(solution)/shard_map/ppermute | solution.py:20
  96.0 3.4 copy.315
  99.3 2.7 multiply_reduce_fusion.29
  102.0 3.3 copy.324
  105.4 2.2 multiply_reduce_fusion.25
  109.0 2.1 collective-permute-start.12
  111.1 5.4 %collective-permute-start.11 = (f32[3,2,128]{2,1,0:T(2,128)S(1)}, f32[3,2,128]{2,1,0:T(2,128)S(1)}, u32[]{:S(2)}, u32[]{:S(2)}) collective-permute-start(f32[3,2,128]{2,1,0:T(2,128)S(1)} %get-tuple-element.395), channel_id=1, source_target_pairs={{0,16},{16,32},{32,48},{48,64},{64,80},{80,96},{96,112},{112,128},... | collective-permute-start | bytes 9224 | tf_op jit(solution)/shard_map/ppermute | solution.py:18
  117.3 1.3 collective-permute-start.14
  118.6 4.2 collective-permute-start.13
  125.4 118.6 %all-reduce = (f32[]{:T(128)}, f32[]{:T(128)}) all-reduce(f32[]{:T(128)} %get-tuple-element.109, f32[]{:T(128)} %get-tuple-element.108), channel_id=1, replica_groups=mesh['gx'=32,'gy'=16] {'gx','gy'}, use_global_device_ids=true, to_apply=%region_35.36 | all-reduce | flops 2 | bytes 16 | tf_op jit(solution)/shard_map/psum | solution.py:78
  245.3 3.1 collective-permute-start.16
  248.4 3.1 collective-permute-start.15
  252.4 1.3 collective-permute-start.18
  253.7 4.0 collective-permute-start.17
  259.5 2.5 collective-permute-start.19
  262.0 4.7 collective-permute-start.20
  267.6 3.9 collective-permute-start.22
  271.5 1.3 collective-permute-start.21
  273.9 2.3 collective-permute-done.21
  277.6 109.9 %psum.30 = f32[]{:T(128)} all-reduce(f32[]{:T(128)} %get-tuple-element.116), channel_id=1, replica_groups=mesh['gx'=32,'gy'=16] {'gx','gy'}, use_global_device_ids=true, to_apply=%region_106.107 | all-reduce | flops 1 | bytes 8 | tf_op jit(solution)/shard_map/psum | solution.py:78
  388.9 4.2 collective-permute-start.23
  393.2 1.9 collective-permute-start.24
  395.1 3.0 collective-permute-done.24
  398.2 1.5 collective-permute-start.25
  399.7 1.3 collective-permute-start.26
  401.1 3.3 collective-permute-done.26
  406.3 1.3 fusion.31
  408.4 104.7 %psum.31 = f32[]{:T(128)} all-reduce(f32[]{:T(128)} %get-tuple-element.112), channel_id=1, replica_groups=mesh['gx'=32,'gy'=16] {'gx','gy'}, use_global_device_ids=true, to_apply=%region_141.142 | all-reduce | flops 1 | bytes 8 | tf_op jit(solution)/shard_map/psum | solution.py:78
  (268 shorter events, 21.4 us)
Async XLA Ops:
  1.5 22.6 %collective-permute-start.1 = (f32[3,2,128]{2,1,0:T(2,128)S(1)}, f32[3,2,128]{2,1,0:T(2,128)S(1)}, u32[]{:S(2)}, u32[]{:S(2)}) collective-permute-start(f32[3,2,128]{2,1,0:T(2,128)S(1)} %get-tuple-element.400), channel_id=1, source_target_pairs={{0,16},{16,32},{32,48},{48,64},{64,80},{80,96},{96,112},{112,128},... | collective-permute-start | bytes 9224 | tf_op jit(solution)/shard_map/ppermute | solution.py:18
  6.4 17.7 %collective-permute-start.2 = (f32[3,2,128]{2,1,0:T(2,128)S(1)}, f32[3,2,128]{2,1,0:T(2,128)S(1)}, u32[]{:S(2)}, u32[]{:S(2)}) collective-permute-start(f32[3,2,128]{2,1,0:T(2,128)S(1)} %get-tuple-element.399), channel_id=1, source_target_pairs={{16,0},{32,16},{48,32},{64,48},{80,64},{96,80},{112,96},{128,112},... | collective-permute-start | bytes 9224 | tf_op jit(solution)/shard_map/ppermute | solution.py:20
  12.7 33.4 %collective-permute-start = (f32[17,3,3,2,128]{4,0,3,2,1:T(8,128)S(1)}, f32[17,3,3,2,128]{4,0,3,2,1:T(8,128)S(1)}, u32[]{:S(2)}, u32[]{:S(2)}) collective-permute-start(f32[17,3,3,2,128]{4,0,3,2,1:T(8,128)S(1)} %copy.402), channel_id=1, source_target_pairs={{16,0},{32,16},{48,32},{64,48},{80,64},{96,80},{112,96},{128,112},... | collective-permute-start | bytes 470024 | tf_op jit(solution)/shard_map/ppermute | solution.py:30
  14.6 30.6 %copy-start.68 = (f32[128]{0:T(128)}, f32[128]{0:T(128)S(1)}, u32[]{:S(2)}) copy-start(f32[128]{0:T(128)S(1)} %get-tuple-element.437) | copy-start | bytes 1540
  14.7 30.5 %copy-start.70 = (f32[128]{0:T(128)}, f32[128]{0:T(128)S(1)}, u32[]{:S(2)}) copy-start(f32[128]{0:T(128)S(1)} %get-tuple-element.436) | copy-start | bytes 1540
  24.2 2.6 collective-permute-start.3
  25.5 4.7 collective-permute-start.4
  30.7 7.3 %collective-permute-start.5 = (f32[3,2,128]{2,1,0:T(2,128)S(1)}, f32[3,2,128]{2,1,0:T(2,128)S(1)}, u32[]{:S(2)}, u32[]{:S(2)}) collective-permute-start(f32[3,2,128]{2,1,0:T(2,128)S(1)} %get-tuple-element.398), channel_id=1, source_target_pairs={{16,0},{32,16},{48,32},{64,48},{80,64},{96,80},{112,96},{128,112},... | collective-permute-start | bytes 9224 | tf_op jit(solution)/shard_map/ppermute | solution.py:20
  32.6 5.5 %collective-permute-start.7 = (f32[3,2,128]{2,1,0:T(2,128)S(1)}, f32[3,2,128]{2,1,0:T(2,128)S(1)}, u32[]{:S(2)}, u32[]{:S(2)}) collective-permute-start(f32[3,2,128]{2,1,0:T(2,128)S(1)} %get-tuple-element.397), channel_id=1, source_target_pairs={{0,16},{16,32},{32,48},{48,64},{64,80},{80,96},{96,112},{112,128},... | collective-permute-start | bytes 9224 | tf_op jit(solution)/shard_map/ppermute | solution.py:18
  38.2 3.5 collective-permute-start.10
  40.4 4.7 collective-permute-start.8
  78.1 17.9 %collective-permute-start.6 = (f32[17,3,3,20,8]{3,4,2,1,0:T(8,128)}, f32[17,3,3,20,8]{3,4,2,1,0:T(8,128)}, u32[]{:S(2)}, u32[]{:S(2)}) collective-permute-start(f32[17,3,3,20,8]{3,4,2,1,0:T(8,128)} %get-tuple-element.156), channel_id=1, source_target_pairs={{1,0},{2,1},{3,2},{4,3},{5,4},{6,5},{7,6},{8,7},{9,8},{10,9},{11,1... | collective-permute-start | bytes 293768 | tf_op jit(solution)/shard_map/ppermute | solution.py:20
  79.4 22.6 %collective-permute-start.9 = (f32[17,3,3,20,8]{3,4,2,1,0:T(8,128)}, f32[17,3,3,20,8]{3,4,2,1,0:T(8,128)}, u32[]{:S(2)}, u32[]{:S(2)}) collective-permute-start(f32[17,3,3,20,8]{3,4,2,1,0:T(8,128)} %get-tuple-element.155), channel_id=1, source_target_pairs={{0,1},{1,2},{2,3},{3,4},{4,5},{5,6},{6,7},{7,8},{8,9},{9,10},{10,1... | collective-permute-start | bytes 293768 | tf_op jit(solution)/shard_map/ppermute | solution.py:18
  109.0 7.5 %collective-permute-start.12 = (f32[3,2,128]{2,1,0:T(2,128)S(1)}, f32[3,2,128]{2,1,0:T(2,128)S(1)}, u32[]{:S(2)}, u32[]{:S(2)}) collective-permute-start(f32[3,2,128]{2,1,0:T(2,128)S(1)} %get-tuple-element.396), channel_id=1, source_target_pairs={{16,0},{32,16},{48,32},{64,48},{80,64},{96,80},{112,96},{128,112},... | collective-permute-start | bytes 9224 | tf_op jit(solution)/shard_map/ppermute | solution.py:20
  111.1 6.1 %collective-permute-start.11 = (f32[3,2,128]{2,1,0:T(2,128)S(1)}, f32[3,2,128]{2,1,0:T(2,128)S(1)}, u32[]{:S(2)}, u32[]{:S(2)}) collective-permute-start(f32[3,2,128]{2,1,0:T(2,128)S(1)} %get-tuple-element.395), channel_id=1, source_target_pairs={{0,16},{16,32},{32,48},{48,64},{64,80},{80,96},{96,112},{112,128},... | collective-permute-start | bytes 9224 | tf_op jit(solution)/shard_map/ppermute | solution.py:18
  117.3 5.5 %collective-permute-start.14 = (f32[3,20,8]{2,1,0:T(8,128)S(1)}, f32[3,20,8]{2,1,0:T(8,128)S(1)}, u32[]{:S(2)}, u32[]{:S(2)}) collective-permute-start(f32[3,20,8]{2,1,0:T(8,128)S(1)} %get-tuple-element.350), channel_id=1, source_target_pairs={{1,0},{2,1},{3,2},{4,3},{5,4},{6,5},{7,6},{8,7},{9,8},{10,9},{11,1... | collective-permute-start | bytes 5768 | tf_op jit(solution)/shard_map/ppermute | solution.py:20
  118.6 5.0 collective-permute-start.13
  124.5 134.4 %copy-start.69 = (f32[128]{0:T(128)S(1)}, f32[128]{0:T(128)}, u32[]{:S(2)}) copy-start(f32[128]{0:T(128)} %copy-done.68) | copy-start | bytes 1540
  124.5 134.4 %copy-start.72 = (f32[128]{0:T(128)S(1)}, f32[128]{0:T(128)}, u32[]{:S(2)}) copy-start(f32[128]{0:T(128)} %copy-done.70) | copy-start | bytes 1540
  124.5 134.4 %copy-start.76 = (f32[128]{0:T(128)S(1)}, f32[128]{0:T(128)}, u32[]{:S(2)}) copy-start(f32[128]{0:T(128)} %copy-done.75) | copy-start | bytes 1540
  245.3 6.2 %collective-permute-start.16 = (f32[3,2,128]{2,1,0:T(2,128)S(1)}, f32[3,2,128]{2,1,0:T(2,128)S(1)}, u32[]{:S(2)}, u32[]{:S(2)}) collective-permute-start(f32[3,2,128]{2,1,0:T(2,128)S(1)} %get-tuple-element.392), channel_id=1, source_target_pairs={{16,0},{32,16},{48,32},{64,48},{80,64},{96,80},{112,96},{128,112},... | collective-permute-start | bytes 9224 | tf_op jit(solution)/shard_map/ppermute | solution.py:20
  248.4 3.9 collective-permute-start.15
  252.4 5.3 %collective-permute-start.18 = (f32[3,20,8]{2,1,0:T(8,128)S(1)}, f32[3,20,8]{2,1,0:T(8,128)S(1)}, u32[]{:S(2)}, u32[]{:S(2)}) collective-permute-start(f32[3,20,8]{2,1,0:T(8,128)S(1)} %get-tuple-element.348), channel_id=1, source_target_pairs={{1,0},{2,1},{3,2},{4,3},{5,4},{6,5},{7,6},{8,7},{9,8},{10,9},{11,1... | collective-permute-start | bytes 5768 | tf_op jit(solution)/shard_map/ppermute | solution.py:20
  253.7 5.2 %collective-permute-start.17 = (f32[3,20,8]{2,1,0:T(8,128)S(1)}, f32[3,20,8]{2,1,0:T(8,128)S(1)}, u32[]{:S(2)}, u32[]{:S(2)}) collective-permute-start(f32[3,20,8]{2,1,0:T(8,128)S(1)} %get-tuple-element.349), channel_id=1, source_target_pairs={{0,1},{1,2},{2,3},{3,4},{4,5},{5,6},{6,7},{7,8},{8,9},{9,10},{10,1... | collective-permute-start | bytes 5768 | tf_op jit(solution)/shard_map/ppermute | solution.py:18
  259.5 7.3 %collective-permute-start.19 = (f32[3,2,128]{2,1,0:T(2,128)S(1)}, f32[3,2,128]{2,1,0:T(2,128)S(1)}, u32[]{:S(2)}, u32[]{:S(2)}) collective-permute-start(f32[3,2,128]{2,1,0:T(2,128)S(1)} %get-tuple-element.390), channel_id=1, source_target_pairs={{16,0},{32,16},{48,32},{64,48},{80,64},{96,80},{112,96},{128,112},... | collective-permute-start | bytes 9224 | tf_op jit(solution)/shard_map/ppermute | solution.py:20
  262.0 5.4 %collective-permute-start.20 = (f32[3,2,128]{2,1,0:T(2,128)S(1)}, f32[3,2,128]{2,1,0:T(2,128)S(1)}, u32[]{:S(2)}, u32[]{:S(2)}) collective-permute-start(f32[3,2,128]{2,1,0:T(2,128)S(1)} %get-tuple-element.389), channel_id=1, source_target_pairs={{0,16},{16,32},{32,48},{48,64},{64,80},{80,96},{96,112},{112,128},... | collective-permute-start | bytes 9224 | tf_op jit(solution)/shard_map/ppermute | solution.py:18
  267.6 6.3 %collective-permute-start.22 = (f32[3,20,8]{2,1,0:T(8,128)S(1)}, f32[3,20,8]{2,1,0:T(8,128)S(1)}, u32[]{:S(2)}, u32[]{:S(2)}) collective-permute-start(f32[3,20,8]{2,1,0:T(8,128)S(1)} %get-tuple-element.346), channel_id=1, source_target_pairs={{0,1},{1,2},{2,3},{3,4},{4,5},{5,6},{6,7},{7,8},{8,9},{9,10},{10,1... | collective-permute-start | bytes 5768 | tf_op jit(solution)/shard_map/ppermute | solution.py:18
  271.5 4.7 collective-permute-start.21
  272.8 128.2 %copy-start.61 = (f32[16,128]{1,0:T(8,128)S(1)}, f32[16,128]{1,0:T(8,128)}, u32[]{:S(2)}) copy-start(f32[16,128]{1,0:T(8,128)} %get-tuple-element.189) | copy-start | bytes 24580
  272.8 128.2 %copy-start.63 = (f32[16,128]{1,0:T(8,128)S(1)}, f32[16,128]{1,0:T(8,128)}, u32[]{:S(2)}) copy-start(f32[16,128]{1,0:T(8,128)} %get-tuple-element.191) | copy-start | bytes 24580
  272.9 128.2 %copy-start.65 = (f32[16,128]{1,0:T(8,128)S(1)}, f32[16,128]{1,0:T(8,128)}, u32[]{:S(2)}) copy-start(f32[16,128]{1,0:T(8,128)} %get-tuple-element.197) | copy-start | bytes 24580
  272.9 128.2 %copy-start.67 = (f32[16,128]{1,0:T(8,128)S(1)}, f32[16,128]{1,0:T(8,128)}, u32[]{:S(2)}) copy-start(f32[16,128]{1,0:T(8,128)} %get-tuple-element.199) | copy-start | bytes 24580
  276.3 128.2 %copy-start.36 = (f32[16,128]{1,0:T(8,128)S(1)}, f32[16,128]{1,0:T(8,128)}, u32[]{:S(2)}) copy-start(f32[16,128]{1,0:T(8,128)} %get-tuple-element.190) | copy-start | bytes 24580
  276.3 128.2 %copy-start.38 = (f32[16,128]{1,0:T(8,128)S(1)}, f32[16,128]{1,0:T(8,128)}, u32[]{:S(2)}) copy-start(f32[16,128]{1,0:T(8,128)} %get-tuple-element.193) | copy-start | bytes 24580
  276.3 128.2 %copy-start.40 = (f32[16,128]{1,0:T(8,128)S(1)}, f32[16,128]{1,0:T(8,128)}, u32[]{:S(2)}) copy-start(f32[16,128]{1,0:T(8,128)} %get-tuple-element.194) | copy-start | bytes 24580
  276.3 128.2 %copy-start.42 = (f32[16,128]{1,0:T(8,128)S(1)}, f32[16,128]{1,0:T(8,128)}, u32[]{:S(2)}) copy-start(f32[16,128]{1,0:T(8,128)} %get-tuple-element.180) | copy-start | bytes 24580
  276.4 128.2 %copy-start.44 = (f32[16,128]{1,0:T(8,128)S(1)}, f32[16,128]{1,0:T(8,128)}, u32[]{:S(2)}) copy-start(f32[16,128]{1,0:T(8,128)} %get-tuple-element.183) | copy-start | bytes 24580
  276.4 128.2 %copy-start.51 = (f32[16,128]{1,0:T(8,128)S(1)}, f32[16,128]{1,0:T(8,128)}, u32[]{:S(2)}) copy-start(f32[16,128]{1,0:T(8,128)} %get-tuple-element.188) | copy-start | bytes 24580
  276.6 128.2 %copy-start.49 = (f32[16,128]{1,0:T(8,128)S(1)}, f32[16,128]{1,0:T(8,128)}, u32[]{:S(2)}) copy-start(f32[16,128]{1,0:T(8,128)} %get-tuple-element.179) | copy-start | bytes 24580
  276.6 128.2 %copy-start.59 = (f32[16,128]{1,0:T(8,128)S(1)}, f32[16,128]{1,0:T(8,128)}, u32[]{:S(2)}) copy-start(f32[16,128]{1,0:T(8,128)} %get-tuple-element.209) | copy-start | bytes 24580
  276.6 128.3 %copy-start.47 = (f32[16,128]{1,0:T(8,128)S(1)}, f32[16,128]{1,0:T(8,128)}, u32[]{:S(2)}) copy-start(f32[16,128]{1,0:T(8,128)} %get-tuple-element.186) | copy-start | bytes 24580
  276.7 128.3 %copy-start.53 = (f32[16,128]{1,0:T(8,128)S(1)}, f32[16,128]{1,0:T(8,128)}, u32[]{:S(2)}) copy-start(f32[16,128]{1,0:T(8,128)} %get-tuple-element.198) | copy-start | bytes 24580
  276.7 128.3 %copy-start.55 = (f32[16,128]{1,0:T(8,128)S(1)}, f32[16,128]{1,0:T(8,128)}, u32[]{:S(2)}) copy-start(f32[16,128]{1,0:T(8,128)} %get-tuple-element.185) | copy-start | bytes 24580
  276.7 128.3 %copy-start.57 = (f32[16,128]{1,0:T(8,128)S(1)}, f32[16,128]{1,0:T(8,128)}, u32[]{:S(2)}) copy-start(f32[16,128]{1,0:T(8,128)} %get-tuple-element.187) | copy-start | bytes 24580
  388.9 6.2 %collective-permute-start.23 = (f32[3,2,128]{2,1,0:T(2,128)S(1)}, f32[3,2,128]{2,1,0:T(2,128)S(1)}, u32[]{:S(2)}, u32[]{:S(2)}) collective-permute-start(f32[3,2,128]{2,1,0:T(2,128)S(1)} %get-tuple-element.387), channel_id=1, source_target_pairs={{0,16},{16,32},{32,48},{48,64},{64,80},{80,96},{96,112},{112,128},... | collective-permute-start | bytes 9224 | tf_op jit(solution)/shard_map/ppermute | solution.py:18
  393.2 4.9 collective-permute-start.24
  398.2 2.9 collective-permute-start.25
  399.7 4.7 collective-permute-start.26
  (56 other events, 717.2 us)
where the time goes:
time: 517 us; the launch traced here: 516 us
  blocking collectives  333 us (64%)
  starting transfers between devices  77.8 us (15%)
  other arithmetic  36.7 us (7%)
  local copies, waits for them, and re-layouts  34.5 us (7%)
  waiting for transfers between devices  26.9 us (5%)
  between operations  6.52 us (1%)
    psum x3, blocking collectives, inner_sum(): return lax.psum(jnp.sum(first * second), ('gx', 'gy'))  333 us
    ppermute x13, starting transfers between devices, extended_2(): lax.ppermute(tail, axis, [(i, (i + 1) % count) for i in range(ends)])  50.1 us
    ppermute x13, starting transfers between devices, extended_2(): lax.ppermute(head, axis, [((i + 1) % count, i) for i in range(ends)])  25.7 us
    ppermute x13, waiting for transfers between devices, extended_2(): lax.ppermute(head, axis, [((i + 1) % count, i) for i in range(ends)])  22.7 us
    concatenate x1, other arithmetic, local(): jnp.concatenate([jnp.zeros_like(upper_rows), factor, upper_rows], axis=3)  15.7 us
  transfers between devices with their start and end apart: 27, of which 12 were waited for; matrix products, arithmetic and copies ran while one was open for 4% of the time, Pallas kernels for 0%

commit v1 on v0

v1 whole, which is shorter than its diff:
```python
import jax
import jax.numpy as jnp
from jax import lax
from jax.experimental import pallas as pl
from jax.experimental.pallas import tpu as pltpu
from jax.sharding import PartitionSpec as P

NZ = 4
ROWS = 16
LANES = 128
LOWER = 17
PLANES = LOWER * 9
GROUPS = (PLANES + 7) // 8
OWN_TILES = (PLANES + 1) // 2 + 2
CENTRE = 0.8
VMEM_LIMIT = 24 * 1024 * 1024


def bond_offsets():
    return [
        (a, b, c)
        for a in range(-2, 3)
        for b in range(-2, 3)
        for c in range(-2, 3)
        if a * a + b * b + c * c <= 4
    ]


OFFSETS = bond_offsets()


def iota(rows, axis):
    return lax.broadcasted_iota(jnp.int32, (rows, LANES), axis)


def entry(p):
    return (p // 9, (p // 3) % 3, p % 3)


def pack_lanes(planes, width):
    shift = width.bit_length() - 1
    slots = LANES // width
    slot = iota(ROWS, 1) >> shift
    to_left = jnp.zeros((ROWS, LANES), jnp.float32)
    to_right = to_left
    for k, plane in enumerate(planes):
        rolled = pltpu.roll(plane, k * width, 1) if k else plane
        to_left = jnp.where(slot == k, rolled, to_left)
        to_right = jnp.where(slot == (k - 1) % slots, rolled, to_right)
    return to_left, to_right


def unpack_lanes(right, left, width, count):
    shift = width.bit_length() - 1
    even = ((iota(right.shape[0], 1) >> shift) & 1) == 0
    mixed = (jnp.where(even, right, left), jnp.where(even, left, right))
    return [pltpu.roll(mixed[k & 1], LANES - k * width, 1) if k else mixed[0] for k in range(count)]


def pack_rows(first, second):
    upper = iota(8, 0) < 4
    down = jnp.where(upper, first[:8], pltpu.roll(second[:8], 4, 0))
    up = jnp.where(upper, pltpu.roll(second[8:], 4, 0), first[8:])
    return down, up


def unpack_rows(down, up):
    upper = iota(8, 0) < 4
    return jnp.where(upper, down, up), pltpu.roll(jnp.where(upper, up, down), 4, 0)


def pack_inputs(factor, field, to_left, to_right, down, up):
    for g in range(GROUPS):
        planes = [factor[entry(p)] for p in range(8 * g, min(8 * g + 8, PLANES))]
        to_left[g], to_right[g] = pack_lanes(planes, 16)
    to_left[GROUPS], to_right[GROUPS] = pack_lanes([field[k] for k in range(3)], 32)
    for m in range(OWN_TILES - 2):
        first = factor[entry(2 * m)]
        second = factor[entry(min(2 * m + 1, PLANES - 1))]
        down[m], up[m] = pack_rows(first, second)
    down[OWN_TILES - 2], up[OWN_TILES - 2] = pack_rows(field[0], field[1])
    down[OWN_TILES - 1], up[OWN_TILES - 1] = pack_rows(field[2], field[2])


def pack_corners(right, left, down, up):
    for g in range(GROUPS + 1):
        down[g], up[g] = pack_rows(right[g], left[g])


def pack_field(field, right, left, down, up):
    down[0], up[0] = pack_rows(field[0], field[1])
    down[1], up[1] = pack_rows(field[2], field[2])
    down[2], up[2] = pack_rows(right[0], left[0])


def unpack_factor(right, left, own_down, own_up, corner_down, corner_up, edge, halo):
    for m in range(OWN_TILES - 2):
        first, second = unpack_rows(own_down[m], own_up[m])
        edge[2 * m] = first
        if 2 * m + 1 < PLANES:
            edge[2 * m + 1] = second
    for g in range(GROUPS):
        edge_right, edge_left = unpack_rows(corner_down[g], corner_up[g])
        right_all = jnp.concatenate([right[g], edge_right], axis=0)
        left_all = jnp.concatenate([left[g], edge_left], axis=0)
        count = min(8, PLANES - 8 * g)
        for k, plane in enumerate(unpack_lanes(right_all, left_all, 16, count)):
            halo[8 * g + k] = plane


def put(wide, component, tile, values):
    column = pl.ds(tile * LANES, LANES)
    wide[component, 0:8, column] = values[16:24]
    wide[component, 8:32, column] = values
    wide[component, 32:40, column] = values[0:8]


def get(wide, component, tile, shift, rows):
    return wide[component, 8 + shift : 8 + shift + rows, tile * LANES : (tile + 1) * LANES]


def shifted(near, far, by):
    if by == 0:
        return near
    lane = iota(near.shape[0], 1)
    amount = (-by) % LANES
    inside = lane < LANES - by if by > 0 else lane >= -by
    return jnp.where(inside, pltpu.roll(near, amount, 1), pltpu.roll(far, amount, 1))


def layer_ok(rows, dz):
    z = (iota(rows, 1) & (NZ - 1)) + dz
    return (z >= 0) & (z < NZ)


def clipped(values, dz):
    return values if dz == 0 else jnp.where(layer_ok(values.shape[0], dz), values, 0.0)


def by_dx(offsets):
    found = {}
    for index, (dx, dy, dz) in enumerate(offsets):
        found.setdefault(dx, []).append((index, dy, dz))
    return found


def mask_edge(values, edge_out):
    return jnp.concatenate([values[:16], jnp.where(edge_out, 0.0, values[16:24])], axis=0)


def coefficient(factor, edge, halo, plane, tile):
    if tile:
        return halo[plane]
    return jnp.concatenate([factor[entry(plane)], edge[plane]], axis=0)


def apply_factor(factor, edge, halo, wide, edge_out):
    total = [[jnp.zeros((24, LANES), jnp.float32) for _ in range(2)] for _ in range(3)]
    for dx, members in by_dx(OFFSETS[:LOWER]).items():
        base = [[get(wide, j, t, dx, 24) for t in range(2)] for j in range(3)]
        for index, dy, dz in members:
            by = dy * NZ + dz
            for j in range(3):
                for t in range(2):
                    piece = clipped(shifted(base[j][t], base[j][1 - t], by), dz)
                    for i in range(3):
                        total[i][t] += coefficient(factor, edge, halo, 9 * index + 3 * i + j, t) * piece
    return [[mask_edge(total[i][t], edge_out) for t in range(2)] for i in range(3)]


def apply_transpose(factor, edge, halo, image, wide, edge_out, side_out):
    clips = {dz: [[clipped(image[j][t], dz) for t in range(2)] for j in range(3)] for dz in range(-2, 2)}
    final = [[jnp.zeros((24, LANES), jnp.float32) for _ in range(2)] for _ in range(3)]
    for dx, members in sorted(by_dx(OFFSETS[:LOWER]).items()):
        total = [[jnp.zeros((24, LANES), jnp.float32) for _ in range(2)] for _ in range(3)]
        for index, dy, dz in members:
            by = -(dy * NZ + dz)
            for i in range(3):
                parts = []
                for t in range(2):
                    part = coefficient(factor, edge, halo, 9 * index + i, t) * clips[dz][0][t]
                    for j in range(1, 3):
                        part += coefficient(factor, edge, halo, 9 * index + 3 * j + i, t) * clips[dz][j][t]
                    parts.append(part)
                for t in range(2):
                    total[i][t] += shifted(parts[t], parts[1 - t], by)
        if dx:
            for i in range(3):
                for t in range(2):
                    put(wide, i, t, total[i][t])
            total = [[get(wide, i, t, -dx, 24) for t in range(2)] for i in range(3)]
        final = [[final[i][t] + total[i][t] for t in range(2)] for i in range(3)]
    out = []
    for i in range(3):
        row = []
        for t in range(2):
            values = mask_edge(final[i][t], edge_out)
            row.append(jnp.where(side_out, 0.0, values) if t else values)
        out.append(row)
    return out


def apply_operator(stiffness, intact, wide):
    total = [jnp.zeros((ROWS, LANES), jnp.float32) for _ in range(3)]
    for dx, members in by_dx(OFFSETS).items():
        base = [[get(wide, j, t, dx, ROWS) for t in range(2)] for j in range(3)]
        for index, dy, dz in members:
            by = dy * NZ + dz
            weight = None
            if index != 16:
                weight = clipped(intact[index if index < 16 else index - 1].astype(jnp.float32), dz)
            for j in range(3):
                piece = shifted(base[j][0], base[j][1], by)
                if weight is not None:
                    piece = piece * weight
                for i in range(3):
                    total[i] += stiffness[index, i, j] * piece
    return total


def outside(ends):
    sub = iota(8, 0)
    edge_out = ((sub < 4) & (ends[1] == 1)) | ((sub >= 4) & (ends[0] == 1))
    lane = iota(24, 1)
    side_out = ((lane < LANES // 2) & (ends[3] == 1)) | ((lane >= LANES // 2) & (ends[2] == 1))
    return edge_out, side_out


def chain(ends, factor, stiffness, intact, field, pieces, edge, halo, wide):
    edge_out, side_out = outside(ends)
    (down_a, up_a), (down_b, up_b), (down_c, up_c), right, left = pieces
    edges = [*unpack_rows(down_a, up_a), unpack_rows(down_b, up_b)[0]]
    edge_right, edge_left = unpack_rows(down_c, up_c)
    sides = unpack_lanes(
        jnp.concatenate([right, edge_right], axis=0), jnp.concatenate([left, edge_left], axis=0), 32, 3
    )
    for j in range(3):
        put(wide, j, 0, mask_edge(jnp.concatenate([field[j], edges[j]], axis=0), edge_out))
        put(wide, j, 1, mask_edge(sides[j], edge_out))
    image = apply_factor(factor, edge, halo, wide, edge_out)
    zvec = apply_transpose(factor, edge, halo, image, wide, edge_out, side_out)
    for i in range(3):
        for t in range(2):
            put(wide, i, t, zvec[i][t])
    product = apply_operator(stiffness, intact, wide)
    return [image[i][0][:ROWS] for i in range(3)], [zvec[i][0][:ROWS] for i in range(3)], product


def first_half(
    ends, factor, field, stiffness, intact, right, left, own_down, own_up, corner_down, corner_up,
    g_out, z_out, w_out, to_left, to_right, edge, halo, wide,
):
    unpack_factor(right, left, own_down, own_up, corner_down, corner_up, edge, halo)
    a, b, c = OWN_TILES - 2, OWN_TILES - 1, GROUPS
    pieces = (
        (own_down[a], own_up[a]), (own_down[b], own_up[b]), (corner_down[c], corner_up[c]), right[c], left[c],
    )
    image, zvec, product = chain(ends, factor, stiffness, intact, field, pieces, edge, halo, wide)
    for i in range(3):
        g_out[i], z_out[i], w_out[i] = image[i], zvec[i], product[i]
    to_left[0], to_right[0] = pack_lanes(product, 32)


def dot(first, second):
    whole = first[0] * second[0] + first[1] * second[1] + first[2] * second[2]
    return whole[:8] + whole[8:]


def second_half(
    ends, factor, stiffness, intact, right, left, own_down, own_up, corner_down, corner_up,
    g_in, z_in, w_in, field_right, field_left, field_down, field_up,
    u_out, au_out, sums, edge, halo, wide,
):
    unpack_factor(right, left, own_down, own_up, corner_down, corner_up, edge, halo)
    pieces = tuple((field_down[k], field_up[k]) for k in range(3)) + (field_right[0], field_left[0])
    v, u, au = chain(ends, factor, stiffness, intact, w_in, pieces, edge, halo, wide)
    for i in range(3):
        u_out[i], au_out[i] = u[i], au[i]
    g, z, w = ([ref[i] for i in range(3)] for ref in (g_in, z_in, w_in))
    g1 = [g[i] - CENTRE * v[i] for i in range(3)]
    z1 = [z[i] - CENTRE * u[i] for i in range(3)]
    az1 = [w[i] - CENTRE * au[i] for i in range(3)]
    parts = [
        dot(g, g), dot(z, w), dot(g1, g1), dot(g1, v), dot(v, v), dot(z1, az1),
        dot(u, az1) + dot(z1, au), dot(u, au), dot(z1, w) + dot(z, az1), dot(u, w) + dot(z, au),
    ]
    lane = lax.broadcasted_iota(jnp.int32, (1, LANES), 1)
    row = jnp.zeros((1, LANES), jnp.float32)
    for k, part in enumerate(parts):
        value = jnp.sum(jnp.sum(part, axis=0, keepdims=True), axis=1, keepdims=True)
        row = jnp.where(lane == k, value, row)
    for k in range(sums.shape[0]):
        sums[k] = row


def finish(sums, field, z_in, w_in, u_in, au_in, x_out, r_out):
    row = sums[0]
    for k in range(1, sums.shape[0]):
        row = row + sums[k]
    lane = lax.broadcasted_iota(jnp.int32, (1, LANES), 1)
    s = [jnp.sum(jnp.where(lane == k, row, 0.0), axis=1, keepdims=True) for k in range(10)]
    alpha = s[0] / s[1]
    off = alpha - CENTRE
    rho = s[2] - 2.0 * off * s[3] + off * off * s[4]
    beta = rho / s[0]
    zaz = s[5] - off * s[6] + off * off * s[7]
    cross = s[8] - off * s[9]
    last = rho / (zaz + beta * cross + beta * beta * s[1])
    kept = alpha + last * (1.0 + beta)
    turned = last * alpha
    for i in range(3):
        x_out[i] = kept * z_in[i] - turned * u_in[i]
        r_out[i] = field[i] - (kept * w_in[i] - turned * au_in[i])


def shape(*dims):
    return jax.ShapeDtypeStruct(dims, jnp.float32)


def call(body, name, outs, scratch=(), scalars=0):
    def run(*operands):
        specs = [pl.BlockSpec(memory_space=pltpu.SMEM)] * scalars
        specs += [pl.BlockSpec(memory_space=pltpu.VMEM)] * (len(operands) - scalars)
        return pl.pallas_call(
            body,
            out_shape=outs,
            in_specs=specs,
            out_specs=[pl.BlockSpec(memory_space=pltpu.VMEM)] * len(outs),
            scratch_shapes=list(scratch),
            compiler_params=pltpu.CompilerParams(vmem_limit_bytes=VMEM_LIMIT),
            name=name,
        )(*operands)

    return run


def swap(first, second, axis, wrap):
    count = lax.axis_size(axis)
    ends = count if wrap else count - 1
    back = [((i + 1) % count, i) for i in range(ends)]
    ahead = [(i, (i + 1) % count) for i in range(ends)]
    return lax.ppermute(first, axis, back), lax.ppermute(second, axis, ahead)


def total_of(row, axis, nxt):
    got = lax.all_to_all(row, axis, 0, 0)
    if nxt is None:
        return got
    return jnp.broadcast_to(jnp.sum(got, axis=0)[None], (nxt, 1, LANES))


def local(right_side, stiffness, factor, intact):
    gx, gy = lax.axis_index("gx"), lax.axis_index("gy")
    nx, ny = lax.axis_size("gx"), lax.axis_size("gy")
    ends = jnp.stack([gx == 0, gx == nx - 1, gy == 0, gy == ny - 1]).astype(jnp.int32)
    plane = shape(3, ROWS, LANES)
    strip = shape(GROUPS + 1, ROWS, LANES)
    own = shape(OWN_TILES, 8, LANES)
    corner = shape(GROUPS + 1, 8, LANES)
    small = shape(1, ROWS, LANES)
    edges = shape(3, 8, LANES)
    scratch = (
        pltpu.VMEM((PLANES, 8, LANES), jnp.float32),
        pltpu.VMEM((PLANES, 24, LANES), jnp.float32),
        pltpu.VMEM((3, 40, 2 * LANES), jnp.float32),
    )

    to_left, to_right, down, up = call(pack_inputs, "pack_inputs", [strip, strip, own, own])(factor, right_side)
    right, left = swap(to_left, to_right, "gy", False)
    own_down, own_up = swap(down, up, "gx", True)
    down, up = call(pack_corners, "pack_corners", [corner, corner])(right, left)
    corner_down, corner_up = swap(down, up, "gx", True)
    halos = (right, left, own_down, own_up, corner_down, corner_up)

    g, z, w, to_left, to_right = call(
        first_half, "first_half", [plane, plane, plane, small, small], scratch, 1
    )(ends, factor, right_side, stiffness, intact, *halos)
    field_right, field_left = swap(to_left, to_right, "gy", False)
    down, up = call(pack_field, "pack_field", [edges, edges])(w, field_right, field_left)
    field_down, field_up = swap(down, up, "gx", True)
    u, au, sums = call(second_half, "second_half", [plane, plane, shape(ny, 1, LANES)], scratch, 1)(
        ends, factor, stiffness, intact, *halos, g, z, w, field_right, field_left, field_down, field_up
    )
    sums = total_of(total_of(sums, "gy", nx), "gx", None)
    x, r = call(finish, "finish", [plane, plane])(sums, right_side, z, w, u, au)
    return x, r


def solution(mesh):
    in_specs = (
        P(None, "gx", "gy"),
        P(None, None, None, "gx", "gy"),
        P(None, None, None, "gx", "gy"),
        P(None, "gx", "gy"),
    )
    out_specs = (P(None, "gx", "gy"), P(None, "gx", "gy"))
    return jax.shard_map(local, mesh=mesh, in_specs=in_specs, out_specs=out_specs, check_vma=False)
```

time: 517 us -> 88.2 us (0.17)
  blocking collectives: 333 us -> 40.2 us
  starting transfers between devices: 77.8 us -> 27.8 us
  other arithmetic: 36.7 us -> 0.11 us
  local copies, waits for them, and re-layouts: 34.5 us -> 5.42 us
  waiting for transfers between devices: 26.9 us -> 7.58 us
  Pallas kernels: 0 us -> 5.89 us
  between operations: 6.52 us -> 0.73 us
    psum x3 -> x0, blocking collectives: 333 us -> none  [inner_sum(): return lax.psum(jnp.sum(first * second), ('gx', 'gy'))]
    ppermute x27 -> x10, starting transfers between devices: 77.8 us -> 27.8 us  [swap(): return (lax.ppermute(first, axis, back), lax.ppermute(second, axis, ahead))]
    all_to_all x0 -> x2, blocking collectives: none -> 40.2 us  [total_of(): got = lax.all_to_all(row, axis, 0, 0)]
    ppermute x27 -> x10, waiting for transfers between devices: 26.9 us -> 7.58 us  [swap(): return (lax.ppermute(first, axis, back), lax.ppermute(second, axis, ahead))]
    concatenate x13 -> x0, other arithmetic: 16.4 us -> none  [the longest x1 15.7 us: local(): jnp.concatenate([jnp.zeros_like(upper_rows), factor, upper_rows], axis=3)]
    reduce_sum x36 -> x1, other arithmetic: 14.4 us -> 0.03 us  [total_of(): return jnp.broadcast_to(jnp.sum(got, axis=0)[None], (nxt, 1, LANES))]
    ppermute x3 -> x0, local copies, waits for them, and re-layouts: 13.3 us -> none  [the longest x1 6.62 us: from_behind(): return lax.ppermute(shard, axis, pairs)]
    concatenate x3 -> x0, local copies, waits for them, and re-layouts: 8.94 us -> none  [local(): jnp.concatenate([jnp.zeros_like(upper_rows), factor, upper_rows], axis=3)]
  transfers between devices with their start and end apart: 27 -> 10, of which waited for: 12 -> 7; matrix products, arithmetic and copies ran while one was open for 4% -> 0% of each run, Pallas kernels for 0% -> 0%
where the time goes in v1:
time: 88.2 us; the launch traced here: 87.7 us
  blocking collectives  40.2 us (46%)
  starting transfers between devices  27.8 us (32%)
  waiting for transfers between devices  7.58 us (9%)
  Pallas kernels  5.89 us (7%)
  local copies, waits for them, and re-layouts  5.42 us (6%)
    all_to_all x2, blocking collectives, total_of(): got = lax.all_to_all(row, axis, 0, 0)  40.2 us
    ppermute x10, starting transfers between devices, swap(): return (lax.ppermute(first, axis, back), lax.ppermute(second, axis, ahead))  27.8 us
    ppermute x10, waiting for transfers between devices, swap(): return (lax.ppermute(first, axis, back), lax.ppermute(second, axis, ahead))  7.58 us
    pallas_call x6, Pallas kernels, run(): pl.pallas_call(body, out_shape=outs, in_specs=specs, out_specs=[pl.BlockS...  5.89 us
    unnamed x16, local copies, waits for them, and re-layouts  5.41 us
  transfers between devices with their start and end apart: 10, of which 7 were waited for; matrix products, arithmetic and copies ran while one was open for 0% of the time, Pallas kernels for 0%

profile of v1, /device:TPU:1, one launch (start us, length us, event | category | flops | bytes accessed | tf_op | source)
XLA Modules:
  0.0 87.7 jit_solution(1664949772340883460)
XLA Ops:
  0.6 0.0 copy-start
  0.6 1.3 %copy-done = f32[17,3,3,16,128]{4,3,2,1,0:T(8,128)S(1)} copy-done((f32[17,3,3,16,128]{4,3,2,1,0:T(8,128)S(1)}, f32[17,3,3,16,128]{4,3,2,1,0:T(8,128)}, u32[]{:S(2)}) %copy-start) | copy-done | bytes 1253400
  1.9 0.0 copy-start.5
  1.9 0.7 copy-done.5
  2.7 0.0 copy-start.1
  2.7 0.4 pack_inputs.1
  3.0 6.9 %collective-permute-start.2 = (f32[79,8,128]{2,1,0:T(8,128)S(1)}, f32[79,8,128]{2,1,0:T(8,128)S(1)}, u32[]{:S(2)}, u32[]{:S(2)}) collective-permute-start(f32[79,8,128]{2,1,0:T(8,128)S(1)} %get-tuple-element.20), channel_id=1, source_target_pairs={{16,0},{32,16},{48,32},{64,48},{80,64},{96,80},{112,96},{128,112},... | collective-permute-start | bytes 970760 | tf_op jit(solution)/shard_map/ppermute | solution.py:342
  9.9 0.0 collective-permute-start.3
  9.9 1.3 %collective-permute-start = (f32[21,16,128]{2,1,0:T(8,128)S(1)}, f32[21,16,128]{2,1,0:T(8,128)S(1)}, u32[]{:S(2)}, u32[]{:S(2)}) collective-permute-start(f32[21,16,128]{2,1,0:T(8,128)S(1)} %get-tuple-element.18), channel_id=1, source_target_pairs={{1,0},{2,1},{3,2},{4,3},{5,4},{6,5},{7,6},{8,7},{9,8},{10,9},{11,1... | collective-permute-start | bytes 516104 | tf_op jit(solution)/shard_map/ppermute | solution.py:342
  11.2 4.0 %collective-permute-start.1 = (f32[21,16,128]{2,1,0:T(8,128)S(1)}, f32[21,16,128]{2,1,0:T(8,128)S(1)}, u32[]{:S(2)}, u32[]{:S(2)}) collective-permute-start(f32[21,16,128]{2,1,0:T(8,128)S(1)} %get-tuple-element.19), channel_id=1, source_target_pairs={{0,1},{1,2},{2,3},{3,4},{4,5},{5,6},{6,7},{7,8},{8,9},{9,10},{10,1... | collective-permute-start | bytes 516104 | tf_op jit(solution)/shard_map/ppermute | solution.py:342
  15.2 0.8 collective-permute-done.right
  16.1 1.5 %collective-permute-done.1.left = f32[21,16,128]{2,1,0:T(8,128)S(1)} collective-permute-done((f32[21,16,128]{2,1,0:T(8,128)S(1)}, f32[21,16,128]{2,1,0:T(8,128)S(1)}, u32[]{:S(2)}, u32[]{:S(2)}) %collective-permute-start.1) | collective-permute-done | bytes 172064 | tf_op jit(solution)/shard_map/ppermute | solution.py:342
  17.6 4.7 %collective-permute-start.4 = (f32[21,8,128]{2,1,0:T(8,128)S(1)}, f32[21,8,128]{2,1,0:T(8,128)S(1)}, u32[]{:S(2)}, u32[]{:S(2)}) collective-permute-start(f32[21,8,128]{2,1,0:T(8,128)S(1)} %get-tuple-element.22), channel_id=1, source_target_pairs={{16,0},{32,16},{48,32},{64,48},{80,64},{96,80},{112,96},{128,112},... | collective-permute-start | bytes 258056 | tf_op jit(solution)/shard_map/ppermute | solution.py:342
  22.3 0.0 collective-permute-start.5
  22.3 0.1 add_convert_fusion.ends
  22.4 0.8 collective-permute-done.4.corner_down
  23.2 2.5 %collective-permute-done.5.corner_up = f32[21,8,128]{2,1,0:T(8,128)S(1)} collective-permute-done((f32[21,8,128]{2,1,0:T(8,128)S(1)}, f32[21,8,128]{2,1,0:T(8,128)S(1)}, u32[]{:S(2)}, u32[]{:S(2)}) %collective-permute-start.5) | collective-permute-done | bytes 86048 | tf_op jit(solution)/shard_map/ppermute | solution.py:342
  25.7 0.0 collective-permute-done.2.own_down
  25.7 0.0 collective-permute-done.3.own_up
  25.7 0.0 copy-done.1
  25.7 0.0 copy-start.2
  25.7 1.7 %copy-done.2 = f32[33,3,3,16,128]{4,3,2,1,0:T(8,128)S(1)} copy-done((f32[33,3,3,16,128]{4,3,2,1,0:T(8,128)S(1)}, f32[33,3,3,16,128]{4,3,2,1,0:T(8,128)}, u32[]{:S(2)}) %copy-start.2) | copy-done | bytes 2433048
  27.4 0.0 copy-start.4
  27.4 0.9 %copy-done.4 = s32[32,16,128]{2,1,0:T(8,128)S(1)} copy-done((s32[32,16,128]{2,1,0:T(8,128)S(1)}, s32[32,16,128]{2,1,0:T(8,128)}, u32[]{:S(2)}) %copy-start.4) | copy-done | bytes 262168
  28.3 0.0 copy-start.6
  28.3 0.7 copy-done.6
  29.1 0.0 copy-start.3
  29.1 2.3 %first_half.1 = (f32[3,16,128]{2,1,0:T(8,128)S(1)}, f32[3,16,128]{2,1,0:T(8,128)S(1)}, f32[3,16,128]{2,1,0:T(8,128)S(1)}, f32[1,16,128]{2,1,0:T(8,128)S(1)}, f32[1,16,128]{2,1,0:T(8,128)S(1)}) custom-call(s32[4]{0:T(128)S(1)} %add_convert_fusion.ends, f32[17,3,3,16,128]{4,3,2,1,0:T(8,128)S(1)} %copy-done.1, f32[3,16,128]{2,1,0:T(8,128)S(1)} %copy-done.6, ...), custom_call_target="tpu_custom_call" | custom-call | tf_op jit(solution)/shard_map/first_half/pallas_call | solution.py:324
  31.4 1.3 %collective-permute-start.6 = (f32[1,16,128]{2,1,0:T(8,128)S(1)}, f32[1,16,128]{2,1,0:T(8,128)S(1)}, u32[]{:S(2)}, u32[]{:S(2)}) collective-permute-start(f32[1,16,128]{2,1,0:T(8,128)S(1)} %get-tuple-element.27), channel_id=1, source_target_pairs={{1,0},{2,1},{3,2},{4,3},{5,4},{6,5},{7,6},{8,7},{9,8},{10,9},{11,1... | collective-permute-start | bytes 24584 | tf_op jit(solution)/shard_map/ppermute | solution.py:342
  32.7 4.4 %collective-permute-start.7 = (f32[1,16,128]{2,1,0:T(8,128)S(1)}, f32[1,16,128]{2,1,0:T(8,128)S(1)}, u32[]{:S(2)}, u32[]{:S(2)}) collective-permute-start(f32[1,16,128]{2,1,0:T(8,128)S(1)} %get-tuple-element.28), channel_id=1, source_target_pairs={{0,1},{1,2},{2,3},{3,4},{4,5},{5,6},{6,7},{7,8},{8,9},{9,10},{10,1... | collective-permute-start | bytes 24584 | tf_op jit(solution)/shard_map/ppermute | solution.py:342
  37.2 0.0 collective-permute-done.6.right.field_right
  37.2 0.8 collective-permute-done.7.left.field_left
  37.9 5.2 %collective-permute-start.8 = (f32[3,8,128]{2,1,0:T(8,128)S(1)}, f32[3,8,128]{2,1,0:T(8,128)S(1)}, u32[]{:S(2)}, u32[]{:S(2)}) collective-permute-start(f32[3,8,128]{2,1,0:T(8,128)S(1)} %get-tuple-element.29), channel_id=1, source_target_pairs={{16,0},{32,16},{48,32},{64,48},{80,64},{96,80},{112,96},{128,112},... | collective-permute-start | bytes 36872 | tf_op jit(solution)/shard_map/ppermute | solution.py:342
  43.1 0.0 collective-permute-start.9
  43.1 0.8 collective-permute-done.8.field_down
  44.0 0.3 collective-permute-done.9.field_up
  44.3 0.0 copy-done.3
  44.3 0.0 copy-start.7
  44.3 2.4 %second_half.1 = (f32[3,16,128]{2,1,0:T(8,128)S(1)}, f32[3,16,128]{2,1,0:T(8,128)S(1)}, f32[16,1,128]{2,1,0:T(1,128)S(1)}) custom-call(s32[4]{0:T(128)S(1)} %add_convert_fusion.ends, f32[17,3,3,16,128]{4,3,2,1,0:T(8,128)S(1)} %copy-done.1, f32[33,3,3,16,128]{4,3,2,1,0:T(8,128)S(1)} %copy-done.3, s32[32,16,128]{2,1,0:T(8,128)S(1)} %copy-done.4, ...), custom_call_target="tpu_custom_call" | custom-call | tf_op jit(solution)/shard_map/second_half/pallas_call | solution.py:324
  46.7 17.8 %all_to_all.10 = f32[16,1,128]{2,1,0:T(1,128)S(1)} all-to-all(f32[16,1,128]{2,1,0:T(1,128)S(1)} %get-tuple-element.31), channel_id=1, replica_groups=mesh['gx'=32,'gy'=16] {'gy'}, dimensions={0} | all-to-all | bytes 16384 | tf_op jit(solution)/shard_map/all_to_all | solution.py:346
  64.6 22.4 %all_to_all.11.sums = f32[32,1,128]{2,1,0:T(1,128)S(1)} all-to-all(f32[32,1,128]{2,1,0:T(1,128)S(1)} %broadcast_in_dim.2), channel_id=1, replica_groups=mesh['gx'=32,'gy'=16] {'gx'}, dimensions={0} | all-to-all | bytes 32768 | tf_op jit(solution)/shard_map/all_to_all | solution.py:346
  87.0 0.0 copy-done.7
  87.0 0.8 finish.1
  (4 shorter events, 0.1 us)
Async XLA Ops:
  0.6 1.3 %copy-start = (f32[17,3,3,16,128]{4,3,2,1,0:T(8,128)S(1)}, f32[17,3,3,16,128]{4,3,2,1,0:T(8,128)}, u32[]{:S(2)}) copy-start(f32[17,3,3,16,128]{4,3,2,1,0:T(8,128)} %factor.5) | copy-start | bytes 3760132
  1.9 0.7 copy-start.5
  2.7 23.0 %copy-start.1 = (f32[17,3,3,16,128]{4,3,2,1,0:T(8,128)S(1)}, f32[17,3,3,16,128]{4,3,2,1,0:T(8,128)}, u32[]{:S(2)}) copy-start(f32[17,3,3,16,128]{4,3,2,1,0:T(8,128)} %factor.5) | copy-start | bytes 3760132
  3.0 22.7 %collective-permute-start.2 = (f32[79,8,128]{2,1,0:T(8,128)S(1)}, f32[79,8,128]{2,1,0:T(8,128)S(1)}, u32[]{:S(2)}, u32[]{:S(2)}) collective-permute-start(f32[79,8,128]{2,1,0:T(8,128)S(1)} %get-tuple-element.20), channel_id=1, source_target_pairs={{16,0},{32,16},{48,32},{64,48},{80,64},{96,80},{112,96},{128,112},... | collective-permute-start | bytes 970760 | tf_op jit(solution)/shard_map/ppermute | solution.py:342
  9.9 15.8 %collective-permute-start.3 = (f32[79,8,128]{2,1,0:T(8,128)S(1)}, f32[79,8,128]{2,1,0:T(8,128)S(1)}, u32[]{:S(2)}, u32[]{:S(2)}) collective-permute-start(f32[79,8,128]{2,1,0:T(8,128)S(1)} %get-tuple-element.21), channel_id=1, source_target_pairs={{0,16},{16,32},{32,48},{48,64},{64,80},{80,96},{96,112},{112,128},... | collective-permute-start | bytes 970760 | tf_op jit(solution)/shard_map/ppermute | solution.py:342
  9.9 6.1 %collective-permute-start = (f32[21,16,128]{2,1,0:T(8,128)S(1)}, f32[21,16,128]{2,1,0:T(8,128)S(1)}, u32[]{:S(2)}, u32[]{:S(2)}) collective-permute-start(f32[21,16,128]{2,1,0:T(8,128)S(1)} %get-tuple-element.18), channel_id=1, source_target_pairs={{1,0},{2,1},{3,2},{4,3},{5,4},{6,5},{7,6},{8,7},{9,8},{10,9},{11,1... | collective-permute-start | bytes 516104 | tf_op jit(solution)/shard_map/ppermute | solution.py:342
  11.2 6.3 %collective-permute-start.1 = (f32[21,16,128]{2,1,0:T(8,128)S(1)}, f32[21,16,128]{2,1,0:T(8,128)S(1)}, u32[]{:S(2)}, u32[]{:S(2)}) collective-permute-start(f32[21,16,128]{2,1,0:T(8,128)S(1)} %get-tuple-element.19), channel_id=1, source_target_pairs={{0,1},{1,2},{2,3},{3,4},{4,5},{5,6},{6,7},{7,8},{8,9},{9,10},{10,1... | collective-permute-start | bytes 516104 | tf_op jit(solution)/shard_map/ppermute | solution.py:342
  17.6 5.6 %collective-permute-start.4 = (f32[21,8,128]{2,1,0:T(8,128)S(1)}, f32[21,8,128]{2,1,0:T(8,128)S(1)}, u32[]{:S(2)}, u32[]{:S(2)}) collective-permute-start(f32[21,8,128]{2,1,0:T(8,128)S(1)} %get-tuple-element.22), channel_id=1, source_target_pairs={{16,0},{32,16},{48,32},{64,48},{80,64},{96,80},{112,96},{128,112},... | collective-permute-start | bytes 258056 | tf_op jit(solution)/shard_map/ppermute | solution.py:342
  22.3 3.4 %collective-permute-start.5 = (f32[21,8,128]{2,1,0:T(8,128)S(1)}, f32[21,8,128]{2,1,0:T(8,128)S(1)}, u32[]{:S(2)}, u32[]{:S(2)}) collective-permute-start(f32[21,8,128]{2,1,0:T(8,128)S(1)} %get-tuple-element.23), channel_id=1, source_target_pairs={{0,16},{16,32},{32,48},{48,64},{64,80},{80,96},{96,112},{112,128},... | collective-permute-start | bytes 258056 | tf_op jit(solution)/shard_map/ppermute | solution.py:342
  25.7 1.7 %copy-start.2 = (f32[33,3,3,16,128]{4,3,2,1,0:T(8,128)S(1)}, f32[33,3,3,16,128]{4,3,2,1,0:T(8,128)}, u32[]{:S(2)}) copy-start(f32[33,3,3,16,128]{4,3,2,1,0:T(8,128)} %stiffness.3) | copy-start | bytes 7299076
  27.4 0.9 %copy-start.4 = (s32[32,16,128]{2,1,0:T(8,128)S(1)}, s32[32,16,128]{2,1,0:T(8,128)}, u32[]{:S(2)}) copy-start(s32[32,16,128]{2,1,0:T(8,128)} %intact.3) | copy-start | bytes 786436
  28.3 0.7 copy-start.6
  29.1 15.3 %copy-start.3 = (f32[33,3,3,16,128]{4,3,2,1,0:T(8,128)S(1)}, f32[33,3,3,16,128]{4,3,2,1,0:T(8,128)}, u32[]{:S(2)}) copy-start(f32[33,3,3,16,128]{4,3,2,1,0:T(8,128)} %stiffness.3) | copy-start | bytes 7299076
  31.4 5.7 %collective-permute-start.6 = (f32[1,16,128]{2,1,0:T(8,128)S(1)}, f32[1,16,128]{2,1,0:T(8,128)S(1)}, u32[]{:S(2)}, u32[]{:S(2)}) collective-permute-start(f32[1,16,128]{2,1,0:T(8,128)S(1)} %get-tuple-element.27), channel_id=1, source_target_pairs={{1,0},{2,1},{3,2},{4,3},{5,4},{6,5},{7,6},{8,7},{9,8},{10,9},{11,1... | collective-permute-start | bytes 24584 | tf_op jit(solution)/shard_map/ppermute | solution.py:342
  32.7 5.2 %collective-permute-start.7 = (f32[1,16,128]{2,1,0:T(8,128)S(1)}, f32[1,16,128]{2,1,0:T(8,128)S(1)}, u32[]{:S(2)}, u32[]{:S(2)}) collective-permute-start(f32[1,16,128]{2,1,0:T(8,128)S(1)} %get-tuple-element.28), channel_id=1, source_target_pairs={{0,1},{1,2},{2,3},{3,4},{4,5},{5,6},{6,7},{7,8},{8,9},{9,10},{10,1... | collective-permute-start | bytes 24584 | tf_op jit(solution)/shard_map/ppermute | solution.py:342
  37.9 6.0 %collective-permute-start.8 = (f32[3,8,128]{2,1,0:T(8,128)S(1)}, f32[3,8,128]{2,1,0:T(8,128)S(1)}, u32[]{:S(2)}, u32[]{:S(2)}) collective-permute-start(f32[3,8,128]{2,1,0:T(8,128)S(1)} %get-tuple-element.29), channel_id=1, source_target_pairs={{16,0},{32,16},{48,32},{64,48},{80,64},{96,80},{112,96},{128,112},... | collective-permute-start | bytes 36872 | tf_op jit(solution)/shard_map/ppermute | solution.py:342
  43.1 1.2 %collective-permute-start.9 = (f32[3,8,128]{2,1,0:T(8,128)S(1)}, f32[3,8,128]{2,1,0:T(8,128)S(1)}, u32[]{:S(2)}, u32[]{:S(2)}) collective-permute-start(f32[3,8,128]{2,1,0:T(8,128)S(1)} %get-tuple-element.30), channel_id=1, source_target_pairs={{0,16},{16,32},{32,48},{48,64},{64,80},{80,96},{96,112},{112,128},... | collective-permute-start | bytes 36872 | tf_op jit(solution)/shard_map/ppermute | solution.py:342
  44.3 42.6 %copy-start.7 = (f32[3,16,128]{2,1,0:T(8,128)S(1)}, f32[3,16,128]{2,1,0:T(8,128)}, u32[]{:S(2)}) copy-start(f32[3,16,128]{2,1,0:T(8,128)} %field.5) | copy-start | bytes 73732

commit v2 on v1

--- a/solution.py
+++ b/solution.py
@@ -14,6 +14,7 @@
 OWN_TILES = (PLANES + 1) // 2 + 2
 CENTRE = 0.8
 VMEM_LIMIT = 24 * 1024 * 1024
+WIDE_LIMIT = 53477376
 
 
 def bond_offsets():
@@ -69,17 +70,46 @@
     return jnp.where(upper, down, up), pltpu.roll(jnp.where(upper, up, down), 4, 0)
 
 
-def pack_inputs(factor, field, to_left, to_right, down, up):
-    for g in range(GROUPS):
-        planes = [factor[entry(p)] for p in range(8 * g, min(8 * g + 8, PLANES))]
-        to_left[g], to_right[g] = pack_lanes(planes, 16)
+CHUNKS = ((0, 5), (5, 9), (9, 13), (13, LOWER))
+
+
+def pack_inputs(factor_hbm, field_hbm, factor, field, to_left, to_right, down, up, sems):
+    copies = [pltpu.make_async_copy(field_hbm, field, sems.at[len(CHUNKS)])]
+    for k, (low, high) in enumerate(CHUNKS):
+        part = pl.ds(low, high - low)
+        copies.append(pltpu.make_async_copy(factor_hbm.at[part], factor.at[part], sems.at[k]))
+    for copy in copies:
+        copy.start()
+    copies[0].wait()
     to_left[GROUPS], to_right[GROUPS] = pack_lanes([field[k] for k in range(3)], 32)
-    for m in range(OWN_TILES - 2):
-        first = factor[entry(2 * m)]
-        second = factor[entry(min(2 * m + 1, PLANES - 1))]
-        down[m], up[m] = pack_rows(first, second)
     down[OWN_TILES - 2], up[OWN_TILES - 2] = pack_rows(field[0], field[1])
     down[OWN_TILES - 1], up[OWN_TILES - 1] = pack_rows(field[2], field[2])
+    group = tile = 0
+    for k, (low, high) in enumerate(CHUNKS):
+        copies[1 + k].wait()
+        ready = 9 * high
+        while group < GROUPS and min(8 * group + 8, PLANES) <= ready:
+            planes = [factor[entry(p)] for p in range(8 * group, min(8 * group + 8, PLANES))]
+            to_left[group], to_right[group] = pack_lanes(planes, 16)
+            group += 1
+        while tile < OWN_TILES - 2 and min(2 * tile + 2, PLANES) <= ready:
+            down[tile], up[tile] = pack_rows(factor[entry(2 * tile)], factor[entry(min(2 * tile + 1, PLANES - 1))])
+            tile += 1
+
+
+def weigh(stiffness_hbm, intact_hbm, weighted, intact, sems):
+    bonds = pltpu.make_async_copy(intact_hbm, intact, sems.at[0])
+    blocks = pltpu.make_async_copy(stiffness_hbm, weighted, sems.at[1])
+    bonds.start()
+    blocks.start()
+    bonds.wait()
+    blocks.wait()
+    for index, (_, _, dz) in enumerate(OFFSETS):
+        if index != 16:
+            weight = clipped(intact[index if index < 16 else index - 1].astype(jnp.float32), dz)
+            for i in range(3):
+                for j in range(3):
+                    weighted[index, i, j] = weighted[index, i, j] * weight
 
 
 def pack_corners(right, left, down, up):
@@ -93,19 +123,22 @@
     down[2], up[2] = pack_rows(right[0], left[0])
 
 
-def unpack_factor(right, left, own_down, own_up, corner_down, corner_up, edge, halo):
+def unpack_sides(right, left, own_down, own_up, corner_down, edge, side):
     for m in range(OWN_TILES - 2):
         first, second = unpack_rows(own_down[m], own_up[m])
         edge[2 * m] = first
         if 2 * m + 1 < PLANES:
             edge[2 * m + 1] = second
     for g in range(GROUPS):
-        edge_right, edge_left = unpack_rows(corner_down[g], corner_up[g])
-        right_all = jnp.concatenate([right[g], edge_right], axis=0)
-        left_all = jnp.concatenate([left[g], edge_left], axis=0)
-        count = min(8, PLANES - 8 * g)
-        for k, plane in enumerate(unpack_lanes(right_all, left_all, 16, count)):
-            halo[8 * g + k] = plane
+        for k, plane in enumerate(unpack_lanes(right[g], left[g], 16, min(8, PLANES - 8 * g))):
+            side[8 * g + k] = plane
+
+
+def unpack_corners(corner_down, corner_up, corner):
+    for g in range(GROUPS):
+        right, left = unpack_rows(corner_down[g], corner_up[g])
+        for k, plane in enumerate(unpack_lanes(right, left, 16, min(8, PLANES - 8 * g))):
+            corner[8 * g + k] = plane
 
 
 def put(wide, component, tile, values):
@@ -148,13 +181,14 @@
     return jnp.concatenate([values[:16], jnp.where(edge_out, 0.0, values[16:24])], axis=0)
 
 
-def coefficient(factor, edge, halo, plane, tile):
+def coefficient(blocks, plane, tile):
+    factor, edge, side, corner = blocks
     if tile:
-        return halo[plane]
+        return jnp.concatenate([side[plane], corner[plane]], axis=0)
     return jnp.concatenate([factor[entry(plane)], edge[plane]], axis=0)
 
 
-def apply_factor(factor, edge, halo, wide, edge_out):
+def apply_factor(blocks, wide, edge_out):
     total = [[jnp.zeros((24, LANES), jnp.float32) for _ in range(2)] for _ in range(3)]
     for dx, members in by_dx(OFFSETS[:LOWER]).items():
         base = [[get(wide, j, t, dx, 24) for t in range(2)] for j in range(3)]
@@ -164,11 +198,11 @@
                 for t in range(2):
                     piece = clipped(shifted(base[j][t], base[j][1 - t], by), dz)
                     for i in range(3):
-                        total[i][t] += coefficient(factor, edge, halo, 9 * index + 3 * i + j, t) * piece
+                        total[i][t] += coefficient(blocks, 9 * index + 3 * i + j, t) * piece
     return [[mask_edge(total[i][t], edge_out) for t in range(2)] for i in range(3)]
 
 
-def apply_transpose(factor, edge, halo, image, wide, edge_out, side_out):
+def apply_transpose(blocks, image, wide, edge_out, side_out):
     clips = {dz: [[clipped(image[j][t], dz) for t in range(2)] for j in range(3)] for dz in range(-2, 2)}
     final = [[jnp.zeros((24, LANES), jnp.float32) for _ in range(2)] for _ in range(3)]
     for dx, members in sorted(by_dx(OFFSETS[:LOWER]).items()):
@@ -178,9 +212,9 @@
             for i in range(3):
                 parts = []
                 for t in range(2):
-                    part = coefficient(factor, edge, halo, 9 * index + i, t) * clips[dz][0][t]
+                    part = coefficient(blocks, 9 * index + i, t) * clips[dz][0][t]
                     for j in range(1, 3):
-                        part += coefficient(factor, edge, halo, 9 * index + 3 * j + i, t) * clips[dz][j][t]
+                        part += coefficient(blocks, 9 * index + 3 * j + i, t) * clips[dz][j][t]
                     parts.append(part)
                 for t in range(2):
                     total[i][t] += shifted(parts[t], parts[1 - t], by)
@@ -200,21 +234,15 @@
     return out
 
 
-def apply_operator(stiffness, intact, wide):
+def apply_operator(weighted, wide):
     total = [jnp.zeros((ROWS, LANES), jnp.float32) for _ in range(3)]
     for dx, members in by_dx(OFFSETS).items():
         base = [[get(wide, j, t, dx, ROWS) for t in range(2)] for j in range(3)]
         for index, dy, dz in members:
-            by = dy * NZ + dz
-            weight = None
-            if index != 16:
-                weight = clipped(intact[index if index < 16 else index - 1].astype(jnp.float32), dz)
             for j in range(3):
-                piece = shifted(base[j][0], base[j][1], by)
-                if weight is not None:
-                    piece = piece * weight
+                piece = shifted(base[j][0], base[j][1], dy * NZ + dz)
                 for i in range(3):
-                    total[i] += stiffness[index, i, j] * piece
+                    total[i] += weighted[index, i, j] * piece
     return total
 
 
@@ -226,7 +254,7 @@
     return edge_out, side_out
 
 
-def chain(ends, factor, stiffness, intact, field, pieces, edge, halo, wide):
+def chain(ends, blocks, weighted, field, pieces, wide):
     edge_out, side_out = outside(ends)
     (down_a, up_a), (down_b, up_b), (down_c, up_c), right, left = pieces
     edges = [*unpack_rows(down_a, up_a), unpack_rows(down_b, up_b)[0]]
@@ -237,25 +265,25 @@
     for j in range(3):
         put(wide, j, 0, mask_edge(jnp.concatenate([field[j], edges[j]], axis=0), edge_out))
         put(wide, j, 1, mask_edge(sides[j], edge_out))
-    image = apply_factor(factor, edge, halo, wide, edge_out)
-    zvec = apply_transpose(factor, edge, halo, image, wide, edge_out, side_out)
+    image = apply_factor(blocks, wide, edge_out)
+    zvec = apply_transpose(blocks, image, wide, edge_out, side_out)
     for i in range(3):
         for t in range(2):
             put(wide, i, t, zvec[i][t])
-    product = apply_operator(stiffness, intact, wide)
+    product = apply_operator(weighted, wide)
     return [image[i][0][:ROWS] for i in range(3)], [zvec[i][0][:ROWS] for i in range(3)], product
 
 
 def first_half(
-    ends, factor, field, stiffness, intact, right, left, own_down, own_up, corner_down, corner_up,
-    g_out, z_out, w_out, to_left, to_right, edge, halo, wide,
+    ends, factor, edge, side, weighted, field, right, left, own_down, own_up, corner_down, corner_up,
+    corner, g_out, z_out, w_out, to_left, to_right, wide,
 ):
-    unpack_factor(right, left, own_down, own_up, corner_down, corner_up, edge, halo)
+    unpack_corners(corner_down, corner_up, corner)
     a, b, c = OWN_TILES - 2, OWN_TILES - 1, GROUPS
     pieces = (
         (own_down[a], own_up[a]), (own_down[b], own_up[b]), (corner_down[c], corner_up[c]), right[c], left[c],
     )
-    image, zvec, product = chain(ends, factor, stiffness, intact, field, pieces, edge, halo, wide)
+    image, zvec, product = chain(ends, (factor, edge, side, corner), weighted, field, pieces, wide)
     for i in range(3):
         g_out[i], z_out[i], w_out[i] = image[i], zvec[i], product[i]
     to_left[0], to_right[0] = pack_lanes(product, 32)
@@ -267,13 +295,11 @@
 
 
 def second_half(
-    ends, factor, stiffness, intact, right, left, own_down, own_up, corner_down, corner_up,
-    g_in, z_in, w_in, field_right, field_left, field_down, field_up,
-    u_out, au_out, sums, edge, halo, wide,
+    ends, factor, edge, side, weighted, corner, g_in, z_in, w_in, field_right, field_left, field_down, field_up,
+    u_out, au_out, sums, wide,
 ):
-    unpack_factor(right, left, own_down, own_up, corner_down, corner_up, edge, halo)
     pieces = tuple((field_down[k], field_up[k]) for k in range(3)) + (field_right[0], field_left[0])
-    v, u, au = chain(ends, factor, stiffness, intact, w_in, pieces, edge, halo, wide)
+    v, u, au = chain(ends, (factor, edge, side, corner), weighted, w_in, pieces, wide)
     for i in range(3):
         u_out[i], au_out[i] = u[i], au[i]
     g, z, w = ([ref[i] for i in range(3)] for ref in (g_in, z_in, w_in))
@@ -294,9 +320,7 @@
 
 
 def finish(sums, field, z_in, w_in, u_in, au_in, x_out, r_out):
-    row = sums[0]
-    for k in range(1, sums.shape[0]):
-        row = row + sums[k]
+    row = sums[...]
     lane = lax.broadcasted_iota(jnp.int32, (1, LANES), 1)
     s = [jnp.sum(jnp.where(lane == k, row, 0.0), axis=1, keepdims=True) for k in range(10)]
     alpha = s[0] / s[1]
@@ -317,21 +341,17 @@
     return jax.ShapeDtypeStruct(dims, jnp.float32)
 
 
-def call(body, name, outs, scratch=(), scalars=0):
-    def run(*operands):
-        specs = [pl.BlockSpec(memory_space=pltpu.SMEM)] * scalars
-        specs += [pl.BlockSpec(memory_space=pltpu.VMEM)] * (len(operands) - scalars)
-        return pl.pallas_call(
-            body,
-            out_shape=outs,
-            in_specs=specs,
-            out_specs=[pl.BlockSpec(memory_space=pltpu.VMEM)] * len(outs),
-            scratch_shapes=list(scratch),
-            compiler_params=pltpu.CompilerParams(vmem_limit_bytes=VMEM_LIMIT),
-            name=name,
-        )(*operands)
-
-    return run
+def call(body, outs, spaces, scratch=(), cost=None, limit=VMEM_LIMIT):
+    return pl.pallas_call(
+        body,
+        out_shape=outs,
+        in_specs=[pl.BlockSpec(memory_space=space) for space in spaces],
+        out_specs=[pl.BlockSpec(memory_space=pltpu.VMEM)] * len(outs),
+        scratch_shapes=list(scratch),
+        compiler_params=pltpu.CompilerParams(vmem_limit_bytes=limit),
+        cost_estimate=cost,
+        name=body.__name__,
+    )
 
 
 def swap(first, second, axis, wrap):
@@ -342,11 +362,8 @@
     return lax.ppermute(first, axis, back), lax.ppermute(second, axis, ahead)
 
 
-def total_of(row, axis, nxt):
-    got = lax.all_to_all(row, axis, 0, 0)
-    if nxt is None:
-        return got
-    return jnp.broadcast_to(jnp.sum(got, axis=0)[None], (nxt, 1, LANES))
+def gathered_sum(rows, axis):
+    return jnp.sum(lax.all_to_all(rows, axis, 0, 0), axis=0)
 
 
 def local(right_side, stiffness, factor, intact):
@@ -356,33 +373,50 @@
     plane = shape(3, ROWS, LANES)
     strip = shape(GROUPS + 1, ROWS, LANES)
     own = shape(OWN_TILES, 8, LANES)
-    corner = shape(GROUPS + 1, 8, LANES)
+    ends_of_strip = shape(GROUPS + 1, 8, LANES)
     small = shape(1, ROWS, LANES)
     edges = shape(3, 8, LANES)
-    scratch = (
-        pltpu.VMEM((PLANES, 8, LANES), jnp.float32),
-        pltpu.VMEM((PLANES, 24, LANES), jnp.float32),
-        pltpu.VMEM((3, 40, 2 * LANES), jnp.float32),
-    )
-
-    to_left, to_right, down, up = call(pack_inputs, "pack_inputs", [strip, strip, own, own])(factor, right_side)
+    tiles = shape(PLANES, 8, LANES)
+    wide = pltpu.VMEM((3, 40, 2 * LANES), jnp.float32)
+    vmem, hbm, smem = pltpu.VMEM, pltpu.HBM, pltpu.SMEM
+
+    factor, field, to_left, to_right, down, up = call(
+        pack_inputs,
+        [shape(*factor.shape), plane, strip, strip, own, own],
+        [hbm] * 2,
+        [pltpu.SemaphoreType.DMA((len(CHUNKS) + 1,))],
+        limit=WIDE_LIMIT,
+    )(factor, right_side)
     right, left = swap(to_left, to_right, "gy", False)
     own_down, own_up = swap(down, up, "gx", True)
-    down, up = call(pack_corners, "pack_corners", [corner, corner])(right, left)
+    (weighted,) = call(
+        weigh,
+        [shape(*stiffness.shape)],
+        [hbm] * 2,
+        [pltpu.VMEM(intact.shape, jnp.int32), pltpu.SemaphoreType.DMA((2,))],
+        pl.CostEstimate(flops=stiffness.size, bytes_accessed=8 * stiffness.size, transcendentals=0),
+    )(stiffness, intact)
+    down, up = call(pack_corners, [ends_of_strip] * 2, [vmem] * 2)(right, left)
+    edge, side = call(
+        unpack_sides,
+        [tiles, shape(PLANES, ROWS, LANES)],
+        [vmem] * 5,
+        cost=pl.CostEstimate(flops=4 * factor.size, bytes_accessed=8 * factor.size, transcendentals=0),
+    )(right, left, own_down, own_up, down)
     corner_down, corner_up = swap(down, up, "gx", True)
-    halos = (right, left, own_down, own_up, corner_down, corner_up)
-
-    g, z, w, to_left, to_right = call(
-        first_half, "first_half", [plane, plane, plane, small, small], scratch, 1
-    )(ends, factor, right_side, stiffness, intact, *halos)
+
+    corner, g, z, w, to_left, to_right = call(
+        first_half, [tiles, plane, plane, plane, small, small], [smem] + [vmem] * 11, [wide]
+    )(ends, factor, edge, side, weighted, field, right, left, own_down, own_up, corner_down, corner_up)
     field_right, field_left = swap(to_left, to_right, "gy", False)
-    down, up = call(pack_field, "pack_field", [edges, edges])(w, field_right, field_left)
+    down, up = call(pack_field, [edges] * 2, [vmem] * 3)(w, field_right, field_left)
     field_down, field_up = swap(down, up, "gx", True)
-    u, au, sums = call(second_half, "second_half", [plane, plane, shape(ny, 1, LANES)], scratch, 1)(
-        ends, factor, stiffness, intact, *halos, g, z, w, field_right, field_left, field_down, field_up
+    u, au, sums = call(second_half, [plane, plane, shape(ny, 1, LANES)], [smem] + [vmem] * 12, [wide])(
+        ends, factor, edge, side, weighted, corner, g, z, w, field_right, field_left, field_down, field_up
     )
-    sums = total_of(total_of(sums, "gy", nx), "gx", None)
-    x, r = call(finish, "finish", [plane, plane])(sums, right_side, z, w, u, au)
+    sums = gathered_sum(sums, "gy")
+    sums = gathered_sum(jnp.broadcast_to(sums[None], (nx, 1, LANES)), "gx")
+    x, r = call(finish, [plane] * 2, [vmem] * 6)(sums, field, z, w, u, au)
     return x, r
 
 

time: 88.2 us -> 85.9 us (0.974)
  waiting for transfers between devices: 7.58 us -> 4.13 us
  local copies, waits for them, and re-layouts: 5.42 us -> 2.47 us
  blocking collectives: 40.2 us -> 42.7 us
  Pallas kernels: 5.89 us -> 7.42 us
    ppermute x10, waiting for transfers between devices: 7.58 us -> 4.13 us  [swap(): return (lax.ppermute(first, axis, back), lax.ppermute(second, axis, ahead))]
    unnamed x16 -> x6, local copies, waits for them, and re-layouts: 5.41 us -> 2.46 us
    all_to_all x2, blocking collectives: 40.2 us -> 42.7 us  [gathered_sum(): return jnp.sum(lax.all_to_all(rows, axis, 0, 0), axis=0)]
    pallas_call x6 -> x8, Pallas kernels: 5.89 us -> 7.42 us  [the longest x1 2.14 us: local(): call(first_half, [tiles, plane, plane, plane, small, small], [smem] + [vm...]
  transfers between devices with their start and end apart: 10 -> 10, of which waited for: 7 -> 6; matrix products, arithmetic and copies ran while one was open for 0% -> 0% of each run, Pallas kernels for 0% -> 1%
where the time goes in v2:
time: 85.9 us; the launch traced here: 85.5 us
  blocking collectives  42.7 us (50%)
  starting transfers between devices  27.9 us (32%)
  Pallas kernels  7.42 us (9%)
  waiting for transfers between devices  4.13 us (5%)
  local copies, waits for them, and re-layouts  2.47 us (3%)
    all_to_all x2, blocking collectives, gathered_sum(): return jnp.sum(lax.all_to_all(rows, axis, 0, 0), axis=0)  42.7 us
    ppermute x10, starting transfers between devices, swap(): return (lax.ppermute(first, axis, back), lax.ppermute(second, axis, ahead))  27.9 us
    ppermute x10, waiting for transfers between devices, swap(): return (lax.ppermute(first, axis, back), lax.ppermute(second, axis, ahead))  4.13 us
    unnamed x6, local copies, waits for them, and re-layouts  2.46 us
    pallas_call x1, Pallas kernels, local(): call(first_half, [tiles, plane, plane, plane, small, small], [smem] + [vm...  2.14 us
    pallas_call x1, Pallas kernels, local(): call(second_half, [plane, plane, shape(ny, 1, LANES)], [smem] + [vmem] *...  2.04 us
  transfers between devices with their start and end apart: 10, of which 6 were waited for; matrix products, arithmetic and copies ran while one was open for 0% of the time, Pallas kernels for 1%

profile of v2, /device:TPU:1, one launch (start us, length us, event | category | flops | bytes accessed | tf_op | source)
XLA Modules:
  0.0 85.5 jit_solution(1902984534888188850)
XLA Ops:
  0.6 0.0 copy-start.1
  0.6 0.0 copy-start.2
  0.6 0.8 copy-done.2
  1.4 1.6 %pack_inputs.1 = (f32[17,3,3,16,128]{4,3,2,1,0:T(8,128)S(1)}, f32[3,16,128]{2,1,0:T(8,128)S(1)}, f32[21,16,128]{2,1,0:T(8,128)S(1)}, f32[21,16,128]{2,1,0:T(8,12...) custom-call(f32[17,3,3,16,128]{4,3,2,1,0:T(8,128)} %factor_hbm.1, f32[3,16,128]{2,1,0:T(8,128)S(1)} %copy-done.2), custom_call_target="tpu_custom_call" | custom-call | tf_op jit(solution)/shard_map/pack_inputs/pallas_call | solution.py:383
  3.1 6.9 %collective-permute-start.2 = (f32[79,8,128]{2,1,0:T(8,128)S(1)}, f32[79,8,128]{2,1,0:T(8,128)S(1)}, u32[]{:S(2)}, u32[]{:S(2)}) collective-permute-start(f32[79,8,128]{2,1,0:T(8,128)S(1)} %get-tuple-element.26), channel_id=1, source_target_pairs={{16,0},{32,16},{48,32},{64,48},{80,64},{96,80},{112,96},{128,112},... | collective-permute-start | bytes 970760 | tf_op jit(solution)/shard_map/ppermute | solution.py:362
  10.0 0.0 collective-permute-start.3
  10.0 1.3 %collective-permute-start = (f32[21,16,128]{2,1,0:T(8,128)S(1)}, f32[21,16,128]{2,1,0:T(8,128)S(1)}, u32[]{:S(2)}, u32[]{:S(2)}) collective-permute-start(f32[21,16,128]{2,1,0:T(8,128)S(1)} %get-tuple-element.24), channel_id=1, source_target_pairs={{1,0},{2,1},{3,2},{4,3},{5,4},{6,5},{7,6},{8,7},{9,8},{10,9},{11,1... | collective-permute-start | bytes 516104 | tf_op jit(solution)/shard_map/ppermute | solution.py:362
  11.2 4.0 %collective-permute-start.1 = (f32[21,16,128]{2,1,0:T(8,128)S(1)}, f32[21,16,128]{2,1,0:T(8,128)S(1)}, u32[]{:S(2)}, u32[]{:S(2)}) collective-permute-start(f32[21,16,128]{2,1,0:T(8,128)S(1)} %get-tuple-element.25), channel_id=1, source_target_pairs={{0,1},{1,2},{2,3},{3,4},{4,5},{5,6},{6,7},{7,8},{8,9},{9,10},{10,1... | collective-permute-start | bytes 516104 | tf_op jit(solution)/shard_map/ppermute | solution.py:362
  15.3 0.0 copy-done.1
  15.3 0.0 copy-start
  15.3 1.7 %copy-done = f32[33,3,3,16,128]{4,3,2,1,0:T(8,128)S(1)} copy-done((f32[33,3,3,16,128]{4,3,2,1,0:T(8,128)S(1)}, f32[33,3,3,16,128]{4,3,2,1,0:T(8,128)}, u32[]{:S(2)}) %copy-start) | copy-done | bytes 2433048
  17.0 0.5 weigh.1.weighted
  17.4 0.0 collective-permute-done.right
  17.4 0.1 collective-permute-done.1.left
  17.6 0.0 collective-permute-start.5
  17.6 4.7 %collective-permute-start.4 = (f32[21,8,128]{2,1,0:T(8,128)S(1)}, f32[21,8,128]{2,1,0:T(8,128)S(1)}, u32[]{:S(2)}, u32[]{:S(2)}) collective-permute-start(f32[21,8,128]{2,1,0:T(8,128)S(1)} %get-tuple-element.28.corner_down), channel_id=1, source_target_pairs={{16,0},{32,16},{48,32},{64,48},{80,64},{96,80},{112,96},{128,112},... | collective-permute-start | bytes 258056 | tf_op jit(solution)/shard_map/ppermute | solution.py:362
  22.3 0.1 add_convert_fusion.ends
  22.4 0.0 collective-permute-done.2.own_down
  22.4 0.0 collective-permute-done.3.own_up
  22.4 0.4 unpack_sides.1
  22.8 0.3 collective-permute-done.5.corner_up
  23.1 0.2 collective-permute-done.4.corner_down
  23.3 2.1 %first_half.1 = (f32[153,8,128]{2,1,0:T(8,128)S(1)}, f32[3,16,128]{2,1,0:T(8,128)S(1)}, f32[3,16,128]{2,1,0:T(8,128)S(1)}, f32[3,16,128]{2,1,0:T(8,128)S(1)}, f3...) custom-call(s32[4]{0:T(128)S(1)} %add_convert_fusion.ends, f32[17,3,3,16,128]{4,3,2,1,0:T(8,128)S(1)} %get-tuple-element.23.factor, ...), custom_call_target="tpu_custom_call" | custom-call | tf_op jit(solution)/shard_map/first_half/pallas_call | solution.py:408
  25.4 1.3 %collective-permute-start.6 = (f32[1,16,128]{2,1,0:T(8,128)S(1)}, f32[1,16,128]{2,1,0:T(8,128)S(1)}, u32[]{:S(2)}, u32[]{:S(2)}) collective-permute-start(f32[1,16,128]{2,1,0:T(8,128)S(1)} %get-tuple-element.37), channel_id=1, source_target_pairs={{1,0},{2,1},{3,2},{4,3},{5,4},{6,5},{7,6},{8,7},{9,8},{10,9},{11,1... | collective-permute-start | bytes 24584 | tf_op jit(solution)/shard_map/ppermute | solution.py:362
  26.7 4.7 %collective-permute-start.7 = (f32[1,16,128]{2,1,0:T(8,128)S(1)}, f32[1,16,128]{2,1,0:T(8,128)S(1)}, u32[]{:S(2)}, u32[]{:S(2)}) collective-permute-start(f32[1,16,128]{2,1,0:T(8,128)S(1)} %get-tuple-element.38), channel_id=1, source_target_pairs={{0,1},{1,2},{2,3},{3,4},{4,5},{5,6},{6,7},{7,8},{8,9},{9,10},{10,1... | collective-permute-start | bytes 24584 | tf_op jit(solution)/shard_map/ppermute | solution.py:362
  31.4 0.0 collective-permute-done.6.right.field_right
  31.4 0.8 collective-permute-done.7.left.field_left
  32.2 5.0 %collective-permute-start.8 = (f32[3,8,128]{2,1,0:T(8,128)S(1)}, f32[3,8,128]{2,1,0:T(8,128)S(1)}, u32[]{:S(2)}, u32[]{:S(2)}) collective-permute-start(f32[3,8,128]{2,1,0:T(8,128)S(1)} %get-tuple-element.39), channel_id=1, source_target_pairs={{16,0},{32,16},{48,32},{64,48},{80,64},{96,80},{112,96},{128,112},... | collective-permute-start | bytes 36872 | tf_op jit(solution)/shard_map/ppermute | solution.py:362
  37.2 0.0 collective-permute-start.9
  37.2 0.8 collective-permute-done.8.field_down
  38.1 1.9 %collective-permute-done.9.field_up = f32[3,8,128]{2,1,0:T(8,128)S(1)} collective-permute-done((f32[3,8,128]{2,1,0:T(8,128)S(1)}, f32[3,8,128]{2,1,0:T(8,128)S(1)}, u32[]{:S(2)}, u32[]{:S(2)}) %collective-permute-start.9) | collective-permute-done | bytes 12320 | tf_op jit(solution)/shard_map/ppermute | solution.py:362
  40.0 2.0 %second_half.1 = (f32[3,16,128]{2,1,0:T(8,128)S(1)}, f32[3,16,128]{2,1,0:T(8,128)S(1)}, f32[16,1,128]{2,1,0:T(1,128)S(1)}) custom-call(s32[4]{0:T(128)S(1)} %add_convert_fusion.ends, f32[17,3,3,16,128]{4,3,2,1,0:T(8,128)S(1)} %get-tuple-element.23.factor, f32[153,8,128]{2,1,0:T(8,128)S(1)} %get-tuple-element.29.edge, ...), custom_call_target="tpu_custom_call" | custom-call | tf_op jit(solution)/shard_map/second_half/pallas_call | solution.py:414
  42.1 17.5 %all_to_all.10 = f32[16,1,128]{2,1,0:T(1,128)S(1)} all-to-all(f32[16,1,128]{2,1,0:T(1,128)S(1)} %get-tuple-element.41), channel_id=1, replica_groups=mesh['gx'=32,'gy'=16] {'gy'}, dimensions={0} | all-to-all | bytes 16384 | tf_op jit(solution)/shard_map/all_to_all | solution.py:366
  59.6 25.2 %all_to_all.11 = f32[32,1,128]{2,1,0:T(1,128)S(1)} all-to-all(f32[32,1,128]{2,1,0:T(1,128)S(1)} %broadcast_in_dim.2), channel_id=1, replica_groups=mesh['gx'=32,'gy'=16] {'gx'}, dimensions={0} | all-to-all | bytes 32768 | tf_op jit(solution)/shard_map/all_to_all | solution.py:366
  84.8 0.7 finish.1
  (5 shorter events, 0.1 us)
Async XLA Ops:
  0.6 14.6 %copy-start.1 = (s32[32,16,128]{2,1,0:T(8,128)S(1)}, s32[32,16,128]{2,1,0:T(8,128)}, u32[]{:S(2)}) copy-start(s32[32,16,128]{2,1,0:T(8,128)} %intact_hbm.1) | copy-start | bytes 786436
  0.6 0.8 copy-start.2
  3.1 19.4 %collective-permute-start.2 = (f32[79,8,128]{2,1,0:T(8,128)S(1)}, f32[79,8,128]{2,1,0:T(8,128)S(1)}, u32[]{:S(2)}, u32[]{:S(2)}) collective-permute-start(f32[79,8,128]{2,1,0:T(8,128)S(1)} %get-tuple-element.26), channel_id=1, source_target_pairs={{16,0},{32,16},{48,32},{64,48},{80,64},{96,80},{112,96},{128,112},... | collective-permute-start | bytes 970760 | tf_op jit(solution)/shard_map/ppermute | solution.py:362
  10.0 12.5 %collective-permute-start.3 = (f32[79,8,128]{2,1,0:T(8,128)S(1)}, f32[79,8,128]{2,1,0:T(8,128)S(1)}, u32[]{:S(2)}, u32[]{:S(2)}) collective-permute-start(f32[79,8,128]{2,1,0:T(8,128)S(1)} %get-tuple-element.27), channel_id=1, source_target_pairs={{0,16},{16,32},{32,48},{48,64},{64,80},{80,96},{96,112},{112,128},... | collective-permute-start | bytes 970760 | tf_op jit(solution)/shard_map/ppermute | solution.py:362
  10.0 7.5 %collective-permute-start = (f32[21,16,128]{2,1,0:T(8,128)S(1)}, f32[21,16,128]{2,1,0:T(8,128)S(1)}, u32[]{:S(2)}, u32[]{:S(2)}) collective-permute-start(f32[21,16,128]{2,1,0:T(8,128)S(1)} %get-tuple-element.24), channel_id=1, source_target_pairs={{1,0},{2,1},{3,2},{4,3},{5,4},{6,5},{7,6},{8,7},{9,8},{10,9},{11,1... | collective-permute-start | bytes 516104 | tf_op jit(solution)/shard_map/ppermute | solution.py:362
  11.2 6.3 %collective-permute-start.1 = (f32[21,16,128]{2,1,0:T(8,128)S(1)}, f32[21,16,128]{2,1,0:T(8,128)S(1)}, u32[]{:S(2)}, u32[]{:S(2)}) collective-permute-start(f32[21,16,128]{2,1,0:T(8,128)S(1)} %get-tuple-element.25), channel_id=1, source_target_pairs={{0,1},{1,2},{2,3},{3,4},{4,5},{5,6},{6,7},{7,8},{8,9},{9,10},{10,1... | collective-permute-start | bytes 516104 | tf_op jit(solution)/shard_map/ppermute | solution.py:362
  15.3 1.7 %copy-start = (f32[33,3,3,16,128]{4,3,2,1,0:T(8,128)S(1)}, f32[33,3,3,16,128]{4,3,2,1,0:T(8,128)}, u32[]{:S(2)}) copy-start(f32[33,3,3,16,128]{4,3,2,1,0:T(8,128)} %stiffness_hbm.1) | copy-start | bytes 7299076
  17.6 5.5 %collective-permute-start.5 = (f32[21,8,128]{2,1,0:T(8,128)S(1)}, f32[21,8,128]{2,1,0:T(8,128)S(1)}, u32[]{:S(2)}, u32[]{:S(2)}) collective-permute-start(f32[21,8,128]{2,1,0:T(8,128)S(1)} %get-tuple-element.32), channel_id=1, source_target_pairs={{0,16},{16,32},{32,48},{48,64},{64,80},{80,96},{96,112},{112,128},... | collective-permute-start | bytes 258056 | tf_op jit(solution)/shard_map/ppermute | solution.py:362
  17.6 5.6 %collective-permute-start.4 = (f32[21,8,128]{2,1,0:T(8,128)S(1)}, f32[21,8,128]{2,1,0:T(8,128)S(1)}, u32[]{:S(2)}, u32[]{:S(2)}) collective-permute-start(f32[21,8,128]{2,1,0:T(8,128)S(1)} %get-tuple-element.28.corner_down), channel_id=1, source_target_pairs={{16,0},{32,16},{48,32},{64,48},{80,64},{96,80},{112,96},{128,112},... | collective-permute-start | bytes 258056 | tf_op jit(solution)/shard_map/ppermute | solution.py:362
  25.4 6.0 %collective-permute-start.6 = (f32[1,16,128]{2,1,0:T(8,128)S(1)}, f32[1,16,128]{2,1,0:T(8,128)S(1)}, u32[]{:S(2)}, u32[]{:S(2)}) collective-permute-start(f32[1,16,128]{2,1,0:T(8,128)S(1)} %get-tuple-element.37), channel_id=1, source_target_pairs={{1,0},{2,1},{3,2},{4,3},{5,4},{6,5},{7,6},{8,7},{9,8},{10,9},{11,1... | collective-permute-start | bytes 24584 | tf_op jit(solution)/shard_map/ppermute | solution.py:362
  26.7 5.5 %collective-permute-start.7 = (f32[1,16,128]{2,1,0:T(8,128)S(1)}, f32[1,16,128]{2,1,0:T(8,128)S(1)}, u32[]{:S(2)}, u32[]{:S(2)}) collective-permute-start(f32[1,16,128]{2,1,0:T(8,128)S(1)} %get-tuple-element.38), channel_id=1, source_target_pairs={{0,1},{1,2},{2,3},{3,4},{4,5},{5,6},{6,7},{7,8},{8,9},{9,10},{10,1... | collective-permute-start | bytes 24584 | tf_op jit(solution)/shard_map/ppermute | solution.py:362
  32.2 5.9 %collective-permute-start.8 = (f32[3,8,128]{2,1,0:T(8,128)S(1)}, f32[3,8,128]{2,1,0:T(8,128)S(1)}, u32[]{:S(2)}, u32[]{:S(2)}) collective-permute-start(f32[3,8,128]{2,1,0:T(8,128)S(1)} %get-tuple-element.39), channel_id=1, source_target_pairs={{16,0},{32,16},{48,32},{64,48},{80,64},{96,80},{112,96},{128,112},... | collective-permute-start | bytes 36872 | tf_op jit(solution)/shard_map/ppermute | solution.py:362
  37.2 2.8 %collective-permute-start.9 = (f32[3,8,128]{2,1,0:T(8,128)S(1)}, f32[3,8,128]{2,1,0:T(8,128)S(1)}, u32[]{:S(2)}, u32[]{:S(2)}) collective-permute-start(f32[3,8,128]{2,1,0:T(8,128)S(1)} %get-tuple-element.40), channel_id=1, source_target_pairs={{0,16},{16,32},{32,48},{48,64},{64,80},{80,96},{96,112},{112,128},... | collective-permute-start | bytes 36872 | tf_op jit(solution)/shard_map/ppermute | solution.py:362

commit v3 on v2

--- a/solution.py
+++ b/solution.py
@@ -14,7 +14,7 @@
 OWN_TILES = (PLANES + 1) // 2 + 2
 CENTRE = 0.8
 VMEM_LIMIT = 24 * 1024 * 1024
-WIDE_LIMIT = 53477376
+WIDE_LIMIT = 51 * 1024 * 1024
 
 
 def bond_offsets():
@@ -73,20 +73,16 @@
 CHUNKS = ((0, 5), (5, 9), (9, 13), (13, LOWER))
 
 
-def pack_inputs(factor_hbm, field_hbm, factor, field, to_left, to_right, down, up, sems):
-    copies = [pltpu.make_async_copy(field_hbm, field, sems.at[len(CHUNKS)])]
+def pack_factor(factor_hbm, factor, to_left, to_right, down, up, sems):
+    copies = []
     for k, (low, high) in enumerate(CHUNKS):
         part = pl.ds(low, high - low)
         copies.append(pltpu.make_async_copy(factor_hbm.at[part], factor.at[part], sems.at[k]))
     for copy in copies:
         copy.start()
-    copies[0].wait()
-    to_left[GROUPS], to_right[GROUPS] = pack_lanes([field[k] for k in range(3)], 32)
-    down[OWN_TILES - 2], up[OWN_TILES - 2] = pack_rows(field[0], field[1])
-    down[OWN_TILES - 1], up[OWN_TILES - 1] = pack_rows(field[2], field[2])
     group = tile = 0
     for k, (low, high) in enumerate(CHUNKS):
-        copies[1 + k].wait()
+        copies[k].wait()
         ready = 9 * high
         while group < GROUPS and min(8 * group + 8, PLANES) <= ready:
             planes = [factor[entry(p)] for p in range(8 * group, min(8 * group + 8, PLANES))]
@@ -95,6 +91,13 @@
         while tile < OWN_TILES - 2 and min(2 * tile + 2, PLANES) <= ready:
             down[tile], up[tile] = pack_rows(factor[entry(2 * tile)], factor[entry(min(2 * tile + 1, PLANES - 1))])
             tile += 1
+
+
+def pack_right_side(field, left_in, right_in, down_in, up_in, kept, to_left, to_right, down, up):
+    kept[...] = field[...]
+    to_left[GROUPS], to_right[GROUPS] = pack_lanes([field[k] for k in range(3)], 32)
+    down[OWN_TILES - 2], up[OWN_TILES - 2] = pack_rows(field[0], field[1])
+    down[OWN_TILES - 1], up[OWN_TILES - 1] = pack_rows(field[2], field[2])
 
 
 def weigh(stiffness_hbm, intact_hbm, weighted, intact, sems):
@@ -156,9 +159,8 @@
     if by == 0:
         return near
     lane = iota(near.shape[0], 1)
-    amount = (-by) % LANES
-    inside = lane < LANES - by if by > 0 else lane >= -by
-    return jnp.where(inside, pltpu.roll(near, amount, 1), pltpu.roll(far, amount, 1))
+    kept = lane >= by if by > 0 else lane < LANES + by
+    return pltpu.roll(jnp.where(kept, near, far), (-by) % LANES, 1)
 
 
 def layer_ok(rows, dz):
@@ -246,7 +248,11 @@
     return total
 
 
-def outside(ends):
+def outside():
+    ends = []
+    for axis in ("gx", "gy"):
+        place = lax.axis_index(axis)
+        ends += [(place == 0).astype(jnp.int32), (place == lax.axis_size(axis) - 1).astype(jnp.int32)]
     sub = iota(8, 0)
     edge_out = ((sub < 4) & (ends[1] == 1)) | ((sub >= 4) & (ends[0] == 1))
     lane = iota(24, 1)
@@ -254,8 +260,8 @@
     return edge_out, side_out
 
 
-def chain(ends, blocks, weighted, field, pieces, wide):
-    edge_out, side_out = outside(ends)
+def chain(blocks, weighted, field, pieces, wide):
+    edge_out, side_out = outside()
     (down_a, up_a), (down_b, up_b), (down_c, up_c), right, left = pieces
     edges = [*unpack_rows(down_a, up_a), unpack_rows(down_b, up_b)[0]]
     edge_right, edge_left = unpack_rows(down_c, up_c)
@@ -275,7 +281,7 @@
 
 
 def first_half(
-    ends, factor, edge, side, weighted, field, right, left, own_down, own_up, corner_down, corner_up,
+    factor, edge, side, weighted, field, right, left, own_down, own_up, corner_down, corner_up,
     corner, g_out, z_out, w_out, to_left, to_right, wide,
 ):
     unpack_corners(corner_down, corner_up, corner)
@@ -283,7 +289,7 @@
     pieces = (
         (own_down[a], own_up[a]), (own_down[b], own_up[b]), (corner_down[c], corner_up[c]), right[c], left[c],
     )
-    image, zvec, product = chain(ends, (factor, edge, side, corner), weighted, field, pieces, wide)
+    image, zvec, product = chain((factor, edge, side, corner), weighted, field, pieces, wide)
     for i in range(3):
         g_out[i], z_out[i], w_out[i] = image[i], zvec[i], product[i]
     to_left[0], to_right[0] = pack_lanes(product, 32)
@@ -295,11 +301,11 @@
 
 
 def second_half(
-    ends, factor, edge, side, weighted, corner, g_in, z_in, w_in, field_right, field_left, field_down, field_up,
+    factor, edge, side, weighted, corner, g_in, z_in, w_in, field_right, field_left, field_down, field_up,
     u_out, au_out, sums, wide,
 ):
     pieces = tuple((field_down[k], field_up[k]) for k in range(3)) + (field_right[0], field_left[0])
-    v, u, au = chain(ends, (factor, edge, side, corner), weighted, w_in, pieces, wide)
+    v, u, au = chain((factor, edge, side, corner), weighted, w_in, pieces, wide)
     for i in range(3):
         u_out[i], au_out[i] = u[i], au[i]
     g, z, w = ([ref[i] for i in range(3)] for ref in (g_in, z_in, w_in))
@@ -341,7 +347,7 @@
     return jax.ShapeDtypeStruct(dims, jnp.float32)
 
 
-def call(body, outs, spaces, scratch=(), cost=None, limit=VMEM_LIMIT):
+def call(body, outs, spaces, scratch=(), cost=None, limit=VMEM_LIMIT, aliases=None):
     return pl.pallas_call(
         body,
         out_shape=outs,
@@ -350,6 +356,7 @@
         scratch_shapes=list(scratch),
         compiler_params=pltpu.CompilerParams(vmem_limit_bytes=limit),
         cost_estimate=cost,
+        input_output_aliases=aliases or {},
         name=body.__name__,
     )
 
@@ -367,9 +374,7 @@
 
 
 def local(right_side, stiffness, factor, intact):
-    gx, gy = lax.axis_index("gx"), lax.axis_index("gy")
     nx, ny = lax.axis_size("gx"), lax.axis_size("gy")
-    ends = jnp.stack([gx == 0, gx == nx - 1, gy == 0, gy == ny - 1]).astype(jnp.int32)
     plane = shape(3, ROWS, LANES)
     strip = shape(GROUPS + 1, ROWS, LANES)
     own = shape(OWN_TILES, 8, LANES)
@@ -378,15 +383,18 @@
     edges = shape(3, 8, LANES)
     tiles = shape(PLANES, 8, LANES)
     wide = pltpu.VMEM((3, 40, 2 * LANES), jnp.float32)
-    vmem, hbm, smem = pltpu.VMEM, pltpu.HBM, pltpu.SMEM
-
-    factor, field, to_left, to_right, down, up = call(
-        pack_inputs,
-        [shape(*factor.shape), plane, strip, strip, own, own],
-        [hbm] * 2,
-        [pltpu.SemaphoreType.DMA((len(CHUNKS) + 1,))],
+    vmem, hbm = pltpu.VMEM, pltpu.HBM
+
+    factor, *packs = call(
+        pack_factor,
+        [shape(*factor.shape), strip, strip, own, own],
+        [hbm],
+        [pltpu.SemaphoreType.DMA((len(CHUNKS),))],
         limit=WIDE_LIMIT,
-    )(factor, right_side)
+    )(factor)
+    field, to_left, to_right, down, up = call(
+        pack_right_side, [plane, strip, strip, own, own], [vmem] * 5, aliases={k: k for k in range(1, 5)}
+    )(right_side, *packs)
     right, left = swap(to_left, to_right, "gy", False)
     own_down, own_up = swap(down, up, "gx", True)
     (weighted,) = call(
@@ -395,6 +403,7 @@
         [hbm] * 2,
         [pltpu.VMEM(intact.shape, jnp.int32), pltpu.SemaphoreType.DMA((2,))],
         pl.CostEstimate(flops=stiffness.size, bytes_accessed=8 * stiffness.size, transcendentals=0),
+        WIDE_LIMIT,
     )(stiffness, intact)
     down, up = call(pack_corners, [ends_of_strip] * 2, [vmem] * 2)(right, left)
     edge, side = call(
@@ -406,13 +415,13 @@
     corner_down, corner_up = swap(down, up, "gx", True)
 
     corner, g, z, w, to_left, to_right = call(
-        first_half, [tiles, plane, plane, plane, small, small], [smem] + [vmem] * 11, [wide]
-    )(ends, factor, edge, side, weighted, field, right, left, own_down, own_up, corner_down, corner_up)
+        first_half, [tiles, plane, plane, plane, small, small], [vmem] * 11, [wide]
+    )(factor, edge, side, weighted, field, right, left, own_down, own_up, corner_down, corner_up)
     field_right, field_left = swap(to_left, to_right, "gy", False)
     down, up = call(pack_field, [edges] * 2, [vmem] * 3)(w, field_right, field_left)
     field_down, field_up = swap(down, up, "gx", True)
-    u, au, sums = call(second_half, [plane, plane, shape(ny, 1, LANES)], [smem] + [vmem] * 12, [wide])(
-        ends, factor, edge, side, weighted, corner, g, z, w, field_right, field_left, field_down, field_up
+    u, au, sums = call(second_half, [plane, plane, shape(ny, 1, LANES)], [vmem] * 12, [wide])(
+        factor, edge, side, weighted, corner, g, z, w, field_right, field_left, field_down, field_up
     )
     sums = gathered_sum(sums, "gy")
     sums = gathered_sum(jnp.broadcast_to(sums[None], (nx, 1, LANES)), "gx")

time: 85.9 us -> 83.8 us (0.976)
  local copies, waits for them, and re-layouts: 2.47 us -> 0.02 us
  waiting for transfers between devices: 4.13 us -> 5.71 us
  starting transfers between devices: 27.9 us -> 26.7 us
    unnamed x6 -> x4, local copies, waits for them, and re-layouts: 2.46 us -> 0.01 us
    ppermute x10, waiting for transfers between devices: 4.13 us -> 5.71 us  [swap(): return (lax.ppermute(first, axis, back), lax.ppermute(second, axis, ahead))]
    pallas_call x1, Pallas kernels: 0.46 us -> 1.88 us  [local(): call(weigh, [shape(*stiffness.shape)], [hbm] * 2, [pltpu.VMEM(intact.shap...]
    pallas_call x3 -> x4, Pallas kernels: 5.81 us -> 4.51 us  [the longest x1 1.66 us: local(): call(pack_factor, [shape(*factor.shape), strip, strip, own, own], [hbm],...]
    ppermute x10, starting transfers between devices: 27.9 us -> 26.7 us  [swap(): return (lax.ppermute(first, axis, back), lax.ppermute(second, axis, ahead))]
  transfers between devices with their start and end apart: 10 -> 10, of which waited for: 6 -> 5; matrix products, arithmetic and copies ran while one was open for 0% -> 0% of each run, Pallas kernels for 1% -> 3%
where the time goes in v3:
time: 83.8 us; the launch traced here: 83.5 us
  blocking collectives  42.7 us (51%)
  starting transfers between devices  26.7 us (32%)
  Pallas kernels  7.54 us (9%)
  waiting for transfers between devices  5.71 us (7%)
    all_to_all x2, blocking collectives, gathered_sum(): return jnp.sum(lax.all_to_all(rows, axis, 0, 0), axis=0)  42.7 us
    ppermute x10, starting transfers between devices, swap(): return (lax.ppermute(first, axis, back), lax.ppermute(second, axis, ahead))  26.7 us
    ppermute x10, waiting for transfers between devices, swap(): return (lax.ppermute(first, axis, back), lax.ppermute(second, axis, ahead))  5.71 us
    pallas_call x1, Pallas kernels, local(): call(weigh, [shape(*stiffness.shape)], [hbm] * 2, [pltpu.VMEM(intact.shap...  1.88 us
  transfers between devices with their start and end apart: 10, of which 5 were waited for; matrix products, arithmetic and copies ran while one was open for 0% of the time, Pallas kernels for 3%

profile of v3, /device:TPU:1, one launch (start us, length us, event | category | flops | bytes accessed | tf_op | source)
XLA Modules:
  0.0 83.5 jit_solution(7977634756711251749)
XLA Ops:
  0.6 0.0 copy-start.1
  0.6 0.0 copy-start
  0.6 1.7 %pack_factor.1 = (f32[17,3,3,16,128]{4,3,2,1,0:T(8,128)S(1)}, f32[21,16,128]{2,1,0:T(8,128)S(1)}, f32[21,16,128]{2,1,0:T(8,128)S(1)}, f32[79,8,128]{2,1,0:T(8,128)S(1)}, f32[79,8,128]{2,1,0:T(8,128)S(1)}) custom-call(f32[17,3,3,16,128]{4,3,2,1,0:T(8,128)} %factor_hbm.1), custom_call_target="tpu_custom_call" | custom-call | tf_op jit(solution)/shard_map/pack_factor/pallas_call | solution.py:388
  2.3 0.0 copy-done.1
  2.3 0.1 pack_right_side.1
  2.4 6.9 %collective-permute-start.2 = (f32[79,8,128]{2,1,0:T(8,128)S(1)}, f32[79,8,128]{2,1,0:T(8,128)S(1)}, u32[]{:S(2)}, u32[]{:S(2)}) collective-permute-start(f32[79,8,128]{2,1,0:T(8,128)S(1)} %get-tuple-element.34), channel_id=1, source_target_pairs={{16,0},{32,16},{48,32},{64,48},{80,64},{96,80},{112,96},{128,112},... | collective-permute-start | bytes 970760 | tf_op jit(solution)/shard_map/ppermute | solution.py:369
  9.3 0.0 collective-permute-start.3
  9.3 1.3 %collective-permute-start = (f32[21,16,128]{2,1,0:T(8,128)S(1)}, f32[21,16,128]{2,1,0:T(8,128)S(1)}, u32[]{:S(2)}, u32[]{:S(2)}) collective-permute-start(f32[21,16,128]{2,1,0:T(8,128)S(1)} %get-tuple-element.32), channel_id=1, source_target_pairs={{1,0},{2,1},{3,2},{4,3},{5,4},{6,5},{7,6},{8,7},{9,8},{10,9},{11,1... | collective-permute-start | bytes 516104 | tf_op jit(solution)/shard_map/ppermute | solution.py:369
  10.6 4.0 %collective-permute-start.1 = (f32[21,16,128]{2,1,0:T(8,128)S(1)}, f32[21,16,128]{2,1,0:T(8,128)S(1)}, u32[]{:S(2)}, u32[]{:S(2)}) collective-permute-start(f32[21,16,128]{2,1,0:T(8,128)S(1)} %get-tuple-element.33), channel_id=1, source_target_pairs={{0,1},{1,2},{2,3},{3,4},{4,5},{5,6},{6,7},{7,8},{8,9},{9,10},{10,1... | collective-permute-start | bytes 516104 | tf_op jit(solution)/shard_map/ppermute | solution.py:369
  14.6 0.8 %collective-permute-done.right = f32[21,16,128]{2,1,0:T(8,128)S(1)} collective-permute-done((f32[21,16,128]{2,1,0:T(8,128)S(1)}, f32[21,16,128]{2,1,0:T(8,128)S(1)}, u32[]{:S(2)}, u32[]{:S(2)}) %collective-permute-start) | collective-permute-done | bytes 172064 | tf_op jit(solution)/shard_map/ppermute | solution.py:369
  15.4 1.5 %collective-permute-done.1.left = f32[21,16,128]{2,1,0:T(8,128)S(1)} collective-permute-done((f32[21,16,128]{2,1,0:T(8,128)S(1)}, f32[21,16,128]{2,1,0:T(8,128)S(1)}, u32[]{:S(2)}, u32[]{:S(2)}) %collective-permute-start.1) | collective-permute-done | bytes 172064 | tf_op jit(solution)/shard_map/ppermute | solution.py:369
  16.9 0.0 collective-permute-start.5
  17.0 4.7 %collective-permute-start.4 = (f32[21,8,128]{2,1,0:T(8,128)S(1)}, f32[21,8,128]{2,1,0:T(8,128)S(1)}, u32[]{:S(2)}, u32[]{:S(2)}) collective-permute-start(f32[21,8,128]{2,1,0:T(8,128)S(1)} %get-tuple-element.36.corner_down), channel_id=1, source_target_pairs={{16,0},{32,16},{48,32},{64,48},{80,64},{96,80},{112,96},{128,112},... | collective-permute-start | bytes 258056 | tf_op jit(solution)/shard_map/ppermute | solution.py:369
  21.7 0.0 copy-done
  21.7 1.9 %weigh.1.weighted = f32[33,3,3,16,128]{4,3,2,1,0:T(8,128)S(1)} custom-call(f32[33,3,3,16,128]{4,3,2,1,0:T(8,128)} %stiffness_hbm.1, s32[32,16,128]{2,1,0:T(8,128)S(1)} %copy-done), custom_call_target="tpu_custom_call" | custom-call | flops 608256 | bytes 4866048 | tf_op jit(solution)/shard_map/weigh/pallas_call | solution.py:400
  23.6 0.0 collective-permute-done.2.own_down
  23.6 0.0 collective-permute-done.3.own_up
  23.6 0.4 unpack_sides.1
  24.0 0.0 collective-permute-done.5.corner_up
  24.0 0.0 collective-permute-done.4.corner_down
  24.0 1.5 %first_half.1 = (f32[153,8,128]{2,1,0:T(8,128)S(1)}, f32[3,16,128]{2,1,0:T(8,128)S(1)}, f32[3,16,128]{2,1,0:T(8,128)S(1)}, f32[3,16,128]{2,1,0:T(8,128)S(1)}, f3...) custom-call(f32[17,3,3,16,128]{4,3,2,1,0:T(8,128)S(1)} %get-tuple-element.27.factor, ...), custom_call_target="tpu_custom_call" | custom-call | tf_op jit(solution)/shard_map/first_half/pallas_call | solution.py:417
  25.4 1.3 %collective-permute-start.6 = (f32[1,16,128]{2,1,0:T(8,128)S(1)}, f32[1,16,128]{2,1,0:T(8,128)S(1)}, u32[]{:S(2)}, u32[]{:S(2)}) collective-permute-start(f32[1,16,128]{2,1,0:T(8,128)S(1)} %get-tuple-element.45), channel_id=1, source_target_pairs={{1,0},{2,1},{3,2},{4,3},{5,4},{6,5},{7,6},{8,7},{9,8},{10,9},{11,1... | collective-permute-start | bytes 24584 | tf_op jit(solution)/shard_map/ppermute | solution.py:369
  26.7 4.7 %collective-permute-start.7 = (f32[1,16,128]{2,1,0:T(8,128)S(1)}, f32[1,16,128]{2,1,0:T(8,128)S(1)}, u32[]{:S(2)}, u32[]{:S(2)}) collective-permute-start(f32[1,16,128]{2,1,0:T(8,128)S(1)} %get-tuple-element.46), channel_id=1, source_target_pairs={{0,1},{1,2},{2,3},{3,4},{4,5},{5,6},{6,7},{7,8},{8,9},{9,10},{10,1... | collective-permute-start | bytes 24584 | tf_op jit(solution)/shard_map/ppermute | solution.py:369
  31.5 0.0 collective-permute-done.6.right.field_right
  31.5 0.8 collective-permute-done.7.left.field_left
  32.3 3.8 %collective-permute-start.8 = (f32[3,8,128]{2,1,0:T(8,128)S(1)}, f32[3,8,128]{2,1,0:T(8,128)S(1)}, u32[]{:S(2)}, u32[]{:S(2)}) collective-permute-start(f32[3,8,128]{2,1,0:T(8,128)S(1)} %get-tuple-element.47), channel_id=1, source_target_pairs={{16,0},{32,16},{48,32},{64,48},{80,64},{96,80},{112,96},{128,112},... | collective-permute-start | bytes 36872 | tf_op jit(solution)/shard_map/ppermute | solution.py:369
  36.0 0.0 collective-permute-start.9
  36.0 0.8 collective-permute-done.8.field_down
  36.9 1.8 %collective-permute-done.9.field_up = f32[3,8,128]{2,1,0:T(8,128)S(1)} collective-permute-done((f32[3,8,128]{2,1,0:T(8,128)S(1)}, f32[3,8,128]{2,1,0:T(8,128)S(1)}, u32[]{:S(2)}, u32[]{:S(2)}) %collective-permute-start.9) | collective-permute-done | bytes 12320 | tf_op jit(solution)/shard_map/ppermute | solution.py:369
  38.7 1.3 %second_half.1 = (f32[3,16,128]{2,1,0:T(8,128)S(1)}, f32[3,16,128]{2,1,0:T(8,128)S(1)}, f32[16,1,128]{2,1,0:T(1,128)S(1)}) custom-call(f32[17,3,3,16,128]{4,3,2,1,0:T(8,128)S(1)} %get-tuple-element.27.factor, f32[153,8,128]{2,1,0:T(8,128)S(1)} %get-tuple-element.37.edge, f32[153,16,128]{2,1,0:T(8,128)S(1)} %get-tuple-element.38.side, ...), custom_call_target="tpu_custom_call" | custom-call | tf_op jit(solution)/shard_map/second_half/pallas_call | solution.py:423
  40.0 17.5 %all_to_all.10 = f32[16,1,128]{2,1,0:T(1,128)S(1)} all-to-all(f32[16,1,128]{2,1,0:T(1,128)S(1)} %get-tuple-element.49), channel_id=1, replica_groups=mesh['gx'=32,'gy'=16] {'gy'}, dimensions={0} | all-to-all | bytes 16384 | tf_op jit(solution)/shard_map/all_to_all | solution.py:373
  57.5 25.2 %all_to_all.11 = f32[32,1,128]{2,1,0:T(1,128)S(1)} all-to-all(f32[32,1,128]{2,1,0:T(1,128)S(1)} %broadcast_in_dim.2), channel_id=1, replica_groups=mesh['gx'=32,'gy'=16] {'gx'}, dimensions={0} | all-to-all | bytes 32768 | tf_op jit(solution)/shard_map/all_to_all | solution.py:373
  82.7 0.7 finish.1
  (5 shorter events, 0.1 us)
Async XLA Ops:
  0.6 1.7 %copy-start.1 = (f32[3,16,128]{2,1,0:T(8,128)S(1)}, f32[3,16,128]{2,1,0:T(8,128)}, u32[]{:S(2)}) copy-start(f32[3,16,128]{2,1,0:T(8,128)} %field.1) | copy-start | bytes 73732
  0.6 21.0 %copy-start = (s32[32,16,128]{2,1,0:T(8,128)S(1)}, s32[32,16,128]{2,1,0:T(8,128)}, u32[]{:S(2)}) copy-start(s32[32,16,128]{2,1,0:T(8,128)} %intact_hbm.1) | copy-start | bytes 786436
  2.4 21.2 %collective-permute-start.2 = (f32[79,8,128]{2,1,0:T(8,128)S(1)}, f32[79,8,128]{2,1,0:T(8,128)S(1)}, u32[]{:S(2)}, u32[]{:S(2)}) collective-permute-start(f32[79,8,128]{2,1,0:T(8,128)S(1)} %get-tuple-element.34), channel_id=1, source_target_pairs={{16,0},{32,16},{48,32},{64,48},{80,64},{96,80},{112,96},{128,112},... | collective-permute-start | bytes 970760 | tf_op jit(solution)/shard_map/ppermute | solution.py:369
  9.3 14.3 %collective-permute-start.3 = (f32[79,8,128]{2,1,0:T(8,128)S(1)}, f32[79,8,128]{2,1,0:T(8,128)S(1)}, u32[]{:S(2)}, u32[]{:S(2)}) collective-permute-start(f32[79,8,128]{2,1,0:T(8,128)S(1)} %get-tuple-element.35), channel_id=1, source_target_pairs={{0,16},{16,32},{32,48},{48,64},{64,80},{80,96},{96,112},{112,128},... | collective-permute-start | bytes 970760 | tf_op jit(solution)/shard_map/ppermute | solution.py:369
  9.3 6.1 %collective-permute-start = (f32[21,16,128]{2,1,0:T(8,128)S(1)}, f32[21,16,128]{2,1,0:T(8,128)S(1)}, u32[]{:S(2)}, u32[]{:S(2)}) collective-permute-start(f32[21,16,128]{2,1,0:T(8,128)S(1)} %get-tuple-element.32), channel_id=1, source_target_pairs={{1,0},{2,1},{3,2},{4,3},{5,4},{6,5},{7,6},{8,7},{9,8},{10,9},{11,1... | collective-permute-start | bytes 516104 | tf_op jit(solution)/shard_map/ppermute | solution.py:369
  10.6 6.3 %collective-permute-start.1 = (f32[21,16,128]{2,1,0:T(8,128)S(1)}, f32[21,16,128]{2,1,0:T(8,128)S(1)}, u32[]{:S(2)}, u32[]{:S(2)}) collective-permute-start(f32[21,16,128]{2,1,0:T(8,128)S(1)} %get-tuple-element.33), channel_id=1, source_target_pairs={{0,1},{1,2},{2,3},{3,4},{4,5},{5,6},{6,7},{7,8},{8,9},{9,10},{10,1... | collective-permute-start | bytes 516104 | tf_op jit(solution)/shard_map/ppermute | solution.py:369
  16.9 7.0 %collective-permute-start.5 = (f32[21,8,128]{2,1,0:T(8,128)S(1)}, f32[21,8,128]{2,1,0:T(8,128)S(1)}, u32[]{:S(2)}, u32[]{:S(2)}) collective-permute-start(f32[21,8,128]{2,1,0:T(8,128)S(1)} %get-tuple-element.40), channel_id=1, source_target_pairs={{0,16},{16,32},{32,48},{48,64},{64,80},{80,96},{96,112},{112,128},... | collective-permute-start | bytes 258056 | tf_op jit(solution)/shard_map/ppermute | solution.py:369
  17.0 7.0 %collective-permute-start.4 = (f32[21,8,128]{2,1,0:T(8,128)S(1)}, f32[21,8,128]{2,1,0:T(8,128)S(1)}, u32[]{:S(2)}, u32[]{:S(2)}) collective-permute-start(f32[21,8,128]{2,1,0:T(8,128)S(1)} %get-tuple-element.36.corner_down), channel_id=1, source_target_pairs={{16,0},{32,16},{48,32},{64,48},{80,64},{96,80},{112,96},{128,112},... | collective-permute-start | bytes 258056 | tf_op jit(solution)/shard_map/ppermute | solution.py:369
  25.4 6.0 %collective-permute-start.6 = (f32[1,16,128]{2,1,0:T(8,128)S(1)}, f32[1,16,128]{2,1,0:T(8,128)S(1)}, u32[]{:S(2)}, u32[]{:S(2)}) collective-permute-start(f32[1,16,128]{2,1,0:T(8,128)S(1)} %get-tuple-element.45), channel_id=1, source_target_pairs={{1,0},{2,1},{3,2},{4,3},{5,4},{6,5},{7,6},{8,7},{9,8},{10,9},{11,1... | collective-permute-start | bytes 24584 | tf_op jit(solution)/shard_map/ppermute | solution.py:369
  26.7 5.5 %collective-permute-start.7 = (f32[1,16,128]{2,1,0:T(8,128)S(1)}, f32[1,16,128]{2,1,0:T(8,128)S(1)}, u32[]{:S(2)}, u32[]{:S(2)}) collective-permute-start(f32[1,16,128]{2,1,0:T(8,128)S(1)} %get-tuple-element.46), channel_id=1, source_target_pairs={{0,1},{1,2},{2,3},{3,4},{4,5},{5,6},{6,7},{7,8},{8,9},{9,10},{10,1... | collective-permute-start | bytes 24584 | tf_op jit(solution)/shard_map/ppermute | solution.py:369
  32.3 4.6 %collective-permute-start.8 = (f32[3,8,128]{2,1,0:T(8,128)S(1)}, f32[3,8,128]{2,1,0:T(8,128)S(1)}, u32[]{:S(2)}, u32[]{:S(2)}) collective-permute-start(f32[3,8,128]{2,1,0:T(8,128)S(1)} %get-tuple-element.47), channel_id=1, source_target_pairs={{16,0},{32,16},{48,32},{64,48},{80,64},{96,80},{112,96},{128,112},... | collective-permute-start | bytes 36872 | tf_op jit(solution)/shard_map/ppermute | solution.py:369
  36.0 2.6 %collective-permute-start.9 = (f32[3,8,128]{2,1,0:T(8,128)S(1)}, f32[3,8,128]{2,1,0:T(8,128)S(1)}, u32[]{:S(2)}, u32[]{:S(2)}) collective-permute-start(f32[3,8,128]{2,1,0:T(8,128)S(1)} %get-tuple-element.48), channel_id=1, source_target_pairs={{0,16},{16,32},{32,48},{48,64},{64,80},{80,96},{96,112},{112,128},... | collective-permute-start | bytes 36872 | tf_op jit(solution)/shard_map/ppermute | solution.py:369

commit v4 on v3

--- a/solution.py
+++ b/solution.py
@@ -115,7 +115,7 @@
                     weighted[index, i, j] = weighted[index, i, j] * weight
 
 
-def pack_corners(right, left, down, up):
+def pack_corners(right, left, weighted, down, up):
     for g in range(GROUPS + 1):
         down[g], up[g] = pack_rows(right[g], left[g])
 
@@ -405,7 +405,7 @@
         pl.CostEstimate(flops=stiffness.size, bytes_accessed=8 * stiffness.size, transcendentals=0),
         WIDE_LIMIT,
     )(stiffness, intact)
-    down, up = call(pack_corners, [ends_of_strip] * 2, [vmem] * 2)(right, left)
+    down, up = call(pack_corners, [ends_of_strip] * 2, [vmem] * 3)(right, left, weighted)
     edge, side = call(
         unpack_sides,
         [tiles, shape(PLANES, ROWS, LANES)],
@@ -420,11 +420,11 @@
     field_right, field_left = swap(to_left, to_right, "gy", False)
     down, up = call(pack_field, [edges] * 2, [vmem] * 3)(w, field_right, field_left)
     field_down, field_up = swap(down, up, "gx", True)
-    u, au, sums = call(second_half, [plane, plane, shape(ny, 1, LANES)], [vmem] * 12, [wide])(
+    u, au, sums = call(second_half, [plane, plane, shape(nx, 1, LANES)], [vmem] * 12, [wide])(
         factor, edge, side, weighted, corner, g, z, w, field_right, field_left, field_down, field_up
     )
-    sums = gathered_sum(sums, "gy")
-    sums = gathered_sum(jnp.broadcast_to(sums[None], (nx, 1, LANES)), "gx")
+    sums = gathered_sum(sums, "gx")
+    sums = gathered_sum(jnp.broadcast_to(sums[None], (ny, 1, LANES)), "gy")
     x, r = call(finish, [plane] * 2, [vmem] * 6)(sums, field, z, w, u, au)
     return x, r
 

time: 83.8 us -> 82.3 us (0.982)
  blocking collectives: 42.7 us -> 41.3 us
  waiting for transfers between devices: 5.71 us -> 4.48 us
  starting transfers between devices: 26.7 us -> 27.9 us
    all_to_all x2, blocking collectives: 42.7 us -> 41.3 us  [gathered_sum(): return jnp.sum(lax.all_to_all(rows, axis, 0, 0), axis=0)]
    ppermute x10, starting transfers between devices: 26.7 us -> 27.9 us  [swap(): return (lax.ppermute(first, axis, back), lax.ppermute(second, axis, ahead))]
    ppermute x10, waiting for transfers between devices: 5.71 us -> 4.48 us  [swap(): return (lax.ppermute(first, axis, back), lax.ppermute(second, axis, ahead))]
  transfers between devices with their start and end apart: 10 -> 10, of which waited for: 5 -> 6; matrix products, arithmetic and copies ran while one was open for 0% -> 0% of each run, Pallas kernels for 3% -> 3%
where the time goes in v4:
time: 82.3 us; the launch traced here: 82 us
  blocking collectives  41.3 us (50%)
  starting transfers between devices  27.9 us (34%)
  Pallas kernels  7.53 us (9%)
  waiting for transfers between devices  4.48 us (5%)
    all_to_all x2, blocking collectives, gathered_sum(): return jnp.sum(lax.all_to_all(rows, axis, 0, 0), axis=0)  41.3 us
    ppermute x10, starting transfers between devices, swap(): return (lax.ppermute(first, axis, back), lax.ppermute(second, axis, ahead))  27.9 us
    ppermute x10, waiting for transfers between devices, swap(): return (lax.ppermute(first, axis, back), lax.ppermute(second, axis, ahead))  4.48 us
    pallas_call x1, Pallas kernels, local(): call(weigh, [shape(*stiffness.shape)], [hbm] * 2, [pltpu.VMEM(intact.shap...  1.89 us
    pallas_call x1, Pallas kernels, local(): call(pack_factor, [shape(*factor.shape), strip, strip, own, own], [hbm],...  1.66 us
  transfers between devices with their start and end apart: 10, of which 6 were waited for; matrix products, arithmetic and copies ran while one was open for 0% of the time, Pallas kernels for 3%

profile of v4, /device:TPU:1, one launch (start us, length us, event | category | flops | bytes accessed | tf_op | source)
XLA Modules:
  0.0 82.0 jit_solution(5606768182992368311)
XLA Ops:
  0.6 0.0 copy-start.1
  0.6 0.0 copy-start
  0.6 1.7 %pack_factor.1 = (f32[17,3,3,16,128]{4,3,2,1,0:T(8,128)S(1)}, f32[21,16,128]{2,1,0:T(8,128)S(1)}, f32[21,16,128]{2,1,0:T(8,128)S(1)}, f32[79,8,128]{2,1,0:T(8,128)S(1)}, f32[79,8,128]{2,1,0:T(8,128)S(1)}) custom-call(f32[17,3,3,16,128]{4,3,2,1,0:T(8,128)} %factor_hbm.1), custom_call_target="tpu_custom_call" | custom-call | tf_op jit(solution)/shard_map/pack_factor/pallas_call | solution.py:388
  2.3 0.0 copy-done.1
  2.3 0.1 pack_right_side.1
  2.4 6.9 %collective-permute-start.2 = (f32[79,8,128]{2,1,0:T(8,128)S(1)}, f32[79,8,128]{2,1,0:T(8,128)S(1)}, u32[]{:S(2)}, u32[]{:S(2)}) collective-permute-start(f32[79,8,128]{2,1,0:T(8,128)S(1)} %get-tuple-element.34), channel_id=1, source_target_pairs={{16,0},{32,16},{48,32},{64,48},{80,64},{96,80},{112,96},{128,112},... | collective-permute-start | bytes 970760 | tf_op jit(solution)/shard_map/ppermute | solution.py:369
  9.3 0.0 collective-permute-start.3
  9.3 1.3 %collective-permute-start = (f32[21,16,128]{2,1,0:T(8,128)S(1)}, f32[21,16,128]{2,1,0:T(8,128)S(1)}, u32[]{:S(2)}, u32[]{:S(2)}) collective-permute-start(f32[21,16,128]{2,1,0:T(8,128)S(1)} %get-tuple-element.32), channel_id=1, source_target_pairs={{1,0},{2,1},{3,2},{4,3},{5,4},{6,5},{7,6},{8,7},{9,8},{10,9},{11,1... | collective-permute-start | bytes 516104 | tf_op jit(solution)/shard_map/ppermute | solution.py:369
  10.6 4.0 %collective-permute-start.1 = (f32[21,16,128]{2,1,0:T(8,128)S(1)}, f32[21,16,128]{2,1,0:T(8,128)S(1)}, u32[]{:S(2)}, u32[]{:S(2)}) collective-permute-start(f32[21,16,128]{2,1,0:T(8,128)S(1)} %get-tuple-element.33), channel_id=1, source_target_pairs={{0,1},{1,2},{2,3},{3,4},{4,5},{5,6},{6,7},{7,8},{8,9},{9,10},{10,1... | collective-permute-start | bytes 516104 | tf_op jit(solution)/shard_map/ppermute | solution.py:369
  14.6 0.0 copy-done
  14.6 1.9 %weigh.1.weighted = f32[33,3,3,16,128]{4,3,2,1,0:T(8,128)S(1)} custom-call(f32[33,3,3,16,128]{4,3,2,1,0:T(8,128)} %stiffness_hbm.1, s32[32,16,128]{2,1,0:T(8,128)S(1)} %copy-done), custom_call_target="tpu_custom_call" | custom-call | flops 608256 | bytes 4866048 | tf_op jit(solution)/shard_map/weigh/pallas_call | solution.py:400
  16.5 0.0 collective-permute-done.right
  16.5 0.4 collective-permute-done.1.left
  16.9 0.0 collective-permute-start.5
  17.0 4.7 %collective-permute-start.4 = (f32[21,8,128]{2,1,0:T(8,128)S(1)}, f32[21,8,128]{2,1,0:T(8,128)S(1)}, u32[]{:S(2)}, u32[]{:S(2)}) collective-permute-start(f32[21,8,128]{2,1,0:T(8,128)S(1)} %get-tuple-element.36.corner_down), channel_id=1, source_target_pairs={{16,0},{32,16},{48,32},{64,48},{80,64},{96,80},{112,96},{128,112},... | collective-permute-start | bytes 258056 | tf_op jit(solution)/shard_map/ppermute | solution.py:369
  21.7 0.0 collective-permute-done.2.own_down
  21.7 0.0 collective-permute-done.3.own_up
  21.7 0.4 unpack_sides.1
  22.1 0.4 collective-permute-done.5.corner_up
  22.4 0.2 collective-permute-done.4.corner_down
  22.6 1.4 %first_half.1 = (f32[153,8,128]{2,1,0:T(8,128)S(1)}, f32[3,16,128]{2,1,0:T(8,128)S(1)}, f32[3,16,128]{2,1,0:T(8,128)S(1)}, f32[3,16,128]{2,1,0:T(8,128)S(1)}, f3...) custom-call(f32[17,3,3,16,128]{4,3,2,1,0:T(8,128)S(1)} %get-tuple-element.27.factor, ...), custom_call_target="tpu_custom_call" | custom-call | tf_op jit(solution)/shard_map/first_half/pallas_call | solution.py:417
  24.0 1.3 %collective-permute-start.6 = (f32[1,16,128]{2,1,0:T(8,128)S(1)}, f32[1,16,128]{2,1,0:T(8,128)S(1)}, u32[]{:S(2)}, u32[]{:S(2)}) collective-permute-start(f32[1,16,128]{2,1,0:T(8,128)S(1)} %get-tuple-element.45), channel_id=1, source_target_pairs={{1,0},{2,1},{3,2},{4,3},{5,4},{6,5},{7,6},{8,7},{9,8},{10,9},{11,1... | collective-permute-start | bytes 24584 | tf_op jit(solution)/shard_map/ppermute | solution.py:369
  25.3 4.7 %collective-permute-start.7 = (f32[1,16,128]{2,1,0:T(8,128)S(1)}, f32[1,16,128]{2,1,0:T(8,128)S(1)}, u32[]{:S(2)}, u32[]{:S(2)}) collective-permute-start(f32[1,16,128]{2,1,0:T(8,128)S(1)} %get-tuple-element.46), channel_id=1, source_target_pairs={{0,1},{1,2},{2,3},{3,4},{4,5},{5,6},{6,7},{7,8},{8,9},{9,10},{10,1... | collective-permute-start | bytes 24584 | tf_op jit(solution)/shard_map/ppermute | solution.py:369
  30.1 0.0 collective-permute-done.6.right.field_right
  30.1 0.8 collective-permute-done.7.left.field_left
  30.8 5.0 %collective-permute-start.8 = (f32[3,8,128]{2,1,0:T(8,128)S(1)}, f32[3,8,128]{2,1,0:T(8,128)S(1)}, u32[]{:S(2)}, u32[]{:S(2)}) collective-permute-start(f32[3,8,128]{2,1,0:T(8,128)S(1)} %get-tuple-element.47), channel_id=1, source_target_pairs={{16,0},{32,16},{48,32},{64,48},{80,64},{96,80},{112,96},{128,112},... | collective-permute-start | bytes 36872 | tf_op jit(solution)/shard_map/ppermute | solution.py:369
  35.9 0.0 collective-permute-start.9
  35.9 0.8 %collective-permute-done.8.field_down = f32[3,8,128]{2,1,0:T(8,128)S(1)} collective-permute-done((f32[3,8,128]{2,1,0:T(8,128)S(1)}, f32[3,8,128]{2,1,0:T(8,128)S(1)}, u32[]{:S(2)}, u32[]{:S(2)}) %collective-permute-start.8) | collective-permute-done | bytes 12320 | tf_op jit(solution)/shard_map/ppermute | solution.py:369
  36.7 1.9 %collective-permute-done.9.field_up = f32[3,8,128]{2,1,0:T(8,128)S(1)} collective-permute-done((f32[3,8,128]{2,1,0:T(8,128)S(1)}, f32[3,8,128]{2,1,0:T(8,128)S(1)}, u32[]{:S(2)}, u32[]{:S(2)}) %collective-permute-start.9) | collective-permute-done | bytes 12320 | tf_op jit(solution)/shard_map/ppermute | solution.py:369
  38.6 1.3 %second_half.1 = (f32[3,16,128]{2,1,0:T(8,128)S(1)}, f32[3,16,128]{2,1,0:T(8,128)S(1)}, f32[32,1,128]{2,1,0:T(1,128)S(1)}) custom-call(f32[17,3,3,16,128]{4,3,2,1,0:T(8,128)S(1)} %get-tuple-element.27.factor, f32[153,8,128]{2,1,0:T(8,128)S(1)} %get-tuple-element.37.edge, f32[153,16,128]{2,1,0:T(8,128)S(1)} %get-tuple-element.38.side, ...), custom_call_target="tpu_custom_call" | custom-call | tf_op jit(solution)/shard_map/second_half/pallas_call | solution.py:423
  40.0 23.7 %all_to_all.10 = f32[32,1,128]{2,1,0:T(1,128)S(1)} all-to-all(f32[32,1,128]{2,1,0:T(1,128)S(1)} %get-tuple-element.49), channel_id=1, replica_groups=mesh['gx'=32,'gy'=16] {'gx'}, dimensions={0} | all-to-all | bytes 32768 | tf_op jit(solution)/shard_map/all_to_all | solution.py:373
  63.7 0.1 reduce_sum.20
  63.8 17.5 %all_to_all.11 = f32[16,1,128]{2,1,0:T(1,128)S(1)} all-to-all(f32[16,1,128]{2,1,0:T(1,128)S(1)} %broadcast_in_dim.2), channel_id=1, replica_groups=mesh['gx'=32,'gy'=16] {'gy'}, dimensions={0} | all-to-all | bytes 16384 | tf_op jit(solution)/shard_map/all_to_all | solution.py:373
  81.3 0.7 finish.1
  (4 shorter events, 0.1 us)
Async XLA Ops:
  0.6 1.7 %copy-start.1 = (f32[3,16,128]{2,1,0:T(8,128)S(1)}, f32[3,16,128]{2,1,0:T(8,128)}, u32[]{:S(2)}) copy-start(f32[3,16,128]{2,1,0:T(8,128)} %field.1) | copy-start | bytes 73732
  0.6 13.9 %copy-start = (s32[32,16,128]{2,1,0:T(8,128)S(1)}, s32[32,16,128]{2,1,0:T(8,128)}, u32[]{:S(2)}) copy-start(s32[32,16,128]{2,1,0:T(8,128)} %intact_hbm.1) | copy-start | bytes 786436
  2.4 19.3 %collective-permute-start.2 = (f32[79,8,128]{2,1,0:T(8,128)S(1)}, f32[79,8,128]{2,1,0:T(8,128)S(1)}, u32[]{:S(2)}, u32[]{:S(2)}) collective-permute-start(f32[79,8,128]{2,1,0:T(8,128)S(1)} %get-tuple-element.34), channel_id=1, source_target_pairs={{16,0},{32,16},{48,32},{64,48},{80,64},{96,80},{112,96},{128,112},... | collective-permute-start | bytes 970760 | tf_op jit(solution)/shard_map/ppermute | solution.py:369
  9.3 12.4 %collective-permute-start.3 = (f32[79,8,128]{2,1,0:T(8,128)S(1)}, f32[79,8,128]{2,1,0:T(8,128)S(1)}, u32[]{:S(2)}, u32[]{:S(2)}) collective-permute-start(f32[79,8,128]{2,1,0:T(8,128)S(1)} %get-tuple-element.35), channel_id=1, source_target_pairs={{0,16},{16,32},{32,48},{48,64},{64,80},{80,96},{96,112},{112,128},... | collective-permute-start | bytes 970760 | tf_op jit(solution)/shard_map/ppermute | solution.py:369
  9.3 7.2 %collective-permute-start = (f32[21,16,128]{2,1,0:T(8,128)S(1)}, f32[21,16,128]{2,1,0:T(8,128)S(1)}, u32[]{:S(2)}, u32[]{:S(2)}) collective-permute-start(f32[21,16,128]{2,1,0:T(8,128)S(1)} %get-tuple-element.32), channel_id=1, source_target_pairs={{1,0},{2,1},{3,2},{4,3},{5,4},{6,5},{7,6},{8,7},{9,8},{10,9},{11,1... | collective-permute-start | bytes 516104 | tf_op jit(solution)/shard_map/ppermute | solution.py:369
  10.6 6.3 %collective-permute-start.1 = (f32[21,16,128]{2,1,0:T(8,128)S(1)}, f32[21,16,128]{2,1,0:T(8,128)S(1)}, u32[]{:S(2)}, u32[]{:S(2)}) collective-permute-start(f32[21,16,128]{2,1,0:T(8,128)S(1)} %get-tuple-element.33), channel_id=1, source_target_pairs={{0,1},{1,2},{2,3},{3,4},{4,5},{5,6},{6,7},{7,8},{8,9},{9,10},{10,1... | collective-permute-start | bytes 516104 | tf_op jit(solution)/shard_map/ppermute | solution.py:369
  16.9 5.5 %collective-permute-start.5 = (f32[21,8,128]{2,1,0:T(8,128)S(1)}, f32[21,8,128]{2,1,0:T(8,128)S(1)}, u32[]{:S(2)}, u32[]{:S(2)}) collective-permute-start(f32[21,8,128]{2,1,0:T(8,128)S(1)} %get-tuple-element.40), channel_id=1, source_target_pairs={{0,16},{16,32},{32,48},{48,64},{64,80},{80,96},{96,112},{112,128},... | collective-permute-start | bytes 258056 | tf_op jit(solution)/shard_map/ppermute | solution.py:369
  17.0 5.6 %collective-permute-start.4 = (f32[21,8,128]{2,1,0:T(8,128)S(1)}, f32[21,8,128]{2,1,0:T(8,128)S(1)}, u32[]{:S(2)}, u32[]{:S(2)}) collective-permute-start(f32[21,8,128]{2,1,0:T(8,128)S(1)} %get-tuple-element.36.corner_down), channel_id=1, source_target_pairs={{16,0},{32,16},{48,32},{64,48},{80,64},{96,80},{112,96},{128,112},... | collective-permute-start | bytes 258056 | tf_op jit(solution)/shard_map/ppermute | solution.py:369
  24.0 6.0 %collective-permute-start.6 = (f32[1,16,128]{2,1,0:T(8,128)S(1)}, f32[1,16,128]{2,1,0:T(8,128)S(1)}, u32[]{:S(2)}, u32[]{:S(2)}) collective-permute-start(f32[1,16,128]{2,1,0:T(8,128)S(1)} %get-tuple-element.45), channel_id=1, source_target_pairs={{1,0},{2,1},{3,2},{4,3},{5,4},{6,5},{7,6},{8,7},{9,8},{10,9},{11,1... | collective-permute-start | bytes 24584 | tf_op jit(solution)/shard_map/ppermute | solution.py:369
  25.3 5.5 %collective-permute-start.7 = (f32[1,16,128]{2,1,0:T(8,128)S(1)}, f32[1,16,128]{2,1,0:T(8,128)S(1)}, u32[]{:S(2)}, u32[]{:S(2)}) collective-permute-start(f32[1,16,128]{2,1,0:T(8,128)S(1)} %get-tuple-element.46), channel_id=1, source_target_pairs={{0,1},{1,2},{2,3},{3,4},{4,5},{5,6},{6,7},{7,8},{8,9},{9,10},{10,1... | collective-permute-start | bytes 24584 | tf_op jit(solution)/shard_map/ppermute | solution.py:369
  30.8 5.9 %collective-permute-start.8 = (f32[3,8,128]{2,1,0:T(8,128)S(1)}, f32[3,8,128]{2,1,0:T(8,128)S(1)}, u32[]{:S(2)}, u32[]{:S(2)}) collective-permute-start(f32[3,8,128]{2,1,0:T(8,128)S(1)} %get-tuple-element.47), channel_id=1, source_target_pairs={{16,0},{32,16},{48,32},{64,48},{80,64},{96,80},{112,96},{128,112},... | collective-permute-start | bytes 36872 | tf_op jit(solution)/shard_map/ppermute | solution.py:369
  35.9 2.8 %collective-permute-start.9 = (f32[3,8,128]{2,1,0:T(8,128)S(1)}, f32[3,8,128]{2,1,0:T(8,128)S(1)}, u32[]{:S(2)}, u32[]{:S(2)}) collective-permute-start(f32[3,8,128]{2,1,0:T(8,128)S(1)} %get-tuple-element.48), channel_id=1, source_target_pairs={{0,16},{16,32},{32,48},{48,64},{64,80},{80,96},{96,112},{112,128},... | collective-permute-start | bytes 36872 | tf_op jit(solution)/shard_map/ppermute | solution.py:369

commit v5 on v4

--- a/solution.py
+++ b/solution.py
@@ -10,7 +10,6 @@
 LANES = 128
 LOWER = 17
 PLANES = LOWER * 9
-GROUPS = (PLANES + 7) // 8
 OWN_TILES = (PLANES + 1) // 2 + 2
 CENTRE = 0.8
 VMEM_LIMIT = 24 * 1024 * 1024
@@ -38,24 +37,69 @@
     return (p // 9, (p // 3) % 3, p % 3)
 
 
-def pack_lanes(planes, width):
+def seating():
+    hosts = [(p, 3 if OFFSETS[p // 9][2] > 0 else 0) for p in range(PLANES) if abs(OFFSETS[p // 9][2]) == 1]
+    below = OFFSETS.index((0, 0, -2))
+    wanted = [(p, layer) for p in [*range(0, 9), *range(18, 24)] for layer in range(NZ)]
+    wanted += [(p, layer) for p in range(9 * below, 9 * below + 9) for layer in (2, 3)]
+    riders, seats = {}, {}
+    for (guest, layer), (host, free) in zip(wanted, hosts):
+        riders[host] = (guest, layer, free)
+        seats.setdefault(guest, []).append((host, layer, free))
+    return riders, seats
+
+
+RIDERS, SEATS = seating()
+CARRIERS = [p for p in range(PLANES) if p not in SEATS]
+GROUPS = (len(CARRIERS) + 7) // 8
+assert len(CARRIERS) % 8 == 1 and sum(map(len, SEATS.values())) == len(RIDERS)
+
+
+def layer_of(rows):
+    return iota(rows, 1) & (NZ - 1)
+
+
+def carried(factor, p):
+    plane = factor[entry(p)]
+    if p in RIDERS:
+        guest, layer, free = RIDERS[p]
+        moved = factor[entry(guest)]
+        if free != layer:
+            moved = pltpu.roll(moved, (free - layer) % LANES, 1)
+        plane = jnp.where(layer_of(ROWS) == free, moved, plane)
+    return plane
+
+
+def seat_guests(store):
+    rows = store.shape[1]
+    for guest, seats in SEATS.items():
+        plane = None
+        for host, layer, free in seats:
+            moved = store[host]
+            if free != layer:
+                moved = pltpu.roll(moved, (layer - free) % LANES, 1)
+            plane = moved if plane is None else jnp.where(layer_of(rows) == layer, moved, plane)
+        store[guest] = plane
+
+
+def pack_lanes(planes, width, first=0):
     shift = width.bit_length() - 1
     slots = LANES // width
     slot = iota(ROWS, 1) >> shift
     to_left = jnp.zeros((ROWS, LANES), jnp.float32)
     to_right = to_left
-    for k, plane in enumerate(planes):
+    for k, plane in enumerate(planes, first):
         rolled = pltpu.roll(plane, k * width, 1) if k else plane
         to_left = jnp.where(slot == k, rolled, to_left)
         to_right = jnp.where(slot == (k - 1) % slots, rolled, to_right)
     return to_left, to_right
 
 
-def unpack_lanes(right, left, width, count):
+def unpack_lanes(right, left, width, count, first=0):
     shift = width.bit_length() - 1
     even = ((iota(right.shape[0], 1) >> shift) & 1) == 0
     mixed = (jnp.where(even, right, left), jnp.where(even, left, right))
-    return [pltpu.roll(mixed[k & 1], LANES - k * width, 1) if k else mixed[0] for k in range(count)]
+    return [pltpu.roll(mixed[k & 1], LANES - k * width, 1) if k else mixed[0] for k in range(first, first + count)]
 
 
 def pack_rows(first, second):
@@ -70,7 +114,7 @@
     return jnp.where(upper, down, up), pltpu.roll(jnp.where(upper, up, down), 4, 0)
 
 
-CHUNKS = ((0, 5), (5, 9), (9, 13), (13, LOWER))
+CHUNKS = ((0, 6), (6, 11), (11, LOWER))
 
 
 def pack_factor(factor_hbm, factor, to_left, to_right, down, up, sems):
@@ -84,9 +128,11 @@
     for k, (low, high) in enumerate(CHUNKS):
         copies[k].wait()
         ready = 9 * high
-        while group < GROUPS and min(8 * group + 8, PLANES) <= ready:
-            planes = [factor[entry(p)] for p in range(8 * group, min(8 * group + 8, PLANES))]
-            to_left[group], to_right[group] = pack_lanes(planes, 16)
+        while group < GROUPS:
+            members = CARRIERS[8 * group : 8 * group + 8]
+            if max([*members, *(RIDERS[p][0] for p in members if p in RIDERS)]) >= ready:
+                break
+            to_left[group], to_right[group] = pack_lanes([carried(factor, p) for p in members], 16)
             group += 1
         while tile < OWN_TILES - 2 and min(2 * tile + 2, PLANES) <= ready:
             down[tile], up[tile] = pack_rows(factor[entry(2 * tile)], factor[entry(min(2 * tile + 1, PLANES - 1))])
@@ -95,7 +141,10 @@
 
 def pack_right_side(field, left_in, right_in, down_in, up_in, kept, to_left, to_right, down, up):
     kept[...] = field[...]
-    to_left[GROUPS], to_right[GROUPS] = pack_lanes([field[k] for k in range(3)], 32)
+    last, lane = GROUPS - 1, iota(ROWS, 1)
+    low, high = pack_lanes([field[k] for k in range(3)], 32, 1)
+    to_left[last] = jnp.where(lane < 32, left_in[last], low)
+    to_right[last] = jnp.where(lane >= 96, right_in[last], high)
     down[OWN_TILES - 2], up[OWN_TILES - 2] = pack_rows(field[0], field[1])
     down[OWN_TILES - 1], up[OWN_TILES - 1] = pack_rows(field[2], field[2])
 
@@ -116,7 +165,7 @@
 
 
 def pack_corners(right, left, weighted, down, up):
-    for g in range(GROUPS + 1):
+    for g in range(GROUPS):
         down[g], up[g] = pack_rows(right[g], left[g])
 
 
@@ -133,15 +182,19 @@
         if 2 * m + 1 < PLANES:
             edge[2 * m + 1] = second
     for g in range(GROUPS):
-        for k, plane in enumerate(unpack_lanes(right[g], left[g], 16, min(8, PLANES - 8 * g))):
-            side[8 * g + k] = plane
+        members = CARRIERS[8 * g : 8 * g + 8]
+        for p, plane in zip(members, unpack_lanes(right[g], left[g], 16, len(members))):
+            side[p] = plane
+    seat_guests(side)
 
 
 def unpack_corners(corner_down, corner_up, corner):
     for g in range(GROUPS):
         right, left = unpack_rows(corner_down[g], corner_up[g])
-        for k, plane in enumerate(unpack_lanes(right, left, 16, min(8, PLANES - 8 * g))):
-            corner[8 * g + k] = plane
+        members = CARRIERS[8 * g : 8 * g + 8]
+        for p, plane in zip(members, unpack_lanes(right, left, 16, len(members))):
+            corner[p] = plane
+    seat_guests(corner)
 
 
 def put(wide, component, tile, values):
@@ -266,7 +319,7 @@
     edges = [*unpack_rows(down_a, up_a), unpack_rows(down_b, up_b)[0]]
     edge_right, edge_left = unpack_rows(down_c, up_c)
     sides = unpack_lanes(
-        jnp.concatenate([right, edge_right], axis=0), jnp.concatenate([left, edge_left], axis=0), 32, 3
+        jnp.concatenate([right, edge_right], axis=0), jnp.concatenate([left, edge_left], axis=0), 32, 3, 1
     )
     for j in range(3):
         put(wide, j, 0, mask_edge(jnp.concatenate([field[j], edges[j]], axis=0), edge_out))
@@ -285,14 +338,14 @@
     corner, g_out, z_out, w_out, to_left, to_right, wide,
 ):
     unpack_corners(corner_down, corner_up, corner)
-    a, b, c = OWN_TILES - 2, OWN_TILES - 1, GROUPS
+    a, b, c = OWN_TILES - 2, OWN_TILES - 1, GROUPS - 1
     pieces = (
         (own_down[a], own_up[a]), (own_down[b], own_up[b]), (corner_down[c], corner_up[c]), right[c], left[c],
     )
     image, zvec, product = chain((factor, edge, side, corner), weighted, field, pieces, wide)
     for i in range(3):
         g_out[i], z_out[i], w_out[i] = image[i], zvec[i], product[i]
-    to_left[0], to_right[0] = pack_lanes(product, 32)
+    to_left[0], to_right[0] = pack_lanes(product, 32, 1)
 
 
 def dot(first, second):
@@ -376,9 +429,9 @@
 def local(right_side, stiffness, factor, intact):
     nx, ny = lax.axis_size("gx"), lax.axis_size("gy")
     plane = shape(3, ROWS, LANES)
-    strip = shape(GROUPS + 1, ROWS, LANES)
+    strip = shape(GROUPS, ROWS, LANES)
     own = shape(OWN_TILES, 8, LANES)
-    ends_of_strip = shape(GROUPS + 1, 8, LANES)
+    ends_of_strip = shape(GROUPS, 8, LANES)
     small = shape(1, ROWS, LANES)
     edges = shape(3, 8, LANES)
     tiles = shape(PLANES, 8, LANES)

time: 82.3 us -> 81.7 us (level)
  no operation moved by 1% of the time
where the time goes in v5:
time: 81.7 us; the launch traced here: 81.4 us
  blocking collectives  40.9 us (50%)
  starting transfers between devices  27.8 us (34%)
  Pallas kernels  7.8 us (10%)
  waiting for transfers between devices  4.06 us (5%)
    all_to_all x2, blocking collectives, gathered_sum(): return jnp.sum(lax.all_to_all(rows, axis, 0, 0), axis=0)  40.9 us
    ppermute x10, starting transfers between devices, swap(): return (lax.ppermute(first, axis, back), lax.ppermute(second, axis, ahead))  27.8 us
    ppermute x10, waiting for transfers between devices, swap(): return (lax.ppermute(first, axis, back), lax.ppermute(second, axis, ahead))  4.06 us
    pallas_call x1, Pallas kernels, local(): call(weigh, [shape(*stiffness.shape)], [hbm] * 2, [pltpu.VMEM(intact.shap...  1.89 us
    pallas_call x1, Pallas kernels, local(): call(pack_factor, [shape(*factor.shape), strip, strip, own, own], [hbm],...  1.79 us
  transfers between devices with their start and end apart: 10, of which 6 were waited for; matrix products, arithmetic and copies ran while one was open for 0% of the time, Pallas kernels for 3%

profile of v5, /device:TPU:1, one launch (start us, length us, event | category | flops | bytes accessed | tf_op | source)
XLA Modules:
  0.0 81.4 jit_solution(2199513004269477395)
XLA Ops:
  0.6 0.0 copy-start.1
  0.6 0.0 copy-start
  0.6 1.8 %pack_factor.1 = (f32[17,3,3,16,128]{4,3,2,1,0:T(8,128)S(1)}, f32[17,16,128]{2,1,0:T(8,128)S(1)}, f32[17,16,128]{2,1,0:T(8,128)S(1)}, f32[79,8,128]{2,1,0:T(8,128)S(1)}, f32[79,8,128]{2,1,0:T(8,128)S(1)}) custom-call(f32[17,3,3,16,128]{4,3,2,1,0:T(8,128)} %factor_hbm.1), custom_call_target="tpu_custom_call" | custom-call | tf_op jit(solution)/shard_map/pack_factor/pallas_call | solution.py:441
  2.4 0.0 copy-done.1
  2.5 0.1 pack_right_side.1
  2.5 6.9 %collective-permute-start.2 = (f32[79,8,128]{2,1,0:T(8,128)S(1)}, f32[79,8,128]{2,1,0:T(8,128)S(1)}, u32[]{:S(2)}, u32[]{:S(2)}) collective-permute-start(f32[79,8,128]{2,1,0:T(8,128)S(1)} %get-tuple-element.34), channel_id=1, source_target_pairs={{16,0},{32,16},{48,32},{64,48},{80,64},{96,80},{112,96},{128,112},... | collective-permute-start | bytes 970760 | tf_op jit(solution)/shard_map/ppermute | solution.py:422
  9.4 0.0 collective-permute-start.3
  9.4 1.3 %collective-permute-start = (f32[17,16,128]{2,1,0:T(8,128)S(1)}, f32[17,16,128]{2,1,0:T(8,128)S(1)}, u32[]{:S(2)}, u32[]{:S(2)}) collective-permute-start(f32[17,16,128]{2,1,0:T(8,128)S(1)} %get-tuple-element.32), channel_id=1, source_target_pairs={{1,0},{2,1},{3,2},{4,3},{5,4},{6,5},{7,6},{8,7},{9,8},{10,9},{11,1... | collective-permute-start | bytes 417800 | tf_op jit(solution)/shard_map/ppermute | solution.py:422
  10.7 4.0 %collective-permute-start.1 = (f32[17,16,128]{2,1,0:T(8,128)S(1)}, f32[17,16,128]{2,1,0:T(8,128)S(1)}, u32[]{:S(2)}, u32[]{:S(2)}) collective-permute-start(f32[17,16,128]{2,1,0:T(8,128)S(1)} %get-tuple-element.33), channel_id=1, source_target_pairs={{0,1},{1,2},{2,3},{3,4},{4,5},{5,6},{6,7},{7,8},{8,9},{9,10},{10,1... | collective-permute-start | bytes 417800 | tf_op jit(solution)/shard_map/ppermute | solution.py:422
  14.7 0.0 copy-done
  14.7 1.9 %weigh.1.weighted = f32[33,3,3,16,128]{4,3,2,1,0:T(8,128)S(1)} custom-call(f32[33,3,3,16,128]{4,3,2,1,0:T(8,128)} %stiffness_hbm.1, s32[32,16,128]{2,1,0:T(8,128)S(1)} %copy-done), custom_call_target="tpu_custom_call" | custom-call | flops 608256 | bytes 4866048 | tf_op jit(solution)/shard_map/weigh/pallas_call | solution.py:453
  16.6 0.0 collective-permute-done.right
  16.6 0.1 collective-permute-done.1.left
  16.7 0.0 collective-permute-start.5
  16.8 4.7 %collective-permute-start.4 = (f32[17,8,128]{2,1,0:T(8,128)S(1)}, f32[17,8,128]{2,1,0:T(8,128)S(1)}, u32[]{:S(2)}, u32[]{:S(2)}) collective-permute-start(f32[17,8,128]{2,1,0:T(8,128)S(1)} %get-tuple-element.36.corner_down), channel_id=1, source_target_pairs={{16,0},{32,16},{48,32},{64,48},{80,64},{96,80},{112,96},{128,112},... | collective-permute-start | bytes 208904 | tf_op jit(solution)/shard_map/ppermute | solution.py:422
  21.5 0.0 collective-permute-done.2.own_down
  21.5 0.0 collective-permute-done.3.own_up
  21.5 0.5 unpack_sides.1
  21.9 0.3 collective-permute-done.5.corner_up
  22.2 0.2 collective-permute-done.4.corner_down
  22.4 1.5 %first_half.1 = (f32[153,8,128]{2,1,0:T(8,128)S(1)}, f32[3,16,128]{2,1,0:T(8,128)S(1)}, f32[3,16,128]{2,1,0:T(8,128)S(1)}, f32[3,16,128]{2,1,0:T(8,128)S(1)}, f3...) custom-call(f32[17,3,3,16,128]{4,3,2,1,0:T(8,128)S(1)} %get-tuple-element.27.factor, ...), custom_call_target="tpu_custom_call" | custom-call | tf_op jit(solution)/shard_map/first_half/pallas_call | solution.py:470
  23.9 1.3 %collective-permute-start.6 = (f32[1,16,128]{2,1,0:T(8,128)S(1)}, f32[1,16,128]{2,1,0:T(8,128)S(1)}, u32[]{:S(2)}, u32[]{:S(2)}) collective-permute-start(f32[1,16,128]{2,1,0:T(8,128)S(1)} %get-tuple-element.45), channel_id=1, source_target_pairs={{1,0},{2,1},{3,2},{4,3},{5,4},{6,5},{7,6},{8,7},{9,8},{10,9},{11,1... | collective-permute-start | bytes 24584 | tf_op jit(solution)/shard_map/ppermute | solution.py:422
  25.2 4.7 %collective-permute-start.7 = (f32[1,16,128]{2,1,0:T(8,128)S(1)}, f32[1,16,128]{2,1,0:T(8,128)S(1)}, u32[]{:S(2)}, u32[]{:S(2)}) collective-permute-start(f32[1,16,128]{2,1,0:T(8,128)S(1)} %get-tuple-element.46), channel_id=1, source_target_pairs={{0,1},{1,2},{2,3},{3,4},{4,5},{5,6},{6,7},{7,8},{8,9},{9,10},{10,1... | collective-permute-start | bytes 24584 | tf_op jit(solution)/shard_map/ppermute | solution.py:422
  29.9 0.0 collective-permute-done.6.right.field_right
  29.9 0.8 collective-permute-done.7.left.field_left
  30.7 4.9 %collective-permute-start.8 = (f32[3,8,128]{2,1,0:T(8,128)S(1)}, f32[3,8,128]{2,1,0:T(8,128)S(1)}, u32[]{:S(2)}, u32[]{:S(2)}) collective-permute-start(f32[3,8,128]{2,1,0:T(8,128)S(1)} %get-tuple-element.47), channel_id=1, source_target_pairs={{16,0},{32,16},{48,32},{64,48},{80,64},{96,80},{112,96},{128,112},... | collective-permute-start | bytes 36872 | tf_op jit(solution)/shard_map/ppermute | solution.py:422
  35.5 0.0 collective-permute-start.9
  35.5 0.8 %collective-permute-done.8.field_down = f32[3,8,128]{2,1,0:T(8,128)S(1)} collective-permute-done((f32[3,8,128]{2,1,0:T(8,128)S(1)}, f32[3,8,128]{2,1,0:T(8,128)S(1)}, u32[]{:S(2)}, u32[]{:S(2)}) %collective-permute-start.8) | collective-permute-done | bytes 12320 | tf_op jit(solution)/shard_map/ppermute | solution.py:422
  36.4 1.9 %collective-permute-done.9.field_up = f32[3,8,128]{2,1,0:T(8,128)S(1)} collective-permute-done((f32[3,8,128]{2,1,0:T(8,128)S(1)}, f32[3,8,128]{2,1,0:T(8,128)S(1)}, u32[]{:S(2)}, u32[]{:S(2)}) %collective-permute-start.9) | collective-permute-done | bytes 12320 | tf_op jit(solution)/shard_map/ppermute | solution.py:422
  38.3 1.3 %second_half.1 = (f32[3,16,128]{2,1,0:T(8,128)S(1)}, f32[3,16,128]{2,1,0:T(8,128)S(1)}, f32[32,1,128]{2,1,0:T(1,128)S(1)}) custom-call(f32[17,3,3,16,128]{4,3,2,1,0:T(8,128)S(1)} %get-tuple-element.27.factor, f32[153,8,128]{2,1,0:T(8,128)S(1)} %get-tuple-element.37.edge, f32[153,16,128]{2,1,0:T(8,128)S(1)} %get-tuple-element.38.side, ...), custom_call_target="tpu_custom_call" | custom-call | tf_op jit(solution)/shard_map/second_half/pallas_call | solution.py:476
  39.6 23.4 %all_to_all.10 = f32[32,1,128]{2,1,0:T(1,128)S(1)} all-to-all(f32[32,1,128]{2,1,0:T(1,128)S(1)} %get-tuple-element.49), channel_id=1, replica_groups=mesh['gx'=32,'gy'=16] {'gx'}, dimensions={0} | all-to-all | bytes 32768 | tf_op jit(solution)/shard_map/all_to_all | solution.py:426
  63.0 0.1 reduce_sum.20
  63.1 17.5 %all_to_all.11 = f32[16,1,128]{2,1,0:T(1,128)S(1)} all-to-all(f32[16,1,128]{2,1,0:T(1,128)S(1)} %broadcast_in_dim.2), channel_id=1, replica_groups=mesh['gx'=32,'gy'=16] {'gy'}, dimensions={0} | all-to-all | bytes 16384 | tf_op jit(solution)/shard_map/all_to_all | solution.py:426
  80.6 0.7 finish.1
  (4 shorter events, 0.1 us)
Async XLA Ops:
  0.6 1.8 %copy-start.1 = (f32[3,16,128]{2,1,0:T(8,128)S(1)}, f32[3,16,128]{2,1,0:T(8,128)}, u32[]{:S(2)}) copy-start(f32[3,16,128]{2,1,0:T(8,128)} %field.1) | copy-start | bytes 73732
  0.6 14.1 %copy-start = (s32[32,16,128]{2,1,0:T(8,128)S(1)}, s32[32,16,128]{2,1,0:T(8,128)}, u32[]{:S(2)}) copy-start(s32[32,16,128]{2,1,0:T(8,128)} %intact_hbm.1) | copy-start | bytes 786436
  2.5 18.9 %collective-permute-start.2 = (f32[79,8,128]{2,1,0:T(8,128)S(1)}, f32[79,8,128]{2,1,0:T(8,128)S(1)}, u32[]{:S(2)}, u32[]{:S(2)}) collective-permute-start(f32[79,8,128]{2,1,0:T(8,128)S(1)} %get-tuple-element.34), channel_id=1, source_target_pairs={{16,0},{32,16},{48,32},{64,48},{80,64},{96,80},{112,96},{128,112},... | collective-permute-start | bytes 970760 | tf_op jit(solution)/shard_map/ppermute | solution.py:422
  9.4 12.1 %collective-permute-start.3 = (f32[79,8,128]{2,1,0:T(8,128)S(1)}, f32[79,8,128]{2,1,0:T(8,128)S(1)}, u32[]{:S(2)}, u32[]{:S(2)}) collective-permute-start(f32[79,8,128]{2,1,0:T(8,128)S(1)} %get-tuple-element.35), channel_id=1, source_target_pairs={{0,16},{16,32},{32,48},{48,64},{64,80},{80,96},{96,112},{112,128},... | collective-permute-start | bytes 970760 | tf_op jit(solution)/shard_map/ppermute | solution.py:422
  9.4 7.2 %collective-permute-start = (f32[17,16,128]{2,1,0:T(8,128)S(1)}, f32[17,16,128]{2,1,0:T(8,128)S(1)}, u32[]{:S(2)}, u32[]{:S(2)}) collective-permute-start(f32[17,16,128]{2,1,0:T(8,128)S(1)} %get-tuple-element.32), channel_id=1, source_target_pairs={{1,0},{2,1},{3,2},{4,3},{5,4},{6,5},{7,6},{8,7},{9,8},{10,9},{11,1... | collective-permute-start | bytes 417800 | tf_op jit(solution)/shard_map/ppermute | solution.py:422
  10.7 6.0 %collective-permute-start.1 = (f32[17,16,128]{2,1,0:T(8,128)S(1)}, f32[17,16,128]{2,1,0:T(8,128)S(1)}, u32[]{:S(2)}, u32[]{:S(2)}) collective-permute-start(f32[17,16,128]{2,1,0:T(8,128)S(1)} %get-tuple-element.33), channel_id=1, source_target_pairs={{0,1},{1,2},{2,3},{3,4},{4,5},{5,6},{6,7},{7,8},{8,9},{9,10},{10,1... | collective-permute-start | bytes 417800 | tf_op jit(solution)/shard_map/ppermute | solution.py:422
  16.7 5.5 %collective-permute-start.5 = (f32[17,8,128]{2,1,0:T(8,128)S(1)}, f32[17,8,128]{2,1,0:T(8,128)S(1)}, u32[]{:S(2)}, u32[]{:S(2)}) collective-permute-start(f32[17,8,128]{2,1,0:T(8,128)S(1)} %get-tuple-element.40), channel_id=1, source_target_pairs={{0,16},{16,32},{32,48},{48,64},{64,80},{80,96},{96,112},{112,128},... | collective-permute-start | bytes 208904 | tf_op jit(solution)/shard_map/ppermute | solution.py:422
  16.8 5.6 %collective-permute-start.4 = (f32[17,8,128]{2,1,0:T(8,128)S(1)}, f32[17,8,128]{2,1,0:T(8,128)S(1)}, u32[]{:S(2)}, u32[]{:S(2)}) collective-permute-start(f32[17,8,128]{2,1,0:T(8,128)S(1)} %get-tuple-element.36.corner_down), channel_id=1, source_target_pairs={{16,0},{32,16},{48,32},{64,48},{80,64},{96,80},{112,96},{128,112},... | collective-permute-start | bytes 208904 | tf_op jit(solution)/shard_map/ppermute | solution.py:422
  23.9 6.0 %collective-permute-start.6 = (f32[1,16,128]{2,1,0:T(8,128)S(1)}, f32[1,16,128]{2,1,0:T(8,128)S(1)}, u32[]{:S(2)}, u32[]{:S(2)}) collective-permute-start(f32[1,16,128]{2,1,0:T(8,128)S(1)} %get-tuple-element.45), channel_id=1, source_target_pairs={{1,0},{2,1},{3,2},{4,3},{5,4},{6,5},{7,6},{8,7},{9,8},{10,9},{11,1... | collective-permute-start | bytes 24584 | tf_op jit(solution)/shard_map/ppermute | solution.py:422
  25.2 5.5 %collective-permute-start.7 = (f32[1,16,128]{2,1,0:T(8,128)S(1)}, f32[1,16,128]{2,1,0:T(8,128)S(1)}, u32[]{:S(2)}, u32[]{:S(2)}) collective-permute-start(f32[1,16,128]{2,1,0:T(8,128)S(1)} %get-tuple-element.46), channel_id=1, source_target_pairs={{0,1},{1,2},{2,3},{3,4},{4,5},{5,6},{6,7},{7,8},{8,9},{9,10},{10,1... | collective-permute-start | bytes 24584 | tf_op jit(solution)/shard_map/ppermute | solution.py:422
  30.7 5.7 %collective-permute-start.8 = (f32[3,8,128]{2,1,0:T(8,128)S(1)}, f32[3,8,128]{2,1,0:T(8,128)S(1)}, u32[]{:S(2)}, u32[]{:S(2)}) collective-permute-start(f32[3,8,128]{2,1,0:T(8,128)S(1)} %get-tuple-element.47), channel_id=1, source_target_pairs={{16,0},{32,16},{48,32},{64,48},{80,64},{96,80},{112,96},{128,112},... | collective-permute-start | bytes 36872 | tf_op jit(solution)/shard_map/ppermute | solution.py:422
  35.5 2.8 %collective-permute-start.9 = (f32[3,8,128]{2,1,0:T(8,128)S(1)}, f32[3,8,128]{2,1,0:T(8,128)S(1)}, u32[]{:S(2)}, u32[]{:S(2)}) collective-permute-start(f32[3,8,128]{2,1,0:T(8,128)S(1)} %get-tuple-element.48), channel_id=1, source_target_pairs={{0,16},{16,32},{32,48},{48,64},{64,80},{80,96},{96,112},{112,128},... | collective-permute-start | bytes 36872 | tf_op jit(solution)/shard_map/ppermute | solution.py:422

commit v6 on v5

--- a/solution.py
+++ b/solution.py
@@ -86,13 +86,16 @@
     shift = width.bit_length() - 1
     slots = LANES // width
     slot = iota(ROWS, 1) >> shift
-    to_left = jnp.zeros((ROWS, LANES), jnp.float32)
-    to_right = to_left
+    halves = [None, None]
     for k, plane in enumerate(planes, first):
         rolled = pltpu.roll(plane, k * width, 1) if k else plane
-        to_left = jnp.where(slot == k, rolled, to_left)
-        to_right = jnp.where(slot == (k - 1) % slots, rolled, to_right)
-    return to_left, to_right
+        held = halves[k & 1]
+        if held is not None:
+            rolled = jnp.where((slot == k) | (slot == (k - 1) % slots), rolled, held)
+        halves[k & 1] = rolled
+    even, odd = (jnp.zeros((ROWS, LANES), jnp.float32) if half is None else half for half in halves)
+    is_even = (slot & 1) == 0
+    return jnp.where(is_even, even, odd), jnp.where(is_even, odd, even)
 
 
 def unpack_lanes(right, left, width, count, first=0):
@@ -141,6 +144,8 @@
 
 def pack_right_side(field, left_in, right_in, down_in, up_in, kept, to_left, to_right, down, up):
     kept[...] = field[...]
+    for held, packed in ((left_in, to_left), (right_in, to_right), (down_in, down), (up_in, up)):
+        packed[...] = held[...]
     last, lane = GROUPS - 1, iota(ROWS, 1)
     low, high = pack_lanes([field[k] for k in range(3)], 32, 1)
     to_left[last] = jnp.where(lane < 32, left_in[last], low)

time: 81.7 us -> 81.7 us (level)
  no operation moved by 1% of the time
where the time goes in v6:
time: 81.7 us; the launch traced here: 81.4 us
  blocking collectives  40.9 us (50%)
  starting transfers between devices  27.8 us (34%)
  Pallas kernels  7.85 us (10%)
  waiting for transfers between devices  4.06 us (5%)
    all_to_all x2, blocking collectives, gathered_sum(): return jnp.sum(lax.all_to_all(rows, axis, 0, 0), axis=0)  40.9 us
    ppermute x10, starting transfers between devices, swap(): return (lax.ppermute(first, axis, back), lax.ppermute(second, axis, ahead))  27.8 us
    ppermute x10, waiting for transfers between devices, swap(): return (lax.ppermute(first, axis, back), lax.ppermute(second, axis, ahead))  4.06 us
    pallas_call x1, Pallas kernels, local(): call(weigh, [shape(*stiffness.shape)], [hbm] * 2, [pltpu.VMEM(intact.shap...  1.89 us
    pallas_call x1, Pallas kernels, local(): call(pack_factor, [shape(*factor.shape), strip, strip, own, own], [hbm],...  1.78 us
  transfers between devices with their start and end apart: 10, of which 6 were waited for; matrix products, arithmetic and copies ran while one was open for 0% of the time, Pallas kernels for 3%

profile of v6, /device:TPU:1, one launch (start us, length us, event | category | flops | bytes accessed | tf_op | source)
XLA Modules:
  0.0 81.4 jit_solution(12677030323616248113)
XLA Ops:
  0.6 0.0 copy-start.1
  0.6 0.0 copy-start
  0.6 1.8 %pack_factor.1 = (f32[17,3,3,16,128]{4,3,2,1,0:T(8,128)S(1)}, f32[17,16,128]{2,1,0:T(8,128)S(1)}, f32[17,16,128]{2,1,0:T(8,128)S(1)}, f32[79,8,128]{2,1,0:T(8,128)S(1)}, f32[79,8,128]{2,1,0:T(8,128)S(1)}) custom-call(f32[17,3,3,16,128]{4,3,2,1,0:T(8,128)} %factor_hbm.1), custom_call_target="tpu_custom_call" | custom-call | tf_op jit(solution)/shard_map/pack_factor/pallas_call | solution.py:446
  2.4 0.0 copy-done.1
  2.5 0.1 pack_right_side.1
  2.6 6.9 %collective-permute-start.2 = (f32[79,8,128]{2,1,0:T(8,128)S(1)}, f32[79,8,128]{2,1,0:T(8,128)S(1)}, u32[]{:S(2)}, u32[]{:S(2)}) collective-permute-start(f32[79,8,128]{2,1,0:T(8,128)S(1)} %get-tuple-element.34), channel_id=1, source_target_pairs={{16,0},{32,16},{48,32},{64,48},{80,64},{96,80},{112,96},{128,112},... | collective-permute-start | bytes 970760 | tf_op jit(solution)/shard_map/ppermute | solution.py:427
  9.5 0.0 collective-permute-start.3
  9.5 1.3 %collective-permute-start = (f32[17,16,128]{2,1,0:T(8,128)S(1)}, f32[17,16,128]{2,1,0:T(8,128)S(1)}, u32[]{:S(2)}, u32[]{:S(2)}) collective-permute-start(f32[17,16,128]{2,1,0:T(8,128)S(1)} %get-tuple-element.32), channel_id=1, source_target_pairs={{1,0},{2,1},{3,2},{4,3},{5,4},{6,5},{7,6},{8,7},{9,8},{10,9},{11,1... | collective-permute-start | bytes 417800 | tf_op jit(solution)/shard_map/ppermute | solution.py:427
  10.8 4.0 %collective-permute-start.1 = (f32[17,16,128]{2,1,0:T(8,128)S(1)}, f32[17,16,128]{2,1,0:T(8,128)S(1)}, u32[]{:S(2)}, u32[]{:S(2)}) collective-permute-start(f32[17,16,128]{2,1,0:T(8,128)S(1)} %get-tuple-element.33), channel_id=1, source_target_pairs={{0,1},{1,2},{2,3},{3,4},{4,5},{5,6},{6,7},{7,8},{8,9},{9,10},{10,1... | collective-permute-start | bytes 417800 | tf_op jit(solution)/shard_map/ppermute | solution.py:427
  14.8 0.0 copy-done
  14.8 1.9 %weigh.1.weighted = f32[33,3,3,16,128]{4,3,2,1,0:T(8,128)S(1)} custom-call(f32[33,3,3,16,128]{4,3,2,1,0:T(8,128)} %stiffness_hbm.1, s32[32,16,128]{2,1,0:T(8,128)S(1)} %copy-done), custom_call_target="tpu_custom_call" | custom-call | flops 608256 | bytes 4866048 | tf_op jit(solution)/shard_map/weigh/pallas_call | solution.py:458
  16.7 0.0 collective-permute-done.right
  16.7 0.1 collective-permute-done.1.left
  16.8 0.0 collective-permute-start.5
  16.8 4.7 %collective-permute-start.4 = (f32[17,8,128]{2,1,0:T(8,128)S(1)}, f32[17,8,128]{2,1,0:T(8,128)S(1)}, u32[]{:S(2)}, u32[]{:S(2)}) collective-permute-start(f32[17,8,128]{2,1,0:T(8,128)S(1)} %get-tuple-element.36.corner_down), channel_id=1, source_target_pairs={{16,0},{32,16},{48,32},{64,48},{80,64},{96,80},{112,96},{128,112},... | collective-permute-start | bytes 208904 | tf_op jit(solution)/shard_map/ppermute | solution.py:427
  21.5 0.0 collective-permute-done.2.own_down
  21.5 0.0 collective-permute-done.3.own_up
  21.5 0.5 unpack_sides.1
  22.0 0.3 collective-permute-done.5.corner_up
  22.3 0.2 collective-permute-done.4.corner_down
  22.4 1.5 %first_half.1 = (f32[153,8,128]{2,1,0:T(8,128)S(1)}, f32[3,16,128]{2,1,0:T(8,128)S(1)}, f32[3,16,128]{2,1,0:T(8,128)S(1)}, f32[3,16,128]{2,1,0:T(8,128)S(1)}, f3...) custom-call(f32[17,3,3,16,128]{4,3,2,1,0:T(8,128)S(1)} %get-tuple-element.27.factor, ...), custom_call_target="tpu_custom_call" | custom-call | tf_op jit(solution)/shard_map/first_half/pallas_call | solution.py:475
  23.9 1.3 %collective-permute-start.6 = (f32[1,16,128]{2,1,0:T(8,128)S(1)}, f32[1,16,128]{2,1,0:T(8,128)S(1)}, u32[]{:S(2)}, u32[]{:S(2)}) collective-permute-start(f32[1,16,128]{2,1,0:T(8,128)S(1)} %get-tuple-element.45), channel_id=1, source_target_pairs={{1,0},{2,1},{3,2},{4,3},{5,4},{6,5},{7,6},{8,7},{9,8},{10,9},{11,1... | collective-permute-start | bytes 24584 | tf_op jit(solution)/shard_map/ppermute | solution.py:427
  25.2 4.7 %collective-permute-start.7 = (f32[1,16,128]{2,1,0:T(8,128)S(1)}, f32[1,16,128]{2,1,0:T(8,128)S(1)}, u32[]{:S(2)}, u32[]{:S(2)}) collective-permute-start(f32[1,16,128]{2,1,0:T(8,128)S(1)} %get-tuple-element.46), channel_id=1, source_target_pairs={{0,1},{1,2},{2,3},{3,4},{4,5},{5,6},{6,7},{7,8},{8,9},{9,10},{10,1... | collective-permute-start | bytes 24584 | tf_op jit(solution)/shard_map/ppermute | solution.py:427
  29.9 0.0 collective-permute-done.6.right.field_right
  29.9 0.8 collective-permute-done.7.left.field_left
  30.7 4.9 %collective-permute-start.8 = (f32[3,8,128]{2,1,0:T(8,128)S(1)}, f32[3,8,128]{2,1,0:T(8,128)S(1)}, u32[]{:S(2)}, u32[]{:S(2)}) collective-permute-start(f32[3,8,128]{2,1,0:T(8,128)S(1)} %get-tuple-element.47), channel_id=1, source_target_pairs={{16,0},{32,16},{48,32},{64,48},{80,64},{96,80},{112,96},{128,112},... | collective-permute-start | bytes 36872 | tf_op jit(solution)/shard_map/ppermute | solution.py:427
  35.6 0.0 collective-permute-start.9
  35.6 0.8 %collective-permute-done.8.field_down = f32[3,8,128]{2,1,0:T(8,128)S(1)} collective-permute-done((f32[3,8,128]{2,1,0:T(8,128)S(1)}, f32[3,8,128]{2,1,0:T(8,128)S(1)}, u32[]{:S(2)}, u32[]{:S(2)}) %collective-permute-start.8) | collective-permute-done | bytes 12320 | tf_op jit(solution)/shard_map/ppermute | solution.py:427
  36.4 1.9 %collective-permute-done.9.field_up = f32[3,8,128]{2,1,0:T(8,128)S(1)} collective-permute-done((f32[3,8,128]{2,1,0:T(8,128)S(1)}, f32[3,8,128]{2,1,0:T(8,128)S(1)}, u32[]{:S(2)}, u32[]{:S(2)}) %collective-permute-start.9) | collective-permute-done | bytes 12320 | tf_op jit(solution)/shard_map/ppermute | solution.py:427
  38.4 1.3 %second_half.1 = (f32[3,16,128]{2,1,0:T(8,128)S(1)}, f32[3,16,128]{2,1,0:T(8,128)S(1)}, f32[32,1,128]{2,1,0:T(1,128)S(1)}) custom-call(f32[17,3,3,16,128]{4,3,2,1,0:T(8,128)S(1)} %get-tuple-element.27.factor, f32[153,8,128]{2,1,0:T(8,128)S(1)} %get-tuple-element.37.edge, f32[153,16,128]{2,1,0:T(8,128)S(1)} %get-tuple-element.38.side, ...), custom_call_target="tpu_custom_call" | custom-call | tf_op jit(solution)/shard_map/second_half/pallas_call | solution.py:481
  39.7 23.4 %all_to_all.10 = f32[32,1,128]{2,1,0:T(1,128)S(1)} all-to-all(f32[32,1,128]{2,1,0:T(1,128)S(1)} %get-tuple-element.49), channel_id=1, replica_groups=mesh['gx'=32,'gy'=16] {'gx'}, dimensions={0} | all-to-all | bytes 32768 | tf_op jit(solution)/shard_map/all_to_all | solution.py:431
  63.1 0.1 reduce_sum.20
  63.2 17.5 %all_to_all.11 = f32[16,1,128]{2,1,0:T(1,128)S(1)} all-to-all(f32[16,1,128]{2,1,0:T(1,128)S(1)} %broadcast_in_dim.2), channel_id=1, replica_groups=mesh['gx'=32,'gy'=16] {'gy'}, dimensions={0} | all-to-all | bytes 16384 | tf_op jit(solution)/shard_map/all_to_all | solution.py:431
  80.7 0.7 finish.1
  (4 shorter events, 0.1 us)
Async XLA Ops:
  0.6 1.8 %copy-start.1 = (f32[3,16,128]{2,1,0:T(8,128)S(1)}, f32[3,16,128]{2,1,0:T(8,128)}, u32[]{:S(2)}) copy-start(f32[3,16,128]{2,1,0:T(8,128)} %field.1) | copy-start | bytes 73732
  0.6 14.1 %copy-start = (s32[32,16,128]{2,1,0:T(8,128)S(1)}, s32[32,16,128]{2,1,0:T(8,128)}, u32[]{:S(2)}) copy-start(s32[32,16,128]{2,1,0:T(8,128)} %intact_hbm.1) | copy-start | bytes 786436
  2.6 18.9 %collective-permute-start.2 = (f32[79,8,128]{2,1,0:T(8,128)S(1)}, f32[79,8,128]{2,1,0:T(8,128)S(1)}, u32[]{:S(2)}, u32[]{:S(2)}) collective-permute-start(f32[79,8,128]{2,1,0:T(8,128)S(1)} %get-tuple-element.34), channel_id=1, source_target_pairs={{16,0},{32,16},{48,32},{64,48},{80,64},{96,80},{112,96},{128,112},... | collective-permute-start | bytes 970760 | tf_op jit(solution)/shard_map/ppermute | solution.py:427
  9.5 12.1 %collective-permute-start.3 = (f32[79,8,128]{2,1,0:T(8,128)S(1)}, f32[79,8,128]{2,1,0:T(8,128)S(1)}, u32[]{:S(2)}, u32[]{:S(2)}) collective-permute-start(f32[79,8,128]{2,1,0:T(8,128)S(1)} %get-tuple-element.35), channel_id=1, source_target_pairs={{0,16},{16,32},{32,48},{48,64},{64,80},{80,96},{96,112},{112,128},... | collective-permute-start | bytes 970760 | tf_op jit(solution)/shard_map/ppermute | solution.py:427
  9.5 7.2 %collective-permute-start = (f32[17,16,128]{2,1,0:T(8,128)S(1)}, f32[17,16,128]{2,1,0:T(8,128)S(1)}, u32[]{:S(2)}, u32[]{:S(2)}) collective-permute-start(f32[17,16,128]{2,1,0:T(8,128)S(1)} %get-tuple-element.32), channel_id=1, source_target_pairs={{1,0},{2,1},{3,2},{4,3},{5,4},{6,5},{7,6},{8,7},{9,8},{10,9},{11,1... | collective-permute-start | bytes 417800 | tf_op jit(solution)/shard_map/ppermute | solution.py:427
  10.8 6.0 %collective-permute-start.1 = (f32[17,16,128]{2,1,0:T(8,128)S(1)}, f32[17,16,128]{2,1,0:T(8,128)S(1)}, u32[]{:S(2)}, u32[]{:S(2)}) collective-permute-start(f32[17,16,128]{2,1,0:T(8,128)S(1)} %get-tuple-element.33), channel_id=1, source_target_pairs={{0,1},{1,2},{2,3},{3,4},{4,5},{5,6},{6,7},{7,8},{8,9},{9,10},{10,1... | collective-permute-start | bytes 417800 | tf_op jit(solution)/shard_map/ppermute | solution.py:427
  16.8 5.5 %collective-permute-start.5 = (f32[17,8,128]{2,1,0:T(8,128)S(1)}, f32[17,8,128]{2,1,0:T(8,128)S(1)}, u32[]{:S(2)}, u32[]{:S(2)}) collective-permute-start(f32[17,8,128]{2,1,0:T(8,128)S(1)} %get-tuple-element.40), channel_id=1, source_target_pairs={{0,16},{16,32},{32,48},{48,64},{64,80},{80,96},{96,112},{112,128},... | collective-permute-start | bytes 208904 | tf_op jit(solution)/shard_map/ppermute | solution.py:427
  16.8 5.6 %collective-permute-start.4 = (f32[17,8,128]{2,1,0:T(8,128)S(1)}, f32[17,8,128]{2,1,0:T(8,128)S(1)}, u32[]{:S(2)}, u32[]{:S(2)}) collective-permute-start(f32[17,8,128]{2,1,0:T(8,128)S(1)} %get-tuple-element.36.corner_down), channel_id=1, source_target_pairs={{16,0},{32,16},{48,32},{64,48},{80,64},{96,80},{112,96},{128,112},... | collective-permute-start | bytes 208904 | tf_op jit(solution)/shard_map/ppermute | solution.py:427
  23.9 6.0 %collective-permute-start.6 = (f32[1,16,128]{2,1,0:T(8,128)S(1)}, f32[1,16,128]{2,1,0:T(8,128)S(1)}, u32[]{:S(2)}, u32[]{:S(2)}) collective-permute-start(f32[1,16,128]{2,1,0:T(8,128)S(1)} %get-tuple-element.45), channel_id=1, source_target_pairs={{1,0},{2,1},{3,2},{4,3},{5,4},{6,5},{7,6},{8,7},{9,8},{10,9},{11,1... | collective-permute-start | bytes 24584 | tf_op jit(solution)/shard_map/ppermute | solution.py:427
  25.2 5.5 %collective-permute-start.7 = (f32[1,16,128]{2,1,0:T(8,128)S(1)}, f32[1,16,128]{2,1,0:T(8,128)S(1)}, u32[]{:S(2)}, u32[]{:S(2)}) collective-permute-start(f32[1,16,128]{2,1,0:T(8,128)S(1)} %get-tuple-element.46), channel_id=1, source_target_pairs={{0,1},{1,2},{2,3},{3,4},{4,5},{5,6},{6,7},{7,8},{8,9},{9,10},{10,1... | collective-permute-start | bytes 24584 | tf_op jit(solution)/shard_map/ppermute | solution.py:427
  30.7 5.7 %collective-permute-start.8 = (f32[3,8,128]{2,1,0:T(8,128)S(1)}, f32[3,8,128]{2,1,0:T(8,128)S(1)}, u32[]{:S(2)}, u32[]{:S(2)}) collective-permute-start(f32[3,8,128]{2,1,0:T(8,128)S(1)} %get-tuple-element.47), channel_id=1, source_target_pairs={{16,0},{32,16},{48,32},{64,48},{80,64},{96,80},{112,96},{128,112},... | collective-permute-start | bytes 36872 | tf_op jit(solution)/shard_map/ppermute | solution.py:427
  35.6 2.8 %collective-permute-start.9 = (f32[3,8,128]{2,1,0:T(8,128)S(1)}, f32[3,8,128]{2,1,0:T(8,128)S(1)}, u32[]{:S(2)}, u32[]{:S(2)}) collective-permute-start(f32[3,8,128]{2,1,0:T(8,128)S(1)} %get-tuple-element.48), channel_id=1, source_target_pairs={{0,16},{16,32},{32,48},{48,64},{64,80},{80,96},{96,112},{112,128},... | collective-permute-start | bytes 36872 | tf_op jit(solution)/shard_map/ppermute | solution.py:427

commit v7 on v6

--- a/solution.py
+++ b/solution.py
@@ -6,6 +6,7 @@
 from jax.sharding import PartitionSpec as P
 
 NZ = 4
+GX = ("chip", "core")
 ROWS = 16
 LANES = 128
 LOWER = 17
@@ -14,6 +15,7 @@
 CENTRE = 0.8
 VMEM_LIMIT = 24 * 1024 * 1024
 WIDE_LIMIT = 51 * 1024 * 1024
+PACK_LIMIT = 52 * 1024 * 1024 - 384 * 1024
 
 
 def bond_offsets():
@@ -120,14 +122,14 @@
 CHUNKS = ((0, 6), (6, 11), (11, LOWER))
 
 
-def pack_factor(factor_hbm, factor, to_left, to_right, down, up, sems):
+def pack_factor(factor_hbm, factor, to_left, to_right, sems):
     copies = []
     for k, (low, high) in enumerate(CHUNKS):
         part = pl.ds(low, high - low)
         copies.append(pltpu.make_async_copy(factor_hbm.at[part], factor.at[part], sems.at[k]))
     for copy in copies:
         copy.start()
-    group = tile = 0
+    group = 0
     for k, (low, high) in enumerate(CHUNKS):
         copies[k].wait()
         ready = 9 * high
@@ -137,19 +139,22 @@
                 break
             to_left[group], to_right[group] = pack_lanes([carried(factor, p) for p in members], 16)
             group += 1
-        while tile < OWN_TILES - 2 and min(2 * tile + 2, PLANES) <= ready:
-            down[tile], up[tile] = pack_rows(factor[entry(2 * tile)], factor[entry(min(2 * tile + 1, PLANES - 1))])
-            tile += 1
-
-
-def pack_right_side(field, left_in, right_in, down_in, up_in, kept, to_left, to_right, down, up):
+
+
+def pack_right_side(field, left_in, right_in, kept, to_left, to_right):
     kept[...] = field[...]
-    for held, packed in ((left_in, to_left), (right_in, to_right), (down_in, down), (up_in, up)):
-        packed[...] = held[...]
+    to_left[...] = left_in[...]
+    to_right[...] = right_in[...]
     last, lane = GROUPS - 1, iota(ROWS, 1)
     low, high = pack_lanes([field[k] for k in range(3)], 32, 1)
     to_left[last] = jnp.where(lane < 32, left_in[last], low)
     to_right[last] = jnp.where(lane >= 96, right_in[last], high)
+
+
+def pack_own(factor, field, down, up):
+    for tile in range(OWN_TILES - 2):
+        first, second = 2 * tile, min(2 * tile + 1, PLANES - 1)
+        down[tile], up[tile] = pack_rows(factor[entry(first)], factor[entry(second)])
     down[OWN_TILES - 2], up[OWN_TILES - 2] = pack_rows(field[0], field[1])
     down[OWN_TILES - 1], up[OWN_TILES - 1] = pack_rows(field[2], field[2])
 
@@ -308,7 +313,7 @@
 
 def outside():
     ends = []
-    for axis in ("gx", "gy"):
+    for axis in (GX, "gy"):
         place = lax.axis_index(axis)
         ends += [(place == 0).astype(jnp.int32), (place == lax.axis_size(axis) - 1).astype(jnp.int32)]
     sub = iota(8, 0)
@@ -432,7 +437,7 @@
 
 
 def local(right_side, stiffness, factor, intact):
-    nx, ny = lax.axis_size("gx"), lax.axis_size("gy")
+    nx, ny = lax.axis_size(GX), lax.axis_size("gy")
     plane = shape(3, ROWS, LANES)
     strip = shape(GROUPS, ROWS, LANES)
     own = shape(OWN_TILES, 8, LANES)
@@ -445,16 +450,22 @@
 
     factor, *packs = call(
         pack_factor,
-        [shape(*factor.shape), strip, strip, own, own],
+        [shape(*factor.shape), strip, strip],
         [hbm],
         [pltpu.SemaphoreType.DMA((len(CHUNKS),))],
-        limit=WIDE_LIMIT,
+        limit=PACK_LIMIT,
     )(factor)
-    field, to_left, to_right, down, up = call(
-        pack_right_side, [plane, strip, strip, own, own], [vmem] * 5, aliases={k: k for k in range(1, 5)}
+    field, to_left, to_right = call(
+        pack_right_side, [plane, strip, strip], [vmem] * 3, aliases={1: 1, 2: 2}
     )(right_side, *packs)
     right, left = swap(to_left, to_right, "gy", False)
-    own_down, own_up = swap(down, up, "gx", True)
+    down, up = call(
+        pack_own,
+        [own] * 2,
+        [vmem] * 2,
+        cost=pl.CostEstimate(flops=4 * factor.size, bytes_accessed=8 * factor.size, transcendentals=0),
+    )(factor, field)
+    own_down, own_up = swap(down, up, GX, True)
     (weighted,) = call(
         weigh,
         [shape(*stiffness.shape)],
@@ -470,29 +481,31 @@
         [vmem] * 5,
         cost=pl.CostEstimate(flops=4 * factor.size, bytes_accessed=8 * factor.size, transcendentals=0),
     )(right, left, own_down, own_up, down)
-    corner_down, corner_up = swap(down, up, "gx", True)
+    corner_down, corner_up = swap(down, up, GX, True)
 
     corner, g, z, w, to_left, to_right = call(
         first_half, [tiles, plane, plane, plane, small, small], [vmem] * 11, [wide]
     )(factor, edge, side, weighted, field, right, left, own_down, own_up, corner_down, corner_up)
     field_right, field_left = swap(to_left, to_right, "gy", False)
     down, up = call(pack_field, [edges] * 2, [vmem] * 3)(w, field_right, field_left)
-    field_down, field_up = swap(down, up, "gx", True)
-    u, au, sums = call(second_half, [plane, plane, shape(nx, 1, LANES)], [vmem] * 12, [wide])(
+    field_down, field_up = swap(down, up, GX, True)
+    u, au, sums = call(second_half, [plane, plane, shape(2 * ny, 1, LANES)], [vmem] * 12, [wide])(
         factor, edge, side, weighted, corner, g, z, w, field_right, field_left, field_down, field_up
     )
-    sums = gathered_sum(sums, "gx")
-    sums = gathered_sum(jnp.broadcast_to(sums[None], (ny, 1, LANES)), "gy")
+    sums = gathered_sum(sums, ("core", "gy"))
+    sums = gathered_sum(jnp.broadcast_to(sums[None], (nx // 2, 1, LANES)), "chip")
     x, r = call(finish, [plane] * 2, [vmem] * 6)(sums, field, z, w, u, au)
     return x, r
 
 
 def solution(mesh):
+    nx, ny = mesh.devices.shape
+    mesh = jax.sharding.Mesh(mesh.devices.reshape(nx // 2, 2, ny), ("chip", "core", "gy"))
     in_specs = (
-        P(None, "gx", "gy"),
-        P(None, None, None, "gx", "gy"),
-        P(None, None, None, "gx", "gy"),
-        P(None, "gx", "gy"),
+        P(None, GX, "gy"),
+        P(None, None, None, GX, "gy"),
+        P(None, None, None, GX, "gy"),
+        P(None, GX, "gy"),
     )
-    out_specs = (P(None, "gx", "gy"), P(None, "gx", "gy"))
+    out_specs = (P(None, GX, "gy"), P(None, GX, "gy"))
     return jax.shard_map(local, mesh=mesh, in_specs=in_specs, out_specs=out_specs, check_vma=False)

time: 81.7 us -> 81.6 us (level)
    pallas_call x3 -> x4, Pallas kernels: 3.27 us -> 3.21 us  [the longest x1 1.73 us: local(): call(pack_factor, [shape(*factor.shape), strip, strip], [hbm], [pltpu.Sem...]
where the time goes in v7:
time: 81.6 us; the launch traced here: 81.3 us
  blocking collectives  40.9 us (50%)
  starting transfers between devices  27.8 us (34%)
  Pallas kernels  7.8 us (10%)
  waiting for transfers between devices  4.06 us (5%)
    all_to_all x2, blocking collectives, gathered_sum(): return jnp.sum(lax.all_to_all(rows, axis, 0, 0), axis=0)  40.9 us
    ppermute x10, starting transfers between devices, swap(): return (lax.ppermute(first, axis, back), lax.ppermute(second, axis, ahead))  27.8 us
    ppermute x10, waiting for transfers between devices, swap(): return (lax.ppermute(first, axis, back), lax.ppermute(second, axis, ahead))  4.06 us
    pallas_call x1, Pallas kernels, local(): call(weigh, [shape(*stiffness.shape)], [hbm] * 2, [pltpu.VMEM(intact.shap...  1.89 us
    pallas_call x1, Pallas kernels, local(): call(pack_factor, [shape(*factor.shape), strip, strip], [hbm], [pltpu.Sem...  1.73 us
  transfers between devices with their start and end apart: 10, of which 6 were waited for; matrix products, arithmetic and copies ran while one was open for 0% of the time, Pallas kernels for 3%

profile of v7, /device:TPU:1, one launch (start us, length us, event | category | flops | bytes accessed | tf_op | source)
XLA Modules:
  0.0 81.3 jit_solution(10500954722699747072)
XLA Ops:
  0.6 0.0 copy-start.1
  0.6 0.0 copy-start
  0.6 1.7 %pack_factor.1 = (f32[17,3,3,16,128]{4,3,2,1,0:T(8,128)S(1)}, f32[17,16,128]{2,1,0:T(8,128)S(1)}, f32[17,16,128]{2,1,0:T(8,128)S(1)}) custom-call(f32[17,3,3,16,128]{4,3,2,1,0:T(8,128)} %factor_hbm.1), custom_call_target="tpu_custom_call" | custom-call | tf_op jit(solution)/shard_map/pack_factor/pallas_call | solution.py:451
  2.4 0.0 copy-done.1
  2.4 0.1 pack_right_side.1
  2.5 0.1 pack_own.1
  2.5 6.9 %collective-permute-start.2 = (f32[79,8,128]{2,1,0:T(8,128)S(1)}, f32[79,8,128]{2,1,0:T(8,128)S(1)}, u32[]{:S(2)}, u32[]{:S(2)}) collective-permute-start(f32[79,8,128]{2,1,0:T(8,128)S(1)} %get-tuple-element.31), channel_id=1, source_target_pairs={{16,0},{32,16},{48,32},{64,48},{80,64},{96,80},{112,96},{128,112},... | collective-permute-start | bytes 970760 | tf_op jit(solution)/shard_map/ppermute | solution.py:432
  9.4 0.0 collective-permute-start.3
  9.4 1.3 %collective-permute-start = (f32[17,16,128]{2,1,0:T(8,128)S(1)}, f32[17,16,128]{2,1,0:T(8,128)S(1)}, u32[]{:S(2)}, u32[]{:S(2)}) collective-permute-start(f32[17,16,128]{2,1,0:T(8,128)S(1)} %get-tuple-element.28), channel_id=1, source_target_pairs={{1,0},{2,1},{3,2},{4,3},{5,4},{6,5},{7,6},{8,7},{9,8},{10,9},{11,1... | collective-permute-start | bytes 417800 | tf_op jit(solution)/shard_map/ppermute | solution.py:432
  10.7 4.0 %collective-permute-start.1 = (f32[17,16,128]{2,1,0:T(8,128)S(1)}, f32[17,16,128]{2,1,0:T(8,128)S(1)}, u32[]{:S(2)}, u32[]{:S(2)}) collective-permute-start(f32[17,16,128]{2,1,0:T(8,128)S(1)} %get-tuple-element.29), channel_id=1, source_target_pairs={{0,1},{1,2},{2,3},{3,4},{4,5},{5,6},{6,7},{7,8},{8,9},{9,10},{10,1... | collective-permute-start | bytes 417800 | tf_op jit(solution)/shard_map/ppermute | solution.py:432
  14.7 0.0 copy-done
  14.7 1.9 %weigh.1.weighted = f32[33,3,3,16,128]{4,3,2,1,0:T(8,128)S(1)} custom-call(f32[33,3,3,16,128]{4,3,2,1,0:T(8,128)} %stiffness_hbm.1, s32[32,16,128]{2,1,0:T(8,128)S(1)} %copy-done), custom_call_target="tpu_custom_call" | custom-call | flops 608256 | bytes 4866048 | tf_op jit(solution)/shard_map/weigh/pallas_call | solution.py:469
  16.6 0.0 collective-permute-done.right
  16.6 0.1 collective-permute-done.1.left
  16.8 0.0 collective-permute-start.5
  16.8 4.7 %collective-permute-start.4 = (f32[17,8,128]{2,1,0:T(8,128)S(1)}, f32[17,8,128]{2,1,0:T(8,128)S(1)}, u32[]{:S(2)}, u32[]{:S(2)}) collective-permute-start(f32[17,8,128]{2,1,0:T(8,128)S(1)} %get-tuple-element.33.corner_down), channel_id=1, source_target_pairs={{16,0},{32,16},{48,32},{64,48},{80,64},{96,80},{112,96},{128,112},... | collective-permute-start | bytes 208904 | tf_op jit(solution)/shard_map/ppermute | solution.py:432
  21.5 0.0 collective-permute-done.2.own_down
  21.5 0.0 collective-permute-done.3.own_up
  21.5 0.5 unpack_sides.1
  22.0 0.3 collective-permute-done.5.corner_up
  22.2 0.2 collective-permute-done.4.corner_down
  22.4 1.5 %first_half.1 = (f32[153,8,128]{2,1,0:T(8,128)S(1)}, f32[3,16,128]{2,1,0:T(8,128)S(1)}, f32[3,16,128]{2,1,0:T(8,128)S(1)}, f32[3,16,128]{2,1,0:T(8,128)S(1)}, f3...) custom-call(f32[17,3,3,16,128]{4,3,2,1,0:T(8,128)S(1)} %get-tuple-element.25.factor, ...), custom_call_target="tpu_custom_call" | custom-call | tf_op jit(solution)/shard_map/first_half/pallas_call | solution.py:486
  23.9 1.3 %collective-permute-start.6 = (f32[1,16,128]{2,1,0:T(8,128)S(1)}, f32[1,16,128]{2,1,0:T(8,128)S(1)}, u32[]{:S(2)}, u32[]{:S(2)}) collective-permute-start(f32[1,16,128]{2,1,0:T(8,128)S(1)} %get-tuple-element.41), channel_id=1, source_target_pairs={{1,0},{2,1},{3,2},{4,3},{5,4},{6,5},{7,6},{8,7},{9,8},{10,9},{11,1... | collective-permute-start | bytes 24584 | tf_op jit(solution)/shard_map/ppermute | solution.py:432
  25.2 4.7 %collective-permute-start.7 = (f32[1,16,128]{2,1,0:T(8,128)S(1)}, f32[1,16,128]{2,1,0:T(8,128)S(1)}, u32[]{:S(2)}, u32[]{:S(2)}) collective-permute-start(f32[1,16,128]{2,1,0:T(8,128)S(1)} %get-tuple-element.42), channel_id=1, source_target_pairs={{0,1},{1,2},{2,3},{3,4},{4,5},{5,6},{6,7},{7,8},{8,9},{9,10},{10,1... | collective-permute-start | bytes 24584 | tf_op jit(solution)/shard_map/ppermute | solution.py:432
  29.9 0.0 collective-permute-done.6.right.field_right
  29.9 0.8 collective-permute-done.7.left.field_left
  30.7 4.9 %collective-permute-start.8 = (f32[3,8,128]{2,1,0:T(8,128)S(1)}, f32[3,8,128]{2,1,0:T(8,128)S(1)}, u32[]{:S(2)}, u32[]{:S(2)}) collective-permute-start(f32[3,8,128]{2,1,0:T(8,128)S(1)} %get-tuple-element.43), channel_id=1, source_target_pairs={{16,0},{32,16},{48,32},{64,48},{80,64},{96,80},{112,96},{128,112},... | collective-permute-start | bytes 36872 | tf_op jit(solution)/shard_map/ppermute | solution.py:432
  35.5 0.0 collective-permute-start.9
  35.5 0.8 %collective-permute-done.8.field_down = f32[3,8,128]{2,1,0:T(8,128)S(1)} collective-permute-done((f32[3,8,128]{2,1,0:T(8,128)S(1)}, f32[3,8,128]{2,1,0:T(8,128)S(1)}, u32[]{:S(2)}, u32[]{:S(2)}) %collective-permute-start.8) | collective-permute-done | bytes 12320 | tf_op jit(solution)/shard_map/ppermute | solution.py:432
  36.4 1.9 %collective-permute-done.9.field_up = f32[3,8,128]{2,1,0:T(8,128)S(1)} collective-permute-done((f32[3,8,128]{2,1,0:T(8,128)S(1)}, f32[3,8,128]{2,1,0:T(8,128)S(1)}, u32[]{:S(2)}, u32[]{:S(2)}) %collective-permute-start.9) | collective-permute-done | bytes 12320 | tf_op jit(solution)/shard_map/ppermute | solution.py:432
  38.3 1.3 %second_half.1 = (f32[3,16,128]{2,1,0:T(8,128)S(1)}, f32[3,16,128]{2,1,0:T(8,128)S(1)}, f32[32,1,128]{2,1,0:T(1,128)S(1)}) custom-call(f32[17,3,3,16,128]{4,3,2,1,0:T(8,128)S(1)} %get-tuple-element.25.factor, f32[153,8,128]{2,1,0:T(8,128)S(1)} %get-tuple-element.34.edge, f32[153,16,128]{2,1,0:T(8,128)S(1)} %get-tuple-element.35.side, ...), custom_call_target="tpu_custom_call" | custom-call | tf_op jit(solution)/shard_map/second_half/pallas_call | solution.py:492
  39.7 22.0 %all_to_all.10 = f32[32,1,128]{2,1,0:T(1,128)S(1)} all-to-all(f32[32,1,128]{2,1,0:T(1,128)S(1)} %get-tuple-element.45), channel_id=1, replica_groups=mesh['chip'=16,'core'=2,'gy'=16] {'core','gy'}, dimensions={0} | all-to-all | bytes 32768 | tf_op jit(solution)/shard_map/all_to_all | solution.py:436
  61.6 0.1 reduce_sum.20
  61.7 18.9 %all_to_all.11 = f32[16,1,128]{2,1,0:T(1,128)S(1)} all-to-all(f32[16,1,128]{2,1,0:T(1,128)S(1)} %broadcast_in_dim.2), channel_id=1, replica_groups=mesh['chip'=16,'core'=2,'gy'=16] {'chip'}, dimensions={0} | all-to-all | bytes 16384 | tf_op jit(solution)/shard_map/all_to_all | solution.py:436
  80.6 0.7 finish.1
  (4 shorter events, 0.1 us)
Async XLA Ops:
  0.6 1.8 %copy-start.1 = (f32[3,16,128]{2,1,0:T(8,128)S(1)}, f32[3,16,128]{2,1,0:T(8,128)}, u32[]{:S(2)}) copy-start(f32[3,16,128]{2,1,0:T(8,128)} %field.1) | copy-start | bytes 73732
  0.6 14.1 %copy-start = (s32[32,16,128]{2,1,0:T(8,128)S(1)}, s32[32,16,128]{2,1,0:T(8,128)}, u32[]{:S(2)}) copy-start(s32[32,16,128]{2,1,0:T(8,128)} %intact_hbm.1) | copy-start | bytes 786436
  2.5 18.9 %collective-permute-start.2 = (f32[79,8,128]{2,1,0:T(8,128)S(1)}, f32[79,8,128]{2,1,0:T(8,128)S(1)}, u32[]{:S(2)}, u32[]{:S(2)}) collective-permute-start(f32[79,8,128]{2,1,0:T(8,128)S(1)} %get-tuple-element.31), channel_id=1, source_target_pairs={{16,0},{32,16},{48,32},{64,48},{80,64},{96,80},{112,96},{128,112},... | collective-permute-start | bytes 970760 | tf_op jit(solution)/shard_map/ppermute | solution.py:432
  9.4 12.1 %collective-permute-start.3 = (f32[79,8,128]{2,1,0:T(8,128)S(1)}, f32[79,8,128]{2,1,0:T(8,128)S(1)}, u32[]{:S(2)}, u32[]{:S(2)}) collective-permute-start(f32[79,8,128]{2,1,0:T(8,128)S(1)} %get-tuple-element.32), channel_id=1, source_target_pairs={{0,16},{16,32},{32,48},{48,64},{64,80},{80,96},{96,112},{112,128},... | collective-permute-start | bytes 970760 | tf_op jit(solution)/shard_map/ppermute | solution.py:432
  9.4 7.2 %collective-permute-start = (f32[17,16,128]{2,1,0:T(8,128)S(1)}, f32[17,16,128]{2,1,0:T(8,128)S(1)}, u32[]{:S(2)}, u32[]{:S(2)}) collective-permute-start(f32[17,16,128]{2,1,0:T(8,128)S(1)} %get-tuple-element.28), channel_id=1, source_target_pairs={{1,0},{2,1},{3,2},{4,3},{5,4},{6,5},{7,6},{8,7},{9,8},{10,9},{11,1... | collective-permute-start | bytes 417800 | tf_op jit(solution)/shard_map/ppermute | solution.py:432
  10.7 6.0 %collective-permute-start.1 = (f32[17,16,128]{2,1,0:T(8,128)S(1)}, f32[17,16,128]{2,1,0:T(8,128)S(1)}, u32[]{:S(2)}, u32[]{:S(2)}) collective-permute-start(f32[17,16,128]{2,1,0:T(8,128)S(1)} %get-tuple-element.29), channel_id=1, source_target_pairs={{0,1},{1,2},{2,3},{3,4},{4,5},{5,6},{6,7},{7,8},{8,9},{9,10},{10,1... | collective-permute-start | bytes 417800 | tf_op jit(solution)/shard_map/ppermute | solution.py:432
  16.8 5.5 %collective-permute-start.5 = (f32[17,8,128]{2,1,0:T(8,128)S(1)}, f32[17,8,128]{2,1,0:T(8,128)S(1)}, u32[]{:S(2)}, u32[]{:S(2)}) collective-permute-start(f32[17,8,128]{2,1,0:T(8,128)S(1)} %get-tuple-element.36), channel_id=1, source_target_pairs={{0,16},{16,32},{32,48},{48,64},{64,80},{80,96},{96,112},{112,128},... | collective-permute-start | bytes 208904 | tf_op jit(solution)/shard_map/ppermute | solution.py:432
  16.8 5.6 %collective-permute-start.4 = (f32[17,8,128]{2,1,0:T(8,128)S(1)}, f32[17,8,128]{2,1,0:T(8,128)S(1)}, u32[]{:S(2)}, u32[]{:S(2)}) collective-permute-start(f32[17,8,128]{2,1,0:T(8,128)S(1)} %get-tuple-element.33.corner_down), channel_id=1, source_target_pairs={{16,0},{32,16},{48,32},{64,48},{80,64},{96,80},{112,96},{128,112},... | collective-permute-start | bytes 208904 | tf_op jit(solution)/shard_map/ppermute | solution.py:432
  23.9 6.0 %collective-permute-start.6 = (f32[1,16,128]{2,1,0:T(8,128)S(1)}, f32[1,16,128]{2,1,0:T(8,128)S(1)}, u32[]{:S(2)}, u32[]{:S(2)}) collective-permute-start(f32[1,16,128]{2,1,0:T(8,128)S(1)} %get-tuple-element.41), channel_id=1, source_target_pairs={{1,0},{2,1},{3,2},{4,3},{5,4},{6,5},{7,6},{8,7},{9,8},{10,9},{11,1... | collective-permute-start | bytes 24584 | tf_op jit(solution)/shard_map/ppermute | solution.py:432
  25.2 5.5 %collective-permute-start.7 = (f32[1,16,128]{2,1,0:T(8,128)S(1)}, f32[1,16,128]{2,1,0:T(8,128)S(1)}, u32[]{:S(2)}, u32[]{:S(2)}) collective-permute-start(f32[1,16,128]{2,1,0:T(8,128)S(1)} %get-tuple-element.42), channel_id=1, source_target_pairs={{0,1},{1,2},{2,3},{3,4},{4,5},{5,6},{6,7},{7,8},{8,9},{9,10},{10,1... | collective-permute-start | bytes 24584 | tf_op jit(solution)/shard_map/ppermute | solution.py:432
  30.7 5.7 %collective-permute-start.8 = (f32[3,8,128]{2,1,0:T(8,128)S(1)}, f32[3,8,128]{2,1,0:T(8,128)S(1)}, u32[]{:S(2)}, u32[]{:S(2)}) collective-permute-start(f32[3,8,128]{2,1,0:T(8,128)S(1)} %get-tuple-element.43), channel_id=1, source_target_pairs={{16,0},{32,16},{48,32},{64,48},{80,64},{96,80},{112,96},{128,112},... | collective-permute-start | bytes 36872 | tf_op jit(solution)/shard_map/ppermute | solution.py:432
  35.5 2.8 %collective-permute-start.9 = (f32[3,8,128]{2,1,0:T(8,128)S(1)}, f32[3,8,128]{2,1,0:T(8,128)S(1)}, u32[]{:S(2)}, u32[]{:S(2)}) collective-permute-start(f32[3,8,128]{2,1,0:T(8,128)S(1)} %get-tuple-element.44), channel_id=1, source_target_pairs={{0,16},{16,32},{32,48},{48,64},{64,80},{80,96},{96,112},{112,128},... | collective-permute-start | bytes 36872 | tf_op jit(solution)/shard_map/ppermute | solution.py:432

commit v8 on v7

--- a/solution.py
+++ b/solution.py
@@ -119,7 +119,7 @@
     return jnp.where(upper, down, up), pltpu.roll(jnp.where(upper, up, down), 4, 0)
 
 
-CHUNKS = ((0, 6), (6, 11), (11, LOWER))
+CHUNKS = ((0, 8), (8, 13), (13, LOWER))
 
 
 def pack_factor(factor_hbm, factor, to_left, to_right, sems):

time: 81.6 us -> 81.8 us (level)
  no operation moved by 1% of the time
where the time goes in v8:
time: 81.8 us; the launch traced here: 81.5 us
  blocking collectives  40.9 us (50%)
  starting transfers between devices  27.8 us (34%)
  Pallas kernels  7.95 us (10%)
  waiting for transfers between devices  4.06 us (5%)
    all_to_all x2, blocking collectives, gathered_sum(): return jnp.sum(lax.all_to_all(rows, axis, 0, 0), axis=0)  40.9 us
    ppermute x10, starting transfers between devices, swap(): return (lax.ppermute(first, axis, back), lax.ppermute(second, axis, ahead))  27.8 us
    ppermute x10, waiting for transfers between devices, swap(): return (lax.ppermute(first, axis, back), lax.ppermute(second, axis, ahead))  4.06 us
    pallas_call x1, Pallas kernels, local(): call(weigh, [shape(*stiffness.shape)], [hbm] * 2, [pltpu.VMEM(intact.shap...  1.89 us
    pallas_call x1, Pallas kernels, local(): call(pack_factor, [shape(*factor.shape), strip, strip], [hbm], [pltpu.Sem...  1.88 us
  transfers between devices with their start and end apart: 10, of which 6 were waited for; matrix products, arithmetic and copies ran while one was open for 0% of the time, Pallas kernels for 3%

profile of v8, /device:TPU:1, one launch (start us, length us, event | category | flops | bytes accessed | tf_op | source)
XLA Modules:
  0.0 81.5 jit_solution(16771045420759746024)
XLA Ops:
  0.6 0.0 copy-start.1
  0.6 0.0 copy-start
  0.6 1.9 %pack_factor.1 = (f32[17,3,3,16,128]{4,3,2,1,0:T(8,128)S(1)}, f32[17,16,128]{2,1,0:T(8,128)S(1)}, f32[17,16,128]{2,1,0:T(8,128)S(1)}) custom-call(f32[17,3,3,16,128]{4,3,2,1,0:T(8,128)} %factor_hbm.1), custom_call_target="tpu_custom_call" | custom-call | tf_op jit(solution)/shard_map/pack_factor/pallas_call | solution.py:451
  2.5 0.0 copy-done.1
  2.5 0.1 pack_right_side.1
  2.6 0.1 pack_own.1
  2.7 6.9 %collective-permute-start.2 = (f32[79,8,128]{2,1,0:T(8,128)S(1)}, f32[79,8,128]{2,1,0:T(8,128)S(1)}, u32[]{:S(2)}, u32[]{:S(2)}) collective-permute-start(f32[79,8,128]{2,1,0:T(8,128)S(1)} %get-tuple-element.31), channel_id=1, source_target_pairs={{16,0},{32,16},{48,32},{64,48},{80,64},{96,80},{112,96},{128,112},... | collective-permute-start | bytes 970760 | tf_op jit(solution)/shard_map/ppermute | solution.py:432
  9.6 0.0 collective-permute-start.3
  9.6 1.3 %collective-permute-start = (f32[17,16,128]{2,1,0:T(8,128)S(1)}, f32[17,16,128]{2,1,0:T(8,128)S(1)}, u32[]{:S(2)}, u32[]{:S(2)}) collective-permute-start(f32[17,16,128]{2,1,0:T(8,128)S(1)} %get-tuple-element.28), channel_id=1, source_target_pairs={{1,0},{2,1},{3,2},{4,3},{5,4},{6,5},{7,6},{8,7},{9,8},{10,9},{11,1... | collective-permute-start | bytes 417800 | tf_op jit(solution)/shard_map/ppermute | solution.py:432
  10.9 4.0 %collective-permute-start.1 = (f32[17,16,128]{2,1,0:T(8,128)S(1)}, f32[17,16,128]{2,1,0:T(8,128)S(1)}, u32[]{:S(2)}, u32[]{:S(2)}) collective-permute-start(f32[17,16,128]{2,1,0:T(8,128)S(1)} %get-tuple-element.29), channel_id=1, source_target_pairs={{0,1},{1,2},{2,3},{3,4},{4,5},{5,6},{6,7},{7,8},{8,9},{9,10},{10,1... | collective-permute-start | bytes 417800 | tf_op jit(solution)/shard_map/ppermute | solution.py:432
  14.9 0.0 copy-done
  14.9 1.9 %weigh.1.weighted = f32[33,3,3,16,128]{4,3,2,1,0:T(8,128)S(1)} custom-call(f32[33,3,3,16,128]{4,3,2,1,0:T(8,128)} %stiffness_hbm.1, s32[32,16,128]{2,1,0:T(8,128)S(1)} %copy-done), custom_call_target="tpu_custom_call" | custom-call | flops 608256 | bytes 4866048 | tf_op jit(solution)/shard_map/weigh/pallas_call | solution.py:469
  16.8 0.0 collective-permute-done.right
  16.8 0.1 collective-permute-done.1.left
  16.9 0.0 collective-permute-start.5
  16.9 4.7 %collective-permute-start.4 = (f32[17,8,128]{2,1,0:T(8,128)S(1)}, f32[17,8,128]{2,1,0:T(8,128)S(1)}, u32[]{:S(2)}, u32[]{:S(2)}) collective-permute-start(f32[17,8,128]{2,1,0:T(8,128)S(1)} %get-tuple-element.33.corner_down), channel_id=1, source_target_pairs={{16,0},{32,16},{48,32},{64,48},{80,64},{96,80},{112,96},{128,112},... | collective-permute-start | bytes 208904 | tf_op jit(solution)/shard_map/ppermute | solution.py:432
  21.6 0.0 collective-permute-done.2.own_down
  21.6 0.0 collective-permute-done.3.own_up
  21.6 0.5 unpack_sides.1
  22.1 0.3 collective-permute-done.5.corner_up
  22.4 0.2 collective-permute-done.4.corner_down
  22.5 1.5 %first_half.1 = (f32[153,8,128]{2,1,0:T(8,128)S(1)}, f32[3,16,128]{2,1,0:T(8,128)S(1)}, f32[3,16,128]{2,1,0:T(8,128)S(1)}, f32[3,16,128]{2,1,0:T(8,128)S(1)}, f3...) custom-call(f32[17,3,3,16,128]{4,3,2,1,0:T(8,128)S(1)} %get-tuple-element.25.factor, ...), custom_call_target="tpu_custom_call" | custom-call | tf_op jit(solution)/shard_map/first_half/pallas_call | solution.py:486
  24.0 1.3 %collective-permute-start.6 = (f32[1,16,128]{2,1,0:T(8,128)S(1)}, f32[1,16,128]{2,1,0:T(8,128)S(1)}, u32[]{:S(2)}, u32[]{:S(2)}) collective-permute-start(f32[1,16,128]{2,1,0:T(8,128)S(1)} %get-tuple-element.41), channel_id=1, source_target_pairs={{1,0},{2,1},{3,2},{4,3},{5,4},{6,5},{7,6},{8,7},{9,8},{10,9},{11,1... | collective-permute-start | bytes 24584 | tf_op jit(solution)/shard_map/ppermute | solution.py:432
  25.3 4.7 %collective-permute-start.7 = (f32[1,16,128]{2,1,0:T(8,128)S(1)}, f32[1,16,128]{2,1,0:T(8,128)S(1)}, u32[]{:S(2)}, u32[]{:S(2)}) collective-permute-start(f32[1,16,128]{2,1,0:T(8,128)S(1)} %get-tuple-element.42), channel_id=1, source_target_pairs={{0,1},{1,2},{2,3},{3,4},{4,5},{5,6},{6,7},{7,8},{8,9},{9,10},{10,1... | collective-permute-start | bytes 24584 | tf_op jit(solution)/shard_map/ppermute | solution.py:432
  30.0 0.0 collective-permute-done.6.right.field_right
  30.0 0.8 collective-permute-done.7.left.field_left
  30.8 4.9 %collective-permute-start.8 = (f32[3,8,128]{2,1,0:T(8,128)S(1)}, f32[3,8,128]{2,1,0:T(8,128)S(1)}, u32[]{:S(2)}, u32[]{:S(2)}) collective-permute-start(f32[3,8,128]{2,1,0:T(8,128)S(1)} %get-tuple-element.43), channel_id=1, source_target_pairs={{16,0},{32,16},{48,32},{64,48},{80,64},{96,80},{112,96},{128,112},... | collective-permute-start | bytes 36872 | tf_op jit(solution)/shard_map/ppermute | solution.py:432
  35.7 0.0 collective-permute-start.9
  35.7 0.8 %collective-permute-done.8.field_down = f32[3,8,128]{2,1,0:T(8,128)S(1)} collective-permute-done((f32[3,8,128]{2,1,0:T(8,128)S(1)}, f32[3,8,128]{2,1,0:T(8,128)S(1)}, u32[]{:S(2)}, u32[]{:S(2)}) %collective-permute-start.8) | collective-permute-done | bytes 12320 | tf_op jit(solution)/shard_map/ppermute | solution.py:432
  36.5 1.9 %collective-permute-done.9.field_up = f32[3,8,128]{2,1,0:T(8,128)S(1)} collective-permute-done((f32[3,8,128]{2,1,0:T(8,128)S(1)}, f32[3,8,128]{2,1,0:T(8,128)S(1)}, u32[]{:S(2)}, u32[]{:S(2)}) %collective-permute-start.9) | collective-permute-done | bytes 12320 | tf_op jit(solution)/shard_map/ppermute | solution.py:432
  38.5 1.3 %second_half.1 = (f32[3,16,128]{2,1,0:T(8,128)S(1)}, f32[3,16,128]{2,1,0:T(8,128)S(1)}, f32[32,1,128]{2,1,0:T(1,128)S(1)}) custom-call(f32[17,3,3,16,128]{4,3,2,1,0:T(8,128)S(1)} %get-tuple-element.25.factor, f32[153,8,128]{2,1,0:T(8,128)S(1)} %get-tuple-element.34.edge, f32[153,16,128]{2,1,0:T(8,128)S(1)} %get-tuple-element.35.side, ...), custom_call_target="tpu_custom_call" | custom-call | tf_op jit(solution)/shard_map/second_half/pallas_call | solution.py:492
  39.8 22.0 %all_to_all.10 = f32[32,1,128]{2,1,0:T(1,128)S(1)} all-to-all(f32[32,1,128]{2,1,0:T(1,128)S(1)} %get-tuple-element.45), channel_id=1, replica_groups=mesh['chip'=16,'core'=2,'gy'=16] {'core','gy'}, dimensions={0} | all-to-all | bytes 32768 | tf_op jit(solution)/shard_map/all_to_all | solution.py:436
  61.8 0.1 reduce_sum.20
  61.8 18.9 %all_to_all.11 = f32[16,1,128]{2,1,0:T(1,128)S(1)} all-to-all(f32[16,1,128]{2,1,0:T(1,128)S(1)} %broadcast_in_dim.2), channel_id=1, replica_groups=mesh['chip'=16,'core'=2,'gy'=16] {'chip'}, dimensions={0} | all-to-all | bytes 16384 | tf_op jit(solution)/shard_map/all_to_all | solution.py:436
  80.8 0.7 finish.1
  (4 shorter events, 0.1 us)
Async XLA Ops:
  0.6 1.9 %copy-start.1 = (f32[3,16,128]{2,1,0:T(8,128)S(1)}, f32[3,16,128]{2,1,0:T(8,128)}, u32[]{:S(2)}) copy-start(f32[3,16,128]{2,1,0:T(8,128)} %field.1) | copy-start | bytes 73732
  0.6 14.2 %copy-start = (s32[32,16,128]{2,1,0:T(8,128)S(1)}, s32[32,16,128]{2,1,0:T(8,128)}, u32[]{:S(2)}) copy-start(s32[32,16,128]{2,1,0:T(8,128)} %intact_hbm.1) | copy-start | bytes 786436
  2.7 18.9 %collective-permute-start.2 = (f32[79,8,128]{2,1,0:T(8,128)S(1)}, f32[79,8,128]{2,1,0:T(8,128)S(1)}, u32[]{:S(2)}, u32[]{:S(2)}) collective-permute-start(f32[79,8,128]{2,1,0:T(8,128)S(1)} %get-tuple-element.31), channel_id=1, source_target_pairs={{16,0},{32,16},{48,32},{64,48},{80,64},{96,80},{112,96},{128,112},... | collective-permute-start | bytes 970760 | tf_op jit(solution)/shard_map/ppermute | solution.py:432
  9.6 12.1 %collective-permute-start.3 = (f32[79,8,128]{2,1,0:T(8,128)S(1)}, f32[79,8,128]{2,1,0:T(8,128)S(1)}, u32[]{:S(2)}, u32[]{:S(2)}) collective-permute-start(f32[79,8,128]{2,1,0:T(8,128)S(1)} %get-tuple-element.32), channel_id=1, source_target_pairs={{0,16},{16,32},{32,48},{48,64},{64,80},{80,96},{96,112},{112,128},... | collective-permute-start | bytes 970760 | tf_op jit(solution)/shard_map/ppermute | solution.py:432
  9.6 7.2 %collective-permute-start = (f32[17,16,128]{2,1,0:T(8,128)S(1)}, f32[17,16,128]{2,1,0:T(8,128)S(1)}, u32[]{:S(2)}, u32[]{:S(2)}) collective-permute-start(f32[17,16,128]{2,1,0:T(8,128)S(1)} %get-tuple-element.28), channel_id=1, source_target_pairs={{1,0},{2,1},{3,2},{4,3},{5,4},{6,5},{7,6},{8,7},{9,8},{10,9},{11,1... | collective-permute-start | bytes 417800 | tf_op jit(solution)/shard_map/ppermute | solution.py:432
  10.9 6.0 %collective-permute-start.1 = (f32[17,16,128]{2,1,0:T(8,128)S(1)}, f32[17,16,128]{2,1,0:T(8,128)S(1)}, u32[]{:S(2)}, u32[]{:S(2)}) collective-permute-start(f32[17,16,128]{2,1,0:T(8,128)S(1)} %get-tuple-element.29), channel_id=1, source_target_pairs={{0,1},{1,2},{2,3},{3,4},{4,5},{5,6},{6,7},{7,8},{8,9},{9,10},{10,1... | collective-permute-start | bytes 417800 | tf_op jit(solution)/shard_map/ppermute | solution.py:432
  16.9 5.5 %collective-permute-start.5 = (f32[17,8,128]{2,1,0:T(8,128)S(1)}, f32[17,8,128]{2,1,0:T(8,128)S(1)}, u32[]{:S(2)}, u32[]{:S(2)}) collective-permute-start(f32[17,8,128]{2,1,0:T(8,128)S(1)} %get-tuple-element.36), channel_id=1, source_target_pairs={{0,16},{16,32},{32,48},{48,64},{64,80},{80,96},{96,112},{112,128},... | collective-permute-start | bytes 208904 | tf_op jit(solution)/shard_map/ppermute | solution.py:432
  16.9 5.6 %collective-permute-start.4 = (f32[17,8,128]{2,1,0:T(8,128)S(1)}, f32[17,8,128]{2,1,0:T(8,128)S(1)}, u32[]{:S(2)}, u32[]{:S(2)}) collective-permute-start(f32[17,8,128]{2,1,0:T(8,128)S(1)} %get-tuple-element.33.corner_down), channel_id=1, source_target_pairs={{16,0},{32,16},{48,32},{64,48},{80,64},{96,80},{112,96},{128,112},... | collective-permute-start | bytes 208904 | tf_op jit(solution)/shard_map/ppermute | solution.py:432
  24.0 6.0 %collective-permute-start.6 = (f32[1,16,128]{2,1,0:T(8,128)S(1)}, f32[1,16,128]{2,1,0:T(8,128)S(1)}, u32[]{:S(2)}, u32[]{:S(2)}) collective-permute-start(f32[1,16,128]{2,1,0:T(8,128)S(1)} %get-tuple-element.41), channel_id=1, source_target_pairs={{1,0},{2,1},{3,2},{4,3},{5,4},{6,5},{7,6},{8,7},{9,8},{10,9},{11,1... | collective-permute-start | bytes 24584 | tf_op jit(solution)/shard_map/ppermute | solution.py:432
  25.3 5.5 %collective-permute-start.7 = (f32[1,16,128]{2,1,0:T(8,128)S(1)}, f32[1,16,128]{2,1,0:T(8,128)S(1)}, u32[]{:S(2)}, u32[]{:S(2)}) collective-permute-start(f32[1,16,128]{2,1,0:T(8,128)S(1)} %get-tuple-element.42), channel_id=1, source_target_pairs={{0,1},{1,2},{2,3},{3,4},{4,5},{5,6},{6,7},{7,8},{8,9},{9,10},{10,1... | collective-permute-start | bytes 24584 | tf_op jit(solution)/shard_map/ppermute | solution.py:432
  30.8 5.7 %collective-permute-start.8 = (f32[3,8,128]{2,1,0:T(8,128)S(1)}, f32[3,8,128]{2,1,0:T(8,128)S(1)}, u32[]{:S(2)}, u32[]{:S(2)}) collective-permute-start(f32[3,8,128]{2,1,0:T(8,128)S(1)} %get-tuple-element.43), channel_id=1, source_target_pairs={{16,0},{32,16},{48,32},{64,48},{80,64},{96,80},{112,96},{128,112},... | collective-permute-start | bytes 36872 | tf_op jit(solution)/shard_map/ppermute | solution.py:432
  35.7 2.8 %collective-permute-start.9 = (f32[3,8,128]{2,1,0:T(8,128)S(1)}, f32[3,8,128]{2,1,0:T(8,128)S(1)}, u32[]{:S(2)}, u32[]{:S(2)}) collective-permute-start(f32[3,8,128]{2,1,0:T(8,128)S(1)} %get-tuple-element.44), channel_id=1, source_target_pairs={{0,16},{16,32},{32,48},{48,64},{64,80},{80,96},{96,112},{112,128},... | collective-permute-start | bytes 36872 | tf_op jit(solution)/shard_map/ppermute | solution.py:432
